TPU v7x, 256 devices: a whole 4x4x8 slice. The times are simulated.
256 devices in a mesh: row: 32 (over z, y_lo, core), col: 8 (over y_hi, x).
Axes of the slice: x: 4, y: 4 (y_hi: 2, y_lo: 2; y = y_hi * 2 + y_lo), z: 8, core: 2. Of those that a mesh axis runs over, the one named last changes fastest.
Arguments:
- frames_in: bfloat16 [2, 512, 128, 384], P(None, 'row', 'col'), may hold values from -6 to 6
- grad_out: bfloat16 [2, 512, 128, 384], P(None, 'row', 'col'), may hold values from -6 to 6
- norm_gain: float32 [384], replicated, may hold values from 0.1 to 1.9
- norm_shift: float32 [384], replicated, may hold values from -3 to 3
- qkv_weight: bfloat16 [384, 1152], replicated, may hold values from -0.3125 to 0.3125
- proj_weight: bfloat16 [384, 384], replicated, may hold values from -0.3125 to 0.3125
- bias_table: float32 [675, 12], replicated, may hold values from -6 to 330
- pos_index: int32 [128, 128], replicated, may hold values from 0 to 674
- region_ids: int32 [2, 512, 128], P(None, 'row', 'col'), may hold values from 0 to 3
Outputs:
- block_out: bfloat16 [2, 512, 128, 384], P(None, 'row', 'col')
- grad_input: bfloat16 [2, 512, 128, 384], P(None, 'row', 'col')
- grad_qkv_weight: float32 [384, 1152], replicated
- grad_proj_weight: float32 [384, 384], replicated
- grad_table: float32 [675, 12], replicated
- grad_gain: float32 [384], replicated
- grad_shift: float32 [384], replicated
All inputs are finite; a program needn't handle non-finite values.
Results may differ from a plain program's by a relative error of at most 0.0092.
Values may be sent and summed in bfloat16 or wider, within the bound.
No kernel may reach another device: no remote copies, remote signals or barrier semaphores. Data moves between devices by JAX's collectives and lax.ppermute only.
A program may use at most 64 MiB of HBM per device.

v0:
```python
import jax
import jax.numpy as jnp
from jax import lax
from jax.sharding import PartitionSpec as P

HEADS = 12
WIN_T = 2
WIN_H = 8
WIN_W = 8
WIN_TOK = 128
TABLE_ROWS = 675


norm_eps = 1e-05


def shifted(value, axis, steps):
    count = lax.axis_size(axis)
    pairs = [(source, (source + steps) % count) for source in range(count)]
    return lax.ppermute(value, axis, pairs)


def to_windows(grid_cells):
    frame_count, row_count, col_count = (
        grid_cells.shape[0],
        grid_cells.shape[1],
        grid_cells.shape[2],
    )
    trailing = grid_cells.shape[3:]
    split_up = grid_cells.reshape(
        (frame_count // WIN_T, WIN_T, row_count // WIN_H, WIN_H, col_count // WIN_W, WIN_W)
        + trailing
    )
    axis_order = (0, 2, 4, 1, 3, 5) + tuple(range(6, 6 + len(trailing)))
    return split_up.transpose(axis_order).reshape((-1, WIN_TOK) + trailing)


def from_windows(blocks, frame_count, row_count, col_count):
    trailing = blocks.shape[2:]
    split_up = blocks.reshape(
        (frame_count // WIN_T, row_count // WIN_H, col_count // WIN_W, WIN_T, WIN_H, WIN_W)
        + trailing
    )
    axis_order = (0, 3, 1, 4, 2, 5) + tuple(range(6, 6 + len(trailing)))
    return split_up.transpose(axis_order).reshape((frame_count, row_count, col_count) + trailing)


def roll_forward(grid_tile):
    half_h = WIN_H // 2
    half_w = WIN_W // 2
    grid_tile = jnp.roll(grid_tile, -(WIN_T // 2), axis=-4)
    rows_in = shifted(grid_tile[..., :half_h, :, :], "row", -1)
    joined = jnp.concatenate([grid_tile[..., half_h:, :, :], rows_in], axis=-3)
    cols_in = shifted(joined[..., :, :half_w, :], "col", -1)
    joined = jnp.concatenate([joined[..., :, half_w:, :], cols_in], axis=-2)
    return joined


def roll_back(grid_tile):
    half_h = WIN_H // 2
    half_w = WIN_W // 2
    rows_in = shifted(grid_tile[..., -half_h:, :, :], "row", 1)
    joined = jnp.concatenate([rows_in, grid_tile[..., :-half_h, :, :]], axis=-3)
    cols_in = shifted(joined[..., :, -half_w:, :], "col", 1)
    joined = jnp.concatenate([cols_in, joined[..., :, :-half_w, :]], axis=-2)
    return jnp.roll(joined, WIN_T // 2, axis=-4)


def probabilities(queries, key_rows, group_ids, position_bias, score_scale):
    scores = (
        jnp.einsum("wqhd,wkhd->whqk", queries, key_rows, preferred_element_type=jnp.float32)
        * score_scale
        + position_bias[None]
    )
    allowed = group_ids[:, None, :, None] == group_ids[:, None, None, :]
    row_max = jnp.max(jnp.where(allowed, scores, -1e30), axis=-1, keepdims=True)
    exp_scores = jnp.exp(jnp.where(allowed, scores - row_max, -1e30))
    return exp_scores / jnp.sum(exp_scores, axis=-1, keepdims=True)


def forward_part(
    window_x, window_ids, norm_gain, norm_shift, qkv_weight, proj_weight, position_bias
):
    win_count = window_x.shape[0]
    feat_width = window_x.shape[-1]
    head_dim = feat_width // HEADS
    score_scale = head_dim ** (-0.5)
    as_float = window_x.astype(jnp.float32)
    average = jnp.mean(as_float, axis=-1, keepdims=True)
    centered = as_float - average
    variance = jnp.mean(centered * centered, axis=-1, keepdims=True)
    inv_std = lax.rsqrt(variance + norm_eps)
    x_hat = centered * inv_std
    normed = (x_hat * norm_gain + norm_shift).astype(jnp.bfloat16).reshape(-1, feat_width)
    qkv_all = jnp.dot(normed, qkv_weight, preferred_element_type=jnp.float32).astype(jnp.bfloat16)
    group_size = 4
    grouped = qkv_all.reshape(win_count // group_size, group_size, WIN_TOK, 3, HEADS, head_dim)
    grouped_ids = window_ids.reshape(win_count // group_size, group_size, WIN_TOK)

    def attend_group(inputs):
        group_qkv, group_ids = inputs
        attn_prob = probabilities(
            group_qkv[:, :, 0], group_qkv[:, :, 1], group_ids, position_bias, score_scale
        )
        prob_bf16 = attn_prob.astype(jnp.bfloat16)
        return jnp.einsum(
            "whqk,wkhd->wqhd", prob_bf16, group_qkv[:, :, 2], preferred_element_type=jnp.float32
        ).astype(jnp.bfloat16)

    attended = lax.map(attend_group, (grouped, grouped_ids)).reshape(-1, feat_width)
    branch = jnp.dot(attended, proj_weight, preferred_element_type=jnp.float32).astype(jnp.bfloat16)
    return (branch, (x_hat, inv_std, normed, grouped, grouped_ids, attended))


def backward_attn(stored, grad_attended, norm_gain, qkv_weight, position_bias):
    x_hat, inv_std, normed, grouped, grouped_ids, attended = stored
    feat_width = x_hat.shape[-1]
    head_dim = feat_width // HEADS
    score_scale = head_dim ** (-0.5)
    grad_groups = grad_attended.reshape(
        grouped.shape[0], grouped.shape[1], WIN_TOK, HEADS, head_dim
    )

    def back_group(inputs):
        group_qkv, group_ids, grad_heads = inputs
        queries = group_qkv[:, :, 0]
        key_rows = group_qkv[:, :, 1]
        values = group_qkv[:, :, 2]
        attn_prob = probabilities(queries, key_rows, group_ids, position_bias, score_scale)
        prob_bf16 = attn_prob.astype(jnp.bfloat16)
        grad_prob = jnp.einsum(
            "wqhd,wkhd->whqk", grad_heads, values, preferred_element_type=jnp.float32
        )
        row_inner = jnp.sum(attn_prob * grad_prob, axis=-1, keepdims=True)
        grad_score = attn_prob * (grad_prob - row_inner)
        score_bf16 = (grad_score * score_scale).astype(jnp.bfloat16)
        grad_query = jnp.einsum(
            "whqk,wkhd->wqhd", score_bf16, key_rows, preferred_element_type=jnp.float32
        )
        grad_key = jnp.einsum(
            "whqk,wqhd->wkhd", score_bf16, queries, preferred_element_type=jnp.float32
        )
        grad_value = jnp.einsum(
            "whqk,wqhd->wkhd", prob_bf16, grad_heads, preferred_element_type=jnp.float32
        )
        grad_qkv = jnp.stack([grad_query, grad_key, grad_value], axis=2).astype(jnp.bfloat16)
        return (grad_qkv, jnp.sum(grad_score, axis=0))

    grad_qkv, table_parts = lax.map(back_group, (grouped, grouped_ids, grad_groups))
    table_terms = jnp.sum(table_parts, axis=0)
    grad_qkv = grad_qkv.reshape(-1, 3 * feat_width)
    grad_qkv_w = lax.dot_general(
        normed, grad_qkv, (((0,), (0,)), ((), ())), preferred_element_type=jnp.float32
    )
    grad_normed = lax.dot_general(
        grad_qkv, qkv_weight, (((1,), (1,)), ((), ())), preferred_element_type=jnp.float32
    )
    flat_hat = x_hat.reshape(-1, feat_width)
    flat_inv = inv_std.reshape(-1, 1)
    grad_gain = jnp.sum(grad_normed * flat_hat, axis=0)
    grad_shift = jnp.sum(grad_normed, axis=0)
    scaled = grad_normed * norm_gain
    grad_rolled = flat_inv * (
        scaled
        - jnp.mean(scaled, axis=-1, keepdims=True)
        - flat_hat * jnp.mean(scaled * flat_hat, axis=-1, keepdims=True)
    )
    return (grad_rolled.astype(jnp.bfloat16), grad_qkv_w, table_terms, grad_gain, grad_shift)


def backward_all(
    stored, grad_flat, norm_gain, qkv_weight, proj_weight, pos_index, position_bias, token_total
):
    attended = stored[5]
    grad_proj = lax.dot_general(
        attended, grad_flat, (((0,), (0,)), ((), ())), preferred_element_type=jnp.float32
    )
    grad_attended = lax.dot_general(
        grad_flat, proj_weight, (((1,), (1,)), ((), ())), preferred_element_type=jnp.float32
    ).astype(jnp.bfloat16)
    grad_rolled, grad_qkv_w, table_terms, grad_gain, grad_shift = backward_attn(
        stored, grad_attended, norm_gain, qkv_weight, position_bias
    )
    grad_table = jax.ops.segment_sum(
        table_terms.reshape(HEADS, -1).T, pos_index.reshape(-1), num_segments=TABLE_ROWS
    )
    summed_proj, summed_qkv, summed_table, summed_gain, summed_shift = lax.psum(
        (grad_proj, grad_qkv_w, grad_table, grad_gain, grad_shift), ("row", "col")
    )
    factor = token_total ** (-0.5)
    return (
        grad_rolled,
        (
            summed_qkv * factor,
            summed_proj * factor,
            summed_table * factor,
            summed_gain * factor,
            summed_shift * factor,
        ),
    )


def body(
    frames_in,
    grad_out,
    norm_gain,
    norm_shift,
    qkv_weight,
    proj_weight,
    bias_table,
    pos_index,
    region_ids,
):
    frame_count, row_count, col_count, feat_width = frames_in.shape
    token_total = frame_count * row_count * col_count * lax.axis_size("row") * lax.axis_size("col")
    position_bias = jnp.take(bias_table, pos_index, axis=0).transpose(2, 0, 1)
    window_ids = to_windows(region_ids)
    x_rolled = roll_forward(frames_in)
    branch, stored = forward_part(
        to_windows(x_rolled),
        window_ids,
        norm_gain,
        norm_shift,
        qkv_weight,
        proj_weight,
        position_bias,
    )
    branch_tile = from_windows(
        branch.reshape(-1, WIN_TOK, feat_width), frame_count, row_count, col_count
    )
    block_out = (frames_in.astype(jnp.float32) + roll_back(branch_tile).astype(jnp.float32)).astype(
        jnp.bfloat16
    )
    g_rolled = roll_forward(grad_out)
    grad_rolled, grad_sums = backward_all(
        stored,
        to_windows(g_rolled).reshape(-1, feat_width),
        norm_gain,
        qkv_weight,
        proj_weight,
        pos_index,
        position_bias,
        token_total,
    )
    back_tile = from_windows(
        grad_rolled.reshape(-1, WIN_TOK, feat_width), frame_count, row_count, col_count
    )
    grad_input = (grad_out.astype(jnp.float32) + roll_back(back_tile).astype(jnp.float32)).astype(
        jnp.bfloat16
    )
    return (block_out, grad_input) + grad_sums


def solution(mesh):
    placed = (
        P(None, "row", "col", None),
        P(None, "row", "col", None),
        P(),
        P(),
        P(),
        P(),
        P(),
        P(),
        P(None, "row", "col"),
    )
    return jax.shard_map(
        body,
        mesh=mesh,
        in_specs=placed,
        out_specs=(
            P(None, "row", "col", None),
            P(None, "row", "col", None),
            P(),
            P(),
            P(),
            P(),
            P(),
        ),
        check_vma=False,
    )
```

profile of v0, /device:TPU:1, one launch (start us, length us, event | category | flops | bytes accessed | tf_op | source)
XLA Modules:
  0.0 577.7 jit_solution(13398317032375158538)
XLA Ops:
  8.4 3.3 collective-permute-start
  12.8 4.6 collective-permute-start.4
  17.8 54.8 %gather_fusion = f32[16384,12]{1,0:T(8,128)} fusion(f32[675,12]{1,0:T(8,128)S(1)} %copy.104, s32[16384]{0:T(1024)S(1)} %bitcast_clamp_fusion), kind=kCustom, calls=%fused_computation | custom fusion | bytes 1638400 | tf_op jit(solution)/shard_map/jit(_take)/gather | solution.py:216
  72.5 6.7 %copy.105 = f32[128,128,12]{0,1,2:T(8,128)S(1)} copy(f32[128,128,12]{2,1,0:T(8,128)} %bitcast.113) | data formatting | bytes 1572864 | tf_op jit(solution)/shard_map/jit(_take)/gather | solution.py:216
  81.3 4.9 collective-permute-start.1
  90.0 1.4 copy.98
  91.4 2.5 squeeze.35
  97.2 1.9 fusion.28
  100.2 1.7 fusion.12
  102.0 1.7 convolution_bitcast_fusion
  103.7 3.4 fusion.27
  107.0 6.5 %convolution_bitcast_fusion.1 = bf16[4,128,1,12,32]{1,4,3,0,2:T(8,128)(2,1)} fusion(bf16[4,128,1,12,32]{1,0,4,3,2:T(4,128)(2,1)S(1)} %copy-done.5, f32[4,12,128,128]{2,3,1,0:T(8,128)} %fusion.27, f32[4,12,128,128]{2,3,1,0:T(8,128)} %copy-done.21, f32[4,12,128]{2,1,0:T(8,128)S(1)} %get-tuple-element.98), kind=kOutput, calls=%fused_computation.20 | convolution fusion | flops 55842944 | bytes 7102464 | tf_op jit(solution)/shard_map/while/body/eval_jaxpr/whqk,wqhd->wkhd/dot_general | solution.py:140
  113.5 6.4 %convolution_bitcast_fusion.2 = bf16[4,128,1,12,32]{1,4,3,0,2:T(8,128)(2,1)} fusion(bf16[4,128,1,12,32]{1,0,4,3,2:T(4,128)(2,1)S(1)} %copy-done.4, f32[4,12,128,128]{2,3,1,0:T(8,128)} %fusion.27, f32[4,12,128,128]{2,3,1,0:T(8,128)} %copy-done.21, f32[4,12,128]{2,1,0:T(8,128)S(1)} %get-tuple-element.98), kind=kOutput, calls=%fused_computation.21 | convolution fusion | flops 55842944 | bytes 7102464 | tf_op jit(solution)/shard_map/while/body/eval_jaxpr/whqk,wkhd->wqhd/dot_general | solution.py:137
  120.5 1.7 convolution_convert_fusion.3
  123.4 4.0 fusion.57
  131.4 1.9 fusion.13
  134.3 4.7 copy.119
  139.0 87.7 %scatter_custom_fusion = f32[675,12]{1,0:T(8,128)S(1)} fusion(s32[16384]{0:T(1024)} %bitcast.134, f32[16384,12]{1,0:T(8,128)} %copy.119, f32[]{:T(128)} %constant.45.clone.1), kind=kCustom, calls=%fused_computation.78 | custom fusion | flops 196608 | bytes 32912 | tf_op jit(solution)/shard_map/scatter-add | solution.py:184
  226.7 82.7 %all-reduce = (f32[675,12]{1,0:T(8,128)S(1)}, f32[384]{0:T(512)S(1)}, f32[384]{0:T(512)S(1)}) all-reduce(f32[675,12]{1,0:T(8,128)S(1)} %scatter_custom_fusion, f32[384]{0:T(512)S(1)} %get-tuple-element.78, f32[384]{0:T(512)S(1)} %get-tuple-element.81), channel_id=1, replica_groups=mesh['row'=32,'col'=8] {'row','col'}, use_global_device_ids=true, to_apply=%region_11.12 | all-reduce | flops 8868 | bytes 70944 | tf_op jit(solution)/shard_map/psum | solution.py:187
  311.8 1.5 collective-permute-start.3
  315.0 4.0 collective-permute-done.3
  320.0 2.6 collective-permute-done.7
  325.5 241.6 %all-reduce.4.cloned.1.call-done = (f32[384,1152]{1,0:T(8,128)}, f32[384,384]{1,0:T(8,128)}) async-done(((f32[384,1152]{1,0:T(8,128)}, f32[384,384]{1,0:T(8,128)}), (f32[384,1152]{1,0:T(8,128)}, f32[384,384]{1,0:T(8,128)})) %all-reduce.4.cloned.1.call-update) | async-done | bytes 2359312 | tf_op jit(solution)/shard_map/psum | solution.py:187
  567.1 2.9 broadcast_multiply_fusion
  (121 shorter events, 28.1 us)
Async XLA Ops:
  7.2 82.0 %copy-start = (bf16[384,1152]{1,0:T(8,128)(2,1)S(1)}, bf16[384,1152]{1,0:T(8,128)(2,1)}, u32[]{:S(2)}) copy-start(bf16[384,1152]{1,0:T(8,128)(2,1)} %param.13) | copy-start | bytes 2654212
  7.2 10.3 %copy-start.15 = (s32[128,128]{1,0:T(8,128)S(1)}, s32[128,128]{1,0:T(8,128)}, u32[]{:S(2)}) copy-start(s32[128,128]{1,0:T(8,128)} %param.16) | copy-start | bytes 196612
  7.2 10.4 %copy-start.17 = (f32[675,12]{0,1:T(8,128)S(1)}, f32[675,12]{0,1:T(8,128)}, u32[]{:S(2)}) copy-start(f32[675,12]{0,1:T(8,128)} %param.15) | copy-start | bytes 97204
  7.2 559.9 %all-reduce.4.cloned.1.call-start = ((), (), s32[]{:S(2)}) async-start(), calls=%async_computation | async-start | bytes 4718592 | tf_op jit(solution)/shard_map/psum | solution.py:187
  8.4 72.9 %collective-permute-start = (bf16[2,4,16,384]{3,2,1,0:T(8,128)(2,1)S(1)}, bf16[2,4,16,384]{3,2,1,0:T(8,128)(2,1)S(1)}, u32[]{:S(2)}, u32[]{:S(2)}) collective-permute-start(bf16[2,4,16,384]{3,2,1,0:T(8,128)(2,1)S(1)} %pad_maximum_fusion.9), channel_id=1, source_target_pairs={{0,248},{8,0},{16,8},{24,16},{32,24},{40,32},{48,40},{56,48},{64,5... | collective-permute-start | bytes 294920 | tf_op jit(solution)/shard_map/ppermute | solution.py:20
  12.8 73.4 %collective-permute-start.4 = (bf16[2,4,16,384]{3,2,1,0:T(8,128)(2,1)S(1)}, bf16[2,4,16,384]{3,2,1,0:T(8,128)(2,1)S(1)}, u32[]{:S(2)}, u32[]{:S(2)}) collective-permute-start(bf16[2,4,16,384]{3,2,1,0:T(8,128)(2,1)S(1)} %pad_maximum_fusion.6), channel_id=1, source_target_pairs={{0,248},{8,0},{16,8},{24,16},{32,24},{40,32},{48,40},{56,48},{64,5... | collective-permute-start | bytes 294920 | tf_op jit(solution)/shard_map/ppermute | solution.py:20
  72.5 6.8 %copy-start.19 = (s32[2,16,16]{2,1,0:T(8,128)S(1)}, s32[2,16,16]{2,1,0:T(8,128)}, u32[]{:S(2)}) copy-start(s32[2,16,16]{2,1,0:T(8,128)} %param.17) | copy-start | bytes 6148
  81.2 7.7 %copy-start.18 = (f32[384]{0:T(512)S(1)}, f32[384]{0:T(512)}, u32[]{:S(2)}) copy-start(f32[384]{0:T(512)} %param.11) | copy-start | bytes 4612
  81.2 7.7 %copy-start.20 = (f32[384]{0:T(512)S(1)}, f32[384]{0:T(512)}, u32[]{:S(2)}) copy-start(f32[384]{0:T(512)} %param.12) | copy-start | bytes 4612
  81.3 6.7 %collective-permute-start.1 = (bf16[2,16,4,384]{3,2,1,0:T(4,128)(2,1)S(1)}, bf16[2,16,4,384]{3,2,1,0:T(4,128)(2,1)S(1)}, u32[]{:S(2)}, u32[]{:S(2)}) collective-permute-start(bf16[2,16,4,384]{3,2,1,0:T(4,128)(2,1)S(1)} %pad_maximum_fusion.8), channel_id=1, source_target_pairs={{0,7},{1,0},{2,1},{3,2},{4,3},{5,4},{6,5},{7,6},{8,15},{9,8},{10,9... | collective-permute-start | bytes 294920 | tf_op jit(solution)/shard_map/ppermute | solution.py:20
  86.2 9.1 %collective-permute-start.5 = (bf16[2,16,4,384]{3,2,1,0:T(4,128)(2,1)S(1)}, bf16[2,16,4,384]{3,2,1,0:T(4,128)(2,1)S(1)}, u32[]{:S(2)}, u32[]{:S(2)}) collective-permute-start(bf16[2,16,4,384]{3,2,1,0:T(4,128)(2,1)S(1)} %pad_maximum_fusion.5), channel_id=1, source_target_pairs={{0,7},{1,0},{2,1},{3,2},{4,3},{5,4},{6,5},{7,6},{8,15},{9,8},{10,9... | collective-permute-start | bytes 294920 | tf_op jit(solution)/shard_map/ppermute | solution.py:20
  97.2 4.7 copy-start.7
  107.0 6.5 %copy-start.4 = (bf16[4,128,1,12,32]{1,0,4,3,2:T(4,128)(2,1)S(1)}, bf16[4,128,1,12,32]{1,0,4,3,2:T(4,128)(2,1)}, u32[]{:S(2)}) copy-start(bf16[4,128,1,12,32]{1,0,4,3,2:T(4,128)(2,1)} %get-tuple-element.87) | copy-start | bytes 1179652
  113.5 6.7 %copy-start.13 = (bf16[4,128,12,32]{1,3,2,0:T(8,128)(2,1)S(1)}, bf16[4,128,12,32]{1,3,2,0:T(8,128)(2,1)}, u32[]{:S(2)}) copy-start(bf16[4,128,12,32]{1,3,2,0:T(8,128)(2,1)} %fusion.12) | copy-start | bytes 1179652
  119.9 3.4 copy-start.1
  123.4 4.7 copy-start.10
  123.4 4.7 copy-start.11
  123.4 4.7 copy-start.12
  128.1 182.8 %collective-permute-start.2 = (bf16[2,4,16,384]{3,2,1,0:T(8,128)(2,1)}, bf16[2,4,16,384]{3,2,1,0:T(8,128)(2,1)}, u32[]{:S(2)}, u32[]{:S(2)}) collective-permute-start(bf16[2,4,16,384]{3,2,1,0:T(8,128)(2,1)} %slice.130), channel_id=1, source_target_pairs={{0,8},{8,16},{16,24},{24,32},{32,40},{40,48},{48,56},{56,64},{64,7... | collective-permute-start | bytes 294920 | tf_op jit(solution)/shard_map/ppermute | solution.py:20
  131.4 181.8 %collective-permute-start.6 = (bf16[2,4,16,384]{3,2,1,0:T(8,128)(2,1)}, bf16[2,4,16,384]{3,2,1,0:T(8,128)(2,1)}, u32[]{:S(2)}, u32[]{:S(2)}) collective-permute-start(bf16[2,4,16,384]{3,2,1,0:T(8,128)(2,1)} %slice.138), channel_id=1, source_target_pairs={{0,8},{8,16},{16,24},{24,32},{32,40},{40,48},{48,56},{56,64},{64,7... | collective-permute-start | bytes 294920 | tf_op jit(solution)/shard_map/ppermute | solution.py:20
  310.2 13.5 %copy-start.2 = (bf16[2,16,16,384]{3,2,1,0:T(8,128)(2,1)S(1)}, bf16[2,16,16,384]{3,2,1,0:T(8,128)(2,1)}, u32[]{:S(2)}) copy-start(bf16[2,16,16,384]{3,2,1,0:T(8,128)(2,1)} %param.9) | copy-start | bytes 1179652
  310.9 13.7 %copy-start.3 = (bf16[2,16,16,384]{3,2,1,0:T(8,128)(2,1)S(1)}, bf16[2,16,16,384]{3,2,1,0:T(8,128)(2,1)}, u32[]{:S(2)}) copy-start(bf16[2,16,16,384]{3,2,1,0:T(8,128)(2,1)} %param.10) | copy-start | bytes 1179652
  311.8 7.2 %collective-permute-start.3 = (bf16[2,16,4,384]{3,2,1,0:T(4,128)(2,1)S(1)}, bf16[2,16,4,384]{3,2,1,0:T(4,128)(2,1)S(1)}, u32[]{:S(2)}, u32[]{:S(2)}) collective-permute-start(bf16[2,16,4,384]{3,2,1,0:T(4,128)(2,1)S(1)} %pad_maximum_fusion.7), channel_id=1, source_target_pairs={{0,1},{1,2},{2,3},{3,4},{4,5},{5,6},{6,7},{7,0},{8,9},{9,10},{10,1... | collective-permute-start | bytes 294920 | tf_op jit(solution)/shard_map/ppermute | solution.py:20
  314.1 8.5 %collective-permute-start.7 = (bf16[2,16,4,384]{3,2,1,0:T(4,128)(2,1)S(1)}, bf16[2,16,4,384]{3,2,1,0:T(4,128)(2,1)S(1)}, u32[]{:S(2)}, u32[]{:S(2)}) collective-permute-start(bf16[2,16,4,384]{3,2,1,0:T(4,128)(2,1)S(1)} %pad_maximum_fusion.4), channel_id=1, source_target_pairs={{0,1},{1,2},{2,3},{3,4},{4,5},{5,6},{6,7},{7,0},{8,9},{9,10},{10,1... | collective-permute-start | bytes 294920 | tf_op jit(solution)/shard_map/ppermute | solution.py:20
  (7 other events, 16.3 us)
Sparse Core Ops, SparseCore 0:
  310.3 256.6 all-reduce.3
where the time goes:
time: 579 us; the launch traced here: 578 us
  waiting for transfers between devices  248 us (43%)
  other arithmetic  108 us (19%)
  blocking collectives  82.7 us (14%)
  local copies, waits for them, and re-layouts  79.3 us (14%)
  matrix products  28.7 us (5%)
  starting transfers between devices  16 us (3%)
  between operations  14.6 us (3%)
    psum x1, waiting for transfers between devices, backward_all(): lax.psum((grad_proj, grad_qkv_w, grad_table, grad_gain, grad_shift), ('ro...  242 us
    scatter-add x1, other arithmetic, backward_all(): jax.ops.segment_sum(table_terms.reshape(HEADS, -1).T, pos_index.reshape(-...  87.7 us
    psum x1, blocking collectives, backward_all(): lax.psum((grad_proj, grad_qkv_w, grad_table, grad_gain, grad_shift), ('ro...  82.7 us
    gather x2, local copies, waits for them, and re-layouts, body(): position_bias = jnp.take(bias_table, pos_index, axis=0).transpose(2, 0, 1)  61.4 us
    ppermute x8, starting transfers between devices, shifted(): return lax.ppermute(value, axis, pairs)  16 us
  transfers between devices with their start and end apart: 9, of which 3 were waited for; matrix products, arithmetic and copies ran while one was open for 31% of the time, Pallas kernels for 0%

commit v1 on v0

v1 whole, which is shorter than its diff:
```python
import functools

import jax
import jax.numpy as jnp
from jax import lax
from jax.experimental import pallas as pl
from jax.experimental.pallas import tpu as pltpu
from jax.sharding import Mesh
from jax.sharding import PartitionSpec as P

HEADS = 12
WIN_TOK = 128
TABLE_ROWS = 675
WIDTH = 384
HEAD_DIM = 32
GROUP = 128
N_WIN = 4
TOK = N_WIN * WIN_TOK
NORM_EPS = 1e-05
SCALE = HEAD_DIM**-0.5

ROW_PROJ = 9 * WIDTH
ROW_TABLE = 12 * WIDTH
ROW_NORM = ROW_TABLE + 96
PACK_ROWS = 4864

F32 = jnp.float32
BF16 = jnp.bfloat16
VMEM_LIMIT = 50 * 1024 * 1024

NN = (((1,), (0,)), ((), ()))
NT = (((1,), (1,)), ((), ()))
TN = (((0,), (0,)), ((), ()))


def mm(a, b, dims):
    return lax.dot_general(a, b, dims, preferred_element_type=F32)


def whole(n):
    return [pl.BlockSpec(memory_space=pltpu.VMEM)] * n


def bias_kernel(pos_ref, table_ref, bias_ref):
    def rows(step, carry):
        at = pl.multiple_of(step * 8, 8)
        idx = pos_ref[pl.ds(at, 8), :]
        low = idx & 127
        high = idx >> 7
        for h in range(HEADS):
            got = None
            for k in range(6):
                chunk = jnp.broadcast_to(table_ref[h : h + 1, k * 128 : (k + 1) * 128], (8, 128))
                part = jnp.take_along_axis(chunk, low, axis=1)
                got = part if k == 0 else jnp.where(high == k, part, got)
            bias_ref[h, pl.ds(at, 8), :] = got
        return carry

    lax.fori_loop(0, 16, rows, 0)


def gather_bias(pos_t, table_t):
    return pl.pallas_call(
        bias_kernel,
        out_shape=jax.ShapeDtypeStruct((HEADS, WIN_TOK, WIN_TOK), F32),
        in_specs=whole(2),
        out_specs=pl.BlockSpec(memory_space=pltpu.VMEM),
        cost_estimate=pl.CostEstimate(flops=4_000_000, bytes_accessed=900_000, transcendentals=0),
        name="gather_bias",
    )(pos_t, table_t)


def window_tokens(ref, wr, wc):
    block = ref[:, 8 * wr : 8 * wr + 8, :, :].astype(F32)
    return block[:, :, 8 * wc : 8 * wc + 8, :].reshape(WIN_TOK, WIDTH)


def store_tile(ref, tokens):
    for wr in range(2):
        pair = [
            tokens[(2 * wr + wc) * WIN_TOK : (2 * wr + wc + 1) * WIN_TOK].reshape(2, 8, 8, WIDTH)
            for wc in range(2)
        ]
        ref[:, 8 * wr : 8 * wr + 8, :, :] = jnp.concatenate(pair, axis=2).astype(BF16)


def main_kernel(
    x_ref, g_ref, gain_ref, shift_ref, wqkv_ref, wproj_ref, bias_ref, id_row_ref, id_col_ref,
    pos_ref, branch_ref, back_ref, pack_ref,
    hat_s, inv_s, normed_s, g_s, qkv_s, da_s, att_s, gqkv_s, table_s,
):
    for wr in range(2):
        for wc in range(2):
            at = (2 * wr + wc) * WIN_TOK
            rows = slice(at, at + WIN_TOK)
            x = window_tokens(x_ref, wr, wc)
            centered = x - jnp.mean(x, axis=-1, keepdims=True)
            variance = jnp.mean(centered * centered, axis=-1, keepdims=True)
            inv_std = lax.rsqrt(variance + NORM_EPS)
            x_hat = centered * inv_std
            hat_s[rows, :] = x_hat
            inv_s[rows, :] = jnp.broadcast_to(inv_std, (WIN_TOK, 128))
            normed_s[rows, :] = (x_hat * gain_ref[...] + shift_ref[...]).astype(BF16)
            g_s[rows, :] = window_tokens(g_ref, wr, wc).astype(BF16)
    for p in range(3):
        part = mm(normed_s[...], wqkv_ref[:, p * WIDTH : (p + 1) * WIDTH], NN).astype(BF16)
        for k in range(3):
            qkv_s[3 * p + k] = part[:, k * GROUP : (k + 1) * GROUP]
    part = mm(g_s[...], wproj_ref[...], NT).astype(BF16)
    for k in range(3):
        da_s[k] = part[:, k * GROUP : (k + 1) * GROUP]

    table_s[...] = jnp.zeros_like(table_s)
    lane = lax.broadcasted_iota(jnp.int32, (WIN_TOK, GROUP), 1) // HEAD_DIM

    def attend(step, carry):
        w = step // 3
        k = step % 3
        rows = pl.ds(pl.multiple_of(w * WIN_TOK, WIN_TOK), WIN_TOK)
        q = qkv_s[k, rows, :]
        key = qkv_s[3 + k, rows, :]
        v = qkv_s[6 + k, rows, :]
        da = da_s[k, rows, :]
        shut = jnp.where(id_col_ref[w] == id_row_ref[w], 0.0, -1e30)
        zero = jnp.zeros_like(q)
        heads = []
        for h in range(4):
            mine = lane == h
            heads.append(tuple(jnp.where(mine, a, zero) for a in (q, key, v, da)))
        probs, grads = [], []
        for h in range(4):
            _, key_h, v_h, _ = heads[h]
            score = mm(key_h, q, NT) * SCALE + bias_ref[4 * k + h] + shut
            top = jnp.max(score, axis=0, keepdims=True)
            e = jnp.exp(score - top)
            prob = e * (1.0 / jnp.sum(e, axis=0, keepdims=True))
            grad_prob = mm(v_h, da, NT)
            inner = jnp.sum(prob * grad_prob, axis=0, keepdims=True)
            grad_score = prob * (grad_prob - inner)
            table_s[4 * k + h] += grad_score
            probs.append(prob.astype(BF16))
            grads.append((grad_score * SCALE).astype(BF16))
        prob_rows = jnp.concatenate(probs, axis=0)
        grad_rows = jnp.concatenate(grads, axis=0)
        q_all, key_all, v_all, da_all = (
            jnp.concatenate([heads[h][n] for h in range(4)], axis=0) for n in range(4)
        )
        att_s[k, rows, :] = mm(prob_rows, v_all, TN).astype(BF16)
        gqkv_s[k, rows, :] = mm(grad_rows, key_all, TN).astype(BF16)
        gqkv_s[3 + k, rows, :] = mm(jnp.concatenate(grads, axis=1), q_all, NN).astype(BF16)
        gqkv_s[6 + k, rows, :] = mm(jnp.concatenate(probs, axis=1), da_all, NN).astype(BF16)
        return carry

    lax.fori_loop(0, 12, attend, 0)

    attended = jnp.concatenate([att_s[k] for k in range(3)], axis=1)
    store_tile(branch_ref, mm(attended, wproj_ref[...], NN))
    grad_proj = mm(attended, g_s[...], TN)
    for k in range(3):
        at = ROW_PROJ + k * WIDTH
        pack_ref[at : at + WIDTH, :] = grad_proj[:, k * GROUP : (k + 1) * GROUP].astype(BF16)

    grad_normed = None
    for p in range(3):
        grad_part = jnp.concatenate([gqkv_s[3 * p + k] for k in range(3)], axis=1)
        grad_w = mm(normed_s[...], grad_part, TN)
        for k in range(3):
            at = (3 * p + k) * WIDTH
            pack_ref[at : at + WIDTH, :] = grad_w[:, k * GROUP : (k + 1) * GROUP].astype(BF16)
        term = mm(grad_part, wqkv_ref[:, p * WIDTH : (p + 1) * WIDTH], NT)
        grad_normed = term if p == 0 else grad_normed + term
    x_hat = hat_s[...]
    grad_gain = jnp.sum(grad_normed * x_hat, axis=0, keepdims=True)
    grad_shift = jnp.sum(grad_normed, axis=0, keepdims=True)
    scaled = grad_normed * gain_ref[...]
    grad_rolled = inv_s[:, 0:1] * (
        scaled
        - jnp.mean(scaled, axis=-1, keepdims=True)
        - x_hat * jnp.mean(scaled * x_hat, axis=-1, keepdims=True)
    )
    store_tile(back_ref, grad_rolled)

    low_bins = lax.broadcasted_iota(jnp.int32, (256, WIN_TOK), 0)

    def bins(step, acc):
        left, right = [], []
        for n in range(2):
            j = 2 * step + n
            idx = pos_ref[pl.ds(j, 1), :]
            high = idx >> 8
            terms = table_s[:, j, :]
            left.append(
                jnp.concatenate([jnp.where(high == a, terms, 0.0) for a in range(3)], axis=0)
            )
            right.append(jnp.where(low_bins == (idx & 255), 1.0, 0.0).astype(BF16))
        return acc + mm(
            jnp.concatenate(left, axis=1).astype(BF16), jnp.concatenate(right, axis=1), NT
        )

    table = lax.fori_loop(0, WIN_TOK // 2, bins, jnp.zeros((48, 256), F32))
    for n in range(2):
        at = ROW_TABLE + 48 * n
        pack_ref[at : at + 48, :] = table[:, 128 * n : 128 * (n + 1)].astype(BF16)
    norm_rows = [a[:, k * 128 : (k + 1) * 128] for a in (grad_gain, grad_shift) for k in range(3)]
    norm_rows.append(jnp.zeros((10, 128), F32))
    pack_ref[ROW_NORM : ROW_NORM + 16, :] = jnp.concatenate(norm_rows, axis=0).astype(BF16)
    pack_ref[ROW_NORM + 16 :, :] = jnp.zeros((PACK_ROWS - ROW_NORM - 16, 128), BF16)


def main_call(*args):
    tile = jax.ShapeDtypeStruct((2, 16, 16, WIDTH), BF16)
    return pl.pallas_call(
        main_kernel,
        out_shape=(tile, tile, jax.ShapeDtypeStruct((PACK_ROWS, 128), BF16)),
        in_specs=whole(len(args)),
        out_specs=tuple(whole(3)),
        scratch_shapes=[
            pltpu.VMEM((TOK, WIDTH), F32),
            pltpu.VMEM((TOK, 128), F32),
            pltpu.VMEM((TOK, WIDTH), BF16),
            pltpu.VMEM((TOK, WIDTH), BF16),
            pltpu.VMEM((9, TOK, GROUP), BF16),
            pltpu.VMEM((3, TOK, GROUP), BF16),
            pltpu.VMEM((3, TOK, GROUP), BF16),
            pltpu.VMEM((9, TOK, GROUP), BF16),
            pltpu.VMEM((16, WIN_TOK, WIN_TOK), F32),
        ],
        compiler_params=pltpu.CompilerParams(vmem_limit_bytes=VMEM_LIMIT),
        cost_estimate=pl.CostEstimate(
            flops=4_000_000_000, bytes_accessed=6_000_000, transcendentals=800_000
        ),
        name="block_pass",
    )(*args)


def unpack_kernel(factor, pack_ref, qkv_ref, proj_ref, table_ref, norm_ref):
    for k in range(12):
        block = pack_ref[k * WIDTH : (k + 1) * WIDTH, :].astype(F32) * factor
        if k < 9:
            qkv_ref[:, k * 128 : (k + 1) * 128] = block
        else:
            proj_ref[:, (k - 9) * 128 : (k - 8) * 128] = block
    table = pack_ref[ROW_TABLE : ROW_TABLE + 96, :].astype(F32) * factor
    for a in range(3):
        for n in range(2):
            table_ref[:, (2 * a + n) * 128 : (2 * a + n + 1) * 128] = table[
                48 * n + 16 * a : 48 * n + 16 * a + 16
            ]
    norm_ref[...] = pack_ref[ROW_NORM : ROW_NORM + 16, :].astype(F32) * factor


def unpack(pack, factor):
    return pl.pallas_call(
        functools.partial(unpack_kernel, factor),
        out_shape=(
            jax.ShapeDtypeStruct((WIDTH, 3 * WIDTH), F32),
            jax.ShapeDtypeStruct((WIDTH, WIDTH), F32),
            jax.ShapeDtypeStruct((16, 768), F32),
            jax.ShapeDtypeStruct((16, 128), F32),
        ),
        in_specs=whole(1),
        out_specs=tuple(whole(4)),
        compiler_params=pltpu.CompilerParams(vmem_limit_bytes=VMEM_LIMIT),
        cost_estimate=pl.CostEstimate(flops=600_000, bytes_accessed=3_600_000, transcendentals=0),
        name="unpack_sums",
    )(pack)


ROW = ("z", "l", "c")
COL = ("h", "x")
ALL = ROW + COL


def shifted(value, row_step, col_step):
    rows = lax.axis_size(ROW)
    cols = lax.axis_size(COL)
    pairs = [
        (r * cols + c, ((r + row_step) % rows) * cols + (c + col_step) % cols)
        for r in range(rows)
        for c in range(cols)
    ]
    return lax.ppermute(value, ALL, pairs)


def sum_scatter(pack, axes):
    count = lax.axis_size(axes)
    got = lax.all_to_all(pack.reshape(count, -1, 128), axes, 0, 0)
    return jnp.sum(got.astype(F32), axis=0).astype(BF16)


def spread(part, axes):
    count = lax.axis_size(axes)
    sent = jnp.broadcast_to(part[None], (count,) + part.shape)
    return lax.all_to_all(sent, axes, 0, 0)


def sum_everywhere(pack):
    part = sum_scatter(pack, ("c",))
    part = sum_scatter(part, ("l", "h", "x"))
    part = jnp.sum(spread(part, ("z",)).astype(F32), axis=0).astype(BF16)
    part = spread(part, ("l", "h", "x")).reshape(-1, 128)
    return spread(part, ("c",)).reshape(PACK_ROWS, 128)


def body(
    frames_in, grad_out, norm_gain, norm_shift, qkv_weight, proj_weight, bias_table, pos_index,
    region_ids,
):
    frame_count, row_count, col_count, _ = frames_in.shape
    token_total = frame_count * row_count * col_count * lax.axis_size(ALL)
    both = (frames_in, grad_out)
    below = shifted(jnp.stack([a[:, :4] for a in both]), -1, 0)
    right = shifted(jnp.stack([a[:, :, :4] for a in both]), 0, -1)
    corner = shifted(jnp.stack([a[:, :4, :4] for a in both]), -1, -1)
    rolled = []
    for n, a in enumerate(both):
        upper = jnp.concatenate([a[:, 4:, 4:], right[n][:, 4:]], axis=2)
        lower = jnp.concatenate([below[n][:, :, 4:], corner[n]], axis=2)
        tile = jnp.concatenate([upper, lower], axis=1)
        rolled.append(jnp.concatenate([tile[1:], tile[:1]], axis=0))

    pos_t = pos_index.T
    table_t = jnp.pad(bias_table.T, ((0, 4), (0, 768 - TABLE_ROWS)))
    bias = gather_bias(pos_t, table_t)
    ids = region_ids.reshape(2, 2, 8, 2, 8).transpose(1, 3, 0, 2, 4).reshape(N_WIN, WIN_TOK)
    branch, back, pack = main_call(
        rolled[0], rolled[1], norm_gain[None], norm_shift[None], qkv_weight, proj_weight, bias,
        ids[:, None, :], ids[:, :, None], pos_t,
    )
    flipped = [jnp.concatenate([a[1:], a[:1]], axis=0) for a in (branch, back)]
    above = shifted(jnp.stack([a[:, 12:, :12] for a in flipped]), 1, 0)
    left = shifted(jnp.stack([a[:, :12, 12:] for a in flipped]), 0, 1)
    angle = shifted(jnp.stack([a[:, 12:, 12:] for a in flipped]), 1, 1)
    outs = []
    for n, a in enumerate(both):
        upper = jnp.concatenate([angle[n], above[n]], axis=2)
        lower = jnp.concatenate([left[n], flipped[n][:, :12, :12]], axis=2)
        moved = jnp.concatenate([upper, lower], axis=1)
        outs.append((a.astype(F32) + moved.astype(F32)).astype(BF16))

    total = sum_everywhere(pack)
    grad_qkv, grad_proj, table, norm = unpack(total, token_total**-0.5)
    grad_table = table[:HEADS, :TABLE_ROWS].T
    grad_gain = norm[0:3].reshape(WIDTH)
    grad_shift = norm[3:6].reshape(WIDTH)
    return outs[0], outs[1], grad_qkv, grad_proj, grad_table, grad_gain, grad_shift


def solution(mesh):
    rows, cols = mesh.devices.shape
    fine = Mesh(mesh.devices.reshape(rows // 4, 2, 2, 2, cols // 2), ALL)
    tile = P(None, ROW, COL, None)
    return jax.shard_map(
        body,
        mesh=fine,
        in_specs=(tile, tile, P(), P(), P(), P(), P(), P(), P(None, ROW, COL)),
        out_specs=(tile, tile, P(), P(), P(), P(), P()),
        check_vma=False,
    )
```

time: 579 us -> 118 us (0.20)
  waiting for transfers between devices: 248 us -> 22.2 us
  other arithmetic: 108 us -> 4.1 us
  local copies, waits for them, and re-layouts: 79.3 us -> 9.53 us
  blocking collectives: 82.7 us -> 15 us
  Pallas kernels: 0 us -> 31.1 us
  matrix products: 28.7 us -> 0 us
  starting transfers between devices: 16 us -> 34.1 us
  between operations: 14.6 us -> 1.08 us
    psum x1 -> x0, waiting for transfers between devices: 242 us -> none  [backward_all(): lax.psum((grad_proj, grad_qkv_w, grad_table, grad_gain, grad_shift), ('ro...]
    scatter-add x1 -> x0, other arithmetic: 87.7 us -> none  [backward_all(): jax.ops.segment_sum(table_terms.reshape(HEADS, -1).T, pos_index.reshape(-...]
    psum x1 -> x0, blocking collectives: 82.7 us -> none  [backward_all(): lax.psum((grad_proj, grad_qkv_w, grad_table, grad_gain, grad_shift), ('ro...]
    gather x2 -> x0, local copies, waits for them, and re-layouts: 61.4 us -> none  [body(): position_bias = jnp.take(bias_table, pos_index, axis=0).transpose(2, 0, 1)]
    pallas_call x0 -> x3, Pallas kernels: none -> 31.1 us  [the longest x1 25.5 us: main_call(): pl.pallas_call(main_kernel, out_shape=(tile, tile, jax.ShapeDtypeStruct((...]
    dot_general x12 -> x0, matrix products: 28.7 us -> none  [the longest x1 6.46 us: back_group(): jnp.einsum('whqk,wqhd->wkhd', score_bf16, queries, preferred_element_type...]
    all_to_all x0 -> x3, waiting for transfers between devices: none -> 19.6 us  [the longest x2 12.1 us: spread(): return lax.all_to_all(sent, axes, 0, 0)]
    all_to_all x0 -> x2, blocking collectives: none -> 15 us  [the longest x1 8.41 us: spread(): return lax.all_to_all(sent, axes, 0, 0)]
  transfers between devices with their start and end apart: 9 -> 9, of which waited for: 3 -> 4; matrix products, arithmetic and copies ran while one was open for 31% -> 7% of each run, Pallas kernels for 0% -> 3%
where the time goes in v1:
time: 118 us; the launch traced here: 117 us
  starting transfers between devices  34.1 us (29%)
  Pallas kernels  31.1 us (26%)
  waiting for transfers between devices  22.2 us (19%)
  blocking collectives  15 us (13%)
  local copies, waits for them, and re-layouts  9.53 us (8%)
  other arithmetic  4.1 us (3%)
    pallas_call x1, Pallas kernels, main_call(): pl.pallas_call(main_kernel, out_shape=(tile, tile, jax.ShapeDtypeStruct((...  25.5 us
    ppermute x6, starting transfers between devices, shifted(): return lax.ppermute(value, ALL, pairs)  20.3 us
    all_to_all x2, waiting for transfers between devices, spread(): return lax.all_to_all(sent, axes, 0, 0)  12.1 us
    all_to_all x2, starting transfers between devices, spread(): return lax.all_to_all(sent, axes, 0, 0)  8.76 us
    all_to_all x1, blocking collectives, spread(): return lax.all_to_all(sent, axes, 0, 0)  8.41 us
    all_to_all x1, waiting for transfers between devices, sum_scatter(): got = lax.all_to_all(pack.reshape(count, -1, 128), axes, 0, 0)  7.49 us
    all_to_all x1, blocking collectives, sum_scatter(): got = lax.all_to_all(pack.reshape(count, -1, 128), axes, 0, 0)  6.62 us
    all_to_all x1, starting transfers between devices, sum_scatter(): got = lax.all_to_all(pack.reshape(count, -1, 128), axes, 0, 0)  5.01 us
  transfers between devices with their start and end apart: 9, of which 4 were waited for; matrix products, arithmetic and copies ran while one was open for 7% of the time, Pallas kernels for 3%

profile of v1, /device:TPU:1, one launch (start us, length us, event | category | flops | bytes accessed | tf_op | source)
XLA Modules:
  0.0 117.2 jit_solution(4928638430217157268)
XLA Ops:
  1.6 6.6 %collective-permute-start.2 = (bf16[2,2,4,4,384]{4,3,2,1,0:T(4,128)(2,1)S(1)}, bf16[2,2,4,4,384]{4,3,2,1,0:T(4,128)(2,1)S(1)}, u32[]{:S(2)}, u32[]{:S(2)}) collective-permute-start(bf16[2,2,4,4,384]{4,3,2,1,0:T(4,128)(2,1)S(1)} %pad_maximum_fusion.8), channel_id=1, source_target_pairs={{0,255},{1,248},{2,249},{3,250},{4,251},{5,252},{6,253},{7,254},{8... | collective-permute-start | bytes 147464 | tf_op jit(solution)/shard_map/ppermute | solution.py:282
  8.2 1.0 slice_bitcast_fusion.6
  9.2 5.0 %collective-permute-start.1 = (bf16[2,2,4,16,384]{4,3,2,1,0:T(8,128)(2,1)S(1)}, bf16[2,2,4,16,384]{4,3,2,1,0:T(8,128)(2,1)S(1)}, u32[]{:S(2)}, u32[]{:S(2)}) collective-permute-start(bf16[2,2,4,16,384]{4,3,2,1,0:T(8,128)(2,1)S(1)} %pad_maximum_fusion.5), channel_id=1, source_target_pairs={{0,248},{1,249},{2,250},{3,251},{4,252},{5,253},{6,254},{7,255},{8... | collective-permute-start | bytes 589832 | tf_op jit(solution)/shard_map/ppermute | solution.py:282
  14.3 1.1 slice_bitcast_fusion.8
  15.5 1.5 %collective-permute-start = (bf16[2,2,16,4,384]{4,3,2,1,0:T(4,128)(2,1)S(1)}, bf16[2,2,16,4,384]{4,3,2,1,0:T(4,128)(2,1)S(1)}, u32[]{:S(2)}, u32[]{:S(2)}) collective-permute-start(bf16[2,2,16,4,384]{4,3,2,1,0:T(4,128)(2,1)S(1)} %pad_maximum_fusion.4), channel_id=1, source_target_pairs={{0,7},{1,0},{2,1},{3,2},{4,3},{5,4},{6,5},{7,6},{8,15},{9,8},{10,9... | collective-permute-start | bytes 589832 | tf_op jit(solution)/shard_map/ppermute | solution.py:282
  18.9 4.1 %gather_bias.1.bias_ref = f32[12,128,128]{2,1,0:T(8,128)} custom-call(s32[128,128]{1,0:T(8,128)} %bitcast.68, f32[16,768]{1,0:T(8,128)} %pad.4.table_ref), custom_call_target="tpu_custom_call" | custom-call | flops 4000000 | bytes 900000 | tf_op jit(solution)/shard_map/gather_bias/pallas_call | solution.py:63
  23.8 0.9 copy-done
  25.1 25.5 %block_pass.1 = (bf16[2,16,16,384]{3,2,1,0:T(8,128)(2,1)S(1)}, bf16[2,16,16,384]{3,2,1,0:T(8,128)(2,1)S(1)}, bf16[4864,128]{1,0:T(8,128)(2,1)}) custom-call(bf16[2,16,16,384]{3,2,1,0:T(8,128)(2,1)S(1)} %pad_maximum_fusion.2.x_ref, bf16[2,16,16,384]{3,2,1,0:T(8,128)(2,1)S(1)} %pad_maximum_fusion.3.g_ref, f32[1,384]{1,0:T(1,128)S(1)} %broadcast_in_dim.12.gain_ref, ...), custom_call_target="tpu_custom_call" | custom-call | flops 4000000000 | bytes 6000000 | tf_op jit(solution)/shard_map/block_pass/pallas_call | solution.py:212
  50.6 6.6 %all_to_all.25 = bf16[2,2432,128]{2,1,0:T(8,128)(2,1)S(1)} all-to-all(bf16[2,2432,128]{2,1,0:T(8,128)(2,1)} %bitcast.71), channel_id=1, replica_groups=mesh['z'=8,'l'=2,'c'=2,'h'=2,'x'=4] {'c'}, dimensions={0} | all-to-all | bytes 2490368 | tf_op jit(solution)/shard_map/all_to_all | solution.py:287
  57.3 1.2 %reduce_sum.36 = bf16[2432,128]{1,0:T(8,128)(2,1)} reduce(bf16[2,2432,128]{2,1,0:T(8,128)(2,1)S(1)} %all_to_all.25, bf16[]{:T(256)} %constant.7.clone.1), dimensions={0}, to_apply=%region_0.1 | reduce | flops 311296 | bytes 1867778 | tf_op jit(solution)/shard_map/reduce_sum | solution.py:288
  58.5 5.0 %all-to-all-start.1 = ((bf16[16,152,128]{2,1,0:T(8,128)(2,1)}), bf16[16,152,128]{2,1,0:T(8,128)(2,1)S(1)}, u32[]{:S(2)}, u32[]{:S(2)}) async-start(bf16[16,152,128]{2,1,0:T(8,128)(2,1)} %bitcast.28), calls=%async_computation.1 | async-start | bytes 1245184 | tf_op jit(solution)/shard_map/all_to_all | solution.py:287
  63.6 3.2 %collective-permute-start.3 = (bf16[2,2,4,4,384]{4,3,2,1,0:T(4,128)(2,1)S(1)}, bf16[2,2,4,4,384]{4,3,2,1,0:T(4,128)(2,1)S(1)}, u32[]{:S(2)}, u32[]{:S(2)}) collective-permute-start(bf16[2,2,4,4,384]{4,3,2,1,0:T(4,128)(2,1)S(1)} %pad_maximum_fusion.9), channel_id=1, source_target_pairs={{0,9},{1,10},{2,11},{3,12},{4,13},{5,14},{6,15},{7,8},{8,17},{9,18... | collective-permute-start | bytes 147464 | tf_op jit(solution)/shard_map/ppermute | solution.py:282
  67.0 1.3 %collective-permute-start.5 = (bf16[2,2,12,4,384]{4,3,2,1,0:T(4,128)(2,1)S(1)}, bf16[2,2,12,4,384]{4,3,2,1,0:T(4,128)(2,1)S(1)}, u32[]{:S(2)}, u32[]{:S(2)}) collective-permute-start(bf16[2,2,12,4,384]{4,3,2,1,0:T(4,128)(2,1)S(1)} %pad_maximum_fusion.7), channel_id=1, source_target_pairs={{0,1},{1,2},{2,3},{3,4},{4,5},{5,6},{6,7},{7,0},{8,9},{9,10},{10,1... | collective-permute-start | bytes 442376 | tf_op jit(solution)/shard_map/ppermute | solution.py:282
  68.3 7.5 %all-to-all-done.1 = bf16[16,152,128]{2,1,0:T(8,128)(2,1)S(1)} async-done(((bf16[16,152,128]{2,1,0:T(8,128)(2,1)}), bf16[16,152,128]{2,1,0:T(8,128)(2,1)S(1)}, u32[]{:S(2)}, u32[]{:S(2)}) %all-to-all-start.1) | async-done | bytes 622624 | tf_op jit(solution)/shard_map/all_to_all | solution.py:287
  76.6 3.4 %all-to-all-start.2 = ((bf16[8,152,128]{2,1,0:T(8,128)(2,1)}), bf16[8,152,128]{2,1,0:T(8,128)(2,1)S(1)}, u32[]{:S(2)}, u32[]{:S(2)}) async-start(bf16[8,152,128]{2,1,0:T(8,128)(2,1)} %broadcast_in_dim.27), calls=%async_computation.2 | async-start | bytes 622592 | tf_op jit(solution)/shard_map/all_to_all | solution.py:294
  80.1 2.8 %collective-permute-start.4 = (bf16[2,2,4,12,384]{4,3,2,1,0:T(8,128)(2,1)S(1)}, bf16[2,2,4,12,384]{4,3,2,1,0:T(8,128)(2,1)S(1)}, u32[]{:S(2)}, u32[]{:S(2)}) collective-permute-start(bf16[2,2,4,12,384]{4,3,2,1,0:T(8,128)(2,1)S(1)} %pad_maximum_fusion.6), channel_id=1, source_target_pairs={{0,8},{1,9},{2,10},{3,11},{4,12},{5,13},{6,14},{7,15},{8,16},{9,17... | collective-permute-start | bytes 442376 | tf_op jit(solution)/shard_map/ppermute | solution.py:282
  82.9 2.6 %collective-permute-done.4 = bf16[2,2,4,12,384]{4,3,2,1,0:T(8,128)(2,1)S(1)} collective-permute-done((bf16[2,2,4,12,384]{4,3,2,1,0:T(8,128)(2,1)S(1)}, bf16[2,2,4,12,384]{4,3,2,1,0:T(8,128)(2,1)S(1)}, u32[]{:S(2)}, u32[]{:S(2)}) %collective-permute-start.4) | collective-permute-done | bytes 147488 | tf_op jit(solution)/shard_map/ppermute | solution.py:282
  85.5 4.4 %all-to-all-done.2 = bf16[8,152,128]{2,1,0:T(8,128)(2,1)S(1)} async-done(((bf16[8,152,128]{2,1,0:T(8,128)(2,1)}), bf16[8,152,128]{2,1,0:T(8,128)(2,1)S(1)}, u32[]{:S(2)}, u32[]{:S(2)}) %all-to-all-start.2) | async-done | bytes 311328 | tf_op jit(solution)/shard_map/all_to_all | solution.py:294
  90.9 5.3 %all-to-all-start.3 = ((bf16[16,152,128]{2,1,0:T(8,128)(2,1)}), bf16[16,152,128]{2,1,0:T(8,128)(2,1)S(1)}, u32[]{:S(2)}, u32[]{:S(2)}) async-start(bf16[16,152,128]{2,1,0:T(8,128)(2,1)} %broadcast_in_dim.28), calls=%async_computation.3 | async-start | bytes 1245184 | tf_op jit(solution)/shard_map/all_to_all | solution.py:294
  96.3 1.0 add_convert_fusion.1
  97.3 0.9 add_convert_fusion
  98.2 7.7 %all-to-all-done.3 = bf16[16,152,128]{2,1,0:T(8,128)(2,1)S(1)} async-done(((bf16[16,152,128]{2,1,0:T(8,128)(2,1)}), bf16[16,152,128]{2,1,0:T(8,128)(2,1)S(1)}, u32[]{:S(2)}, u32[]{:S(2)}) %all-to-all-start.3) | async-done | bytes 622624 | tf_op jit(solution)/shard_map/all_to_all | solution.py:294
  106.0 8.4 %all_to_all.26 = bf16[2,2432,128]{2,1,0:T(8,128)(2,1)S(1)} all-to-all(bf16[2,2432,128]{2,1,0:T(8,128)(2,1)S(1)} %broadcast_in_dim.30), channel_id=1, replica_groups=mesh['z'=8,'l'=2,'c'=2,'h'=2,'x'=4] {'c'}, dimensions={0} | all-to-all | bytes 2490368 | tf_op jit(solution)/shard_map/all_to_all | solution.py:294
  114.5 1.5 %unpack_sums.1 = (f32[384,1152]{1,0:T(8,128)}, f32[384,384]{1,0:T(8,128)}, f32[16,768]{1,0:T(8,128)S(1)}, f32[16,128]{1,0:T(8,128)S(1)}) custom-call(bf16[4864,128]{1,0:T(8,128)(2,1)S(1)} %bitcast.67), custom_call_target="tpu_custom_call" | custom-call | flops 600000 | bytes 3600000 | tf_op jit(solution)/shard_map/unpack_sums/pallas_call | solution.py:253
  (74 shorter events, 7.6 us)
Async XLA Ops:
  0.6 16.7 %copy-start.4 = (bf16[2,16,16,384]{3,2,1,0:T(8,128)(2,1)S(1)}, bf16[2,16,16,384]{3,2,1,0:T(8,128)(2,1)}, u32[]{:S(2)}) copy-start(bf16[2,16,16,384]{3,2,1,0:T(8,128)(2,1)} %param.9) | copy-start | bytes 1179652
  0.6 16.4 %copy-start.8 = (s32[2,16,16]{2,1,0:T(8,128)S(1)}, s32[2,16,16]{2,1,0:T(8,128)}, u32[]{:S(2)}) copy-start(s32[2,16,16]{2,1,0:T(8,128)} %param.17) | copy-start | bytes 6148
  1.6 15.8 %copy-start.5 = (bf16[2,16,16,384]{3,2,1,0:T(8,128)(2,1)S(1)}, bf16[2,16,16,384]{3,2,1,0:T(8,128)(2,1)}, u32[]{:S(2)}) copy-start(bf16[2,16,16,384]{3,2,1,0:T(8,128)(2,1)} %param.10) | copy-start | bytes 1179652
  1.6 21.4 %collective-permute-start.2 = (bf16[2,2,4,4,384]{4,3,2,1,0:T(4,128)(2,1)S(1)}, bf16[2,2,4,4,384]{4,3,2,1,0:T(4,128)(2,1)S(1)}, u32[]{:S(2)}, u32[]{:S(2)}) collective-permute-start(bf16[2,2,4,4,384]{4,3,2,1,0:T(4,128)(2,1)S(1)} %pad_maximum_fusion.8), channel_id=1, source_target_pairs={{0,255},{1,248},{2,249},{3,250},{4,251},{5,252},{6,253},{7,254},{8... | collective-permute-start | bytes 147464 | tf_op jit(solution)/shard_map/ppermute | solution.py:282
  9.2 8.3 %copy-start.9 = (f32[384]{0:T(512)S(1)}, f32[384]{0:T(512)}, u32[]{:S(2)}) copy-start(f32[384]{0:T(512)} %param.11) | copy-start | bytes 4612
  9.2 8.4 %copy-start.10 = (f32[384]{0:T(512)S(1)}, f32[384]{0:T(512)}, u32[]{:S(2)}) copy-start(f32[384]{0:T(512)} %param.12) | copy-start | bytes 4612
  9.2 8.4 %copy-start.6 = (s32[128,128]{1,0:T(8,128)S(1)}, s32[128,128]{1,0:T(8,128)}, u32[]{:S(2)}) copy-start(s32[128,128]{1,0:T(8,128)} %param.16) | copy-start | bytes 196612
  9.2 9.1 %copy-start.7 = (f32[675,12]{0,1:T(8,128)S(1)}, f32[675,12]{0,1:T(8,128)}, u32[]{:S(2)}) copy-start(f32[675,12]{0,1:T(8,128)} %param.15) | copy-start | bytes 97204
  9.2 13.8 %collective-permute-start.1 = (bf16[2,2,4,16,384]{4,3,2,1,0:T(8,128)(2,1)S(1)}, bf16[2,2,4,16,384]{4,3,2,1,0:T(8,128)(2,1)S(1)}, u32[]{:S(2)}, u32[]{:S(2)}) collective-permute-start(bf16[2,2,4,16,384]{4,3,2,1,0:T(8,128)(2,1)S(1)} %pad_maximum_fusion.5), channel_id=1, source_target_pairs={{0,248},{1,249},{2,250},{3,251},{4,252},{5,253},{6,254},{7,255},{8... | collective-permute-start | bytes 589832 | tf_op jit(solution)/shard_map/ppermute | solution.py:282
  15.5 7.7 %collective-permute-start = (bf16[2,2,16,4,384]{4,3,2,1,0:T(4,128)(2,1)S(1)}, bf16[2,2,16,4,384]{4,3,2,1,0:T(4,128)(2,1)S(1)}, u32[]{:S(2)}, u32[]{:S(2)}) collective-permute-start(bf16[2,2,16,4,384]{4,3,2,1,0:T(4,128)(2,1)S(1)} %pad_maximum_fusion.4), channel_id=1, source_target_pairs={{0,7},{1,0},{2,1},{3,2},{4,3},{5,4},{6,5},{7,6},{8,15},{9,8},{10,9... | collective-permute-start | bytes 589832 | tf_op jit(solution)/shard_map/ppermute | solution.py:282
  23.6 1.1 copy-start
  23.6 1.1 copy-start.1
  23.6 1.4 %copy-start.2 = (bf16[384,1152]{1,0:T(8,128)(2,1)S(1)}, bf16[384,1152]{1,0:T(8,128)(2,1)}, u32[]{:S(2)}) copy-start(bf16[384,1152]{1,0:T(8,128)(2,1)} %wqkv_ref.1) | copy-start | bytes 2654212
  23.7 1.5 %copy-start.3 = (bf16[384,384]{1,0:T(8,128)(2,1)S(1)}, bf16[384,384]{1,0:T(8,128)(2,1)}, u32[]{:S(2)}) copy-start(bf16[384,384]{1,0:T(8,128)(2,1)} %wproj_ref.1) | copy-start | bytes 884740
  58.5 17.3 %all-to-all-start.1 = ((bf16[16,152,128]{2,1,0:T(8,128)(2,1)}), bf16[16,152,128]{2,1,0:T(8,128)(2,1)S(1)}, u32[]{:S(2)}, u32[]{:S(2)}) async-start(bf16[16,152,128]{2,1,0:T(8,128)(2,1)} %bitcast.28), calls=%async_computation.1 | async-start | bytes 1245184 | tf_op jit(solution)/shard_map/all_to_all | solution.py:287
  63.6 19.3 %collective-permute-start.3 = (bf16[2,2,4,4,384]{4,3,2,1,0:T(4,128)(2,1)S(1)}, bf16[2,2,4,4,384]{4,3,2,1,0:T(4,128)(2,1)S(1)}, u32[]{:S(2)}, u32[]{:S(2)}) collective-permute-start(bf16[2,2,4,4,384]{4,3,2,1,0:T(4,128)(2,1)S(1)} %pad_maximum_fusion.9), channel_id=1, source_target_pairs={{0,9},{1,10},{2,11},{3,12},{4,13},{5,14},{6,15},{7,8},{8,17},{9,18... | collective-permute-start | bytes 147464 | tf_op jit(solution)/shard_map/ppermute | solution.py:282
  67.0 29.3 %collective-permute-start.5 = (bf16[2,2,12,4,384]{4,3,2,1,0:T(4,128)(2,1)S(1)}, bf16[2,2,12,4,384]{4,3,2,1,0:T(4,128)(2,1)S(1)}, u32[]{:S(2)}, u32[]{:S(2)}) collective-permute-start(bf16[2,2,12,4,384]{4,3,2,1,0:T(4,128)(2,1)S(1)} %pad_maximum_fusion.7), channel_id=1, source_target_pairs={{0,1},{1,2},{2,3},{3,4},{4,5},{5,6},{6,7},{7,0},{8,9},{9,10},{10,1... | collective-permute-start | bytes 442376 | tf_op jit(solution)/shard_map/ppermute | solution.py:282
  76.6 13.3 %all-to-all-start.2 = ((bf16[8,152,128]{2,1,0:T(8,128)(2,1)}), bf16[8,152,128]{2,1,0:T(8,128)(2,1)S(1)}, u32[]{:S(2)}, u32[]{:S(2)}) async-start(bf16[8,152,128]{2,1,0:T(8,128)(2,1)} %broadcast_in_dim.27), calls=%async_computation.2 | async-start | bytes 622592 | tf_op jit(solution)/shard_map/all_to_all | solution.py:294
  80.1 5.4 %collective-permute-start.4 = (bf16[2,2,4,12,384]{4,3,2,1,0:T(8,128)(2,1)S(1)}, bf16[2,2,4,12,384]{4,3,2,1,0:T(8,128)(2,1)S(1)}, u32[]{:S(2)}, u32[]{:S(2)}) collective-permute-start(bf16[2,2,4,12,384]{4,3,2,1,0:T(8,128)(2,1)S(1)} %pad_maximum_fusion.6), channel_id=1, source_target_pairs={{0,8},{1,9},{2,10},{3,11},{4,12},{5,13},{6,14},{7,15},{8,16},{9,17... | collective-permute-start | bytes 442376 | tf_op jit(solution)/shard_map/ppermute | solution.py:282
  90.9 15.0 %all-to-all-start.3 = ((bf16[16,152,128]{2,1,0:T(8,128)(2,1)}), bf16[16,152,128]{2,1,0:T(8,128)(2,1)S(1)}, u32[]{:S(2)}, u32[]{:S(2)}) async-start(bf16[16,152,128]{2,1,0:T(8,128)(2,1)} %broadcast_in_dim.28), calls=%async_computation.3 | async-start | bytes 1245184 | tf_op jit(solution)/shard_map/all_to_all | solution.py:294

commit v2 on v1

--- a/solution.py
+++ b/solution.py
@@ -23,10 +23,11 @@
 ROW_TABLE = 12 * WIDTH
 ROW_NORM = ROW_TABLE + 96
 PACK_ROWS = 4864
+HALF = PACK_ROWS // 2
 
 F32 = jnp.float32
 BF16 = jnp.bfloat16
-VMEM_LIMIT = 50 * 1024 * 1024
+VMEM_LIMIT = 20 * 1024 * 1024
 
 NN = (((1,), (0,)), ((), ()))
 NT = (((1,), (1,)), ((), ()))
@@ -41,16 +42,59 @@
     return [pl.BlockSpec(memory_space=pltpu.VMEM)] * n
 
 
-def bias_kernel(pos_ref, table_ref, bias_ref):
+def in_vmem(shape, dtype):
+    return pltpu.VMEM(shape, dtype)
+
+
+def edge_kernel(x_ref, g_ref, below_ref, right_ref, corner_ref, x_s, g_s, sems):
+    copies = [
+        pltpu.make_async_copy(x_ref, x_s, sems.at[0]),
+        pltpu.make_async_copy(g_ref, g_s, sems.at[1]),
+    ]
+    for copy in copies:
+        copy.start()
+    for n, ref in enumerate((x_s, g_s)):
+        copies[n].wait()
+        below_ref[n] = ref[:, 0:4, :, :]
+        right_ref[n] = ref[:, 4:16, 0:4, :]
+        corner_ref[n] = ref[:, 0:4, 0:4, :]
+
+
+def edges(x, g):
+    return pl.pallas_call(
+        edge_kernel,
+        out_shape=(
+            in_vmem((2, 2, 4, 16, WIDTH), BF16),
+            in_vmem((2, 2, 12, 4, WIDTH), BF16),
+            in_vmem((2, 2, 4, 4, WIDTH), BF16),
+        ),
+        in_specs=[pl.BlockSpec(memory_space=pltpu.HBM)] * 2,
+        out_specs=tuple(whole(3)),
+        scratch_shapes=[
+            pltpu.VMEM((2, 16, 16, WIDTH), BF16),
+            pltpu.VMEM((2, 16, 16, WIDTH), BF16),
+            pltpu.SemaphoreType.DMA((2,)),
+        ],
+        compiler_params=pltpu.CompilerParams(vmem_limit_bytes=VMEM_LIMIT),
+        cost_estimate=pl.CostEstimate(flops=0, bytes_accessed=1_200_000, transcendentals=0),
+        name="edges",
+    )(*(pltpu.with_memory_space_constraint(a, pltpu.HBM) for a in (x, g)))
+
+
+def bias_kernel(pos_ref, table_ref, bias_ref, pos_t_ref, table_s):
+    pos_t_ref[...] = pos_ref[...].T
+    table_s[...] = jnp.zeros_like(table_s)
+    table_s[0:HEADS, 0:TABLE_ROWS] = table_ref[...]
+
     def rows(step, carry):
         at = pl.multiple_of(step * 8, 8)
-        idx = pos_ref[pl.ds(at, 8), :]
+        idx = pos_t_ref[pl.ds(at, 8), :]
         low = idx & 127
         high = idx >> 7
         for h in range(HEADS):
             got = None
             for k in range(6):
-                chunk = jnp.broadcast_to(table_ref[h : h + 1, k * 128 : (k + 1) * 128], (8, 128))
+                chunk = jnp.broadcast_to(table_s[h : h + 1, k * 128 : (k + 1) * 128], (8, 128))
                 part = jnp.take_along_axis(chunk, low, axis=1)
                 got = part if k == 0 else jnp.where(high == k, part, got)
             bias_ref[h, pl.ds(at, 8), :] = got
@@ -59,15 +103,20 @@
     lax.fori_loop(0, 16, rows, 0)
 
 
-def gather_bias(pos_t, table_t):
+def gather_bias(pos_index, table_t):
     return pl.pallas_call(
         bias_kernel,
-        out_shape=jax.ShapeDtypeStruct((HEADS, WIN_TOK, WIN_TOK), F32),
+        out_shape=(
+            in_vmem((HEADS, WIN_TOK, WIN_TOK), F32),
+            in_vmem((WIN_TOK, WIN_TOK), jnp.int32),
+        ),
         in_specs=whole(2),
-        out_specs=pl.BlockSpec(memory_space=pltpu.VMEM),
+        out_specs=tuple(whole(2)),
+        scratch_shapes=[pltpu.VMEM((16, 768), F32)],
+        compiler_params=pltpu.CompilerParams(vmem_limit_bytes=VMEM_LIMIT),
         cost_estimate=pl.CostEstimate(flops=4_000_000, bytes_accessed=900_000, transcendentals=0),
         name="gather_bias",
-    )(pos_t, table_t)
+    )(pos_index, table_t)
 
 
 def window_tokens(ref, wr, wc):
@@ -85,9 +134,9 @@
 
 
 def main_kernel(
-    x_ref, g_ref, gain_ref, shift_ref, wqkv_ref, wproj_ref, bias_ref, id_row_ref, id_col_ref,
-    pos_ref, branch_ref, back_ref, pack_ref,
-    hat_s, inv_s, normed_s, g_s, qkv_s, da_s, att_s, gqkv_s, table_s,
+    x_ref, g_ref, gain_ref, shift_ref, wqkv_ref, wproj_ref, bias_ref, id_ref,
+    pos_ref, me_ref, kept_ref, sent_ref, att_s, hat_s, inv_s, gnorm_ref,
+    normed_s, g_s, qkv_s, da_s, gqkv_s, table_s, shut_s, pack_ref,
 ):
     for wr in range(2):
         for wc in range(2):
@@ -110,6 +159,9 @@
     for k in range(3):
         da_s[k] = part[:, k * GROUP : (k + 1) * GROUP]
 
+    for w in range(N_WIN):
+        ids = jnp.broadcast_to(id_ref[w : w + 1, :], (WIN_TOK, WIN_TOK))
+        shut_s[w] = jnp.where(ids.T == ids, 0.0, -1e30)
     table_s[...] = jnp.zeros_like(table_s)
     lane = lax.broadcasted_iota(jnp.int32, (WIN_TOK, GROUP), 1) // HEAD_DIM
 
@@ -121,7 +173,7 @@
         key = qkv_s[3 + k, rows, :]
         v = qkv_s[6 + k, rows, :]
         da = da_s[k, rows, :]
-        shut = jnp.where(id_col_ref[w] == id_row_ref[w], 0.0, -1e30)
+        shut = shut_s[w]
         zero = jnp.zeros_like(q)
         heads = []
         for h in range(4):
@@ -154,7 +206,6 @@
     lax.fori_loop(0, 12, attend, 0)
 
     attended = jnp.concatenate([att_s[k] for k in range(3)], axis=1)
-    store_tile(branch_ref, mm(attended, wproj_ref[...], NN))
     grad_proj = mm(attended, g_s[...], TN)
     for k in range(3):
         at = ROW_PROJ + k * WIDTH
@@ -172,58 +223,64 @@
     x_hat = hat_s[...]
     grad_gain = jnp.sum(grad_normed * x_hat, axis=0, keepdims=True)
     grad_shift = jnp.sum(grad_normed, axis=0, keepdims=True)
-    scaled = grad_normed * gain_ref[...]
-    grad_rolled = inv_s[:, 0:1] * (
-        scaled
-        - jnp.mean(scaled, axis=-1, keepdims=True)
-        - x_hat * jnp.mean(scaled * x_hat, axis=-1, keepdims=True)
-    )
-    store_tile(back_ref, grad_rolled)
-
-    low_bins = lax.broadcasted_iota(jnp.int32, (256, WIN_TOK), 0)
+    gnorm_ref[...] = grad_normed
+
+    low_bins = lax.broadcasted_iota(jnp.int32, (128, WIN_TOK), 0)
 
     def bins(step, acc):
-        left, right = [], []
-        for n in range(2):
-            j = 2 * step + n
-            idx = pos_ref[pl.ds(j, 1), :]
-            high = idx >> 8
-            terms = table_s[:, j, :]
-            left.append(
-                jnp.concatenate([jnp.where(high == a, terms, 0.0) for a in range(3)], axis=0)
+        at = pl.multiple_of(step * 8, 8)
+        index = pos_ref[pl.ds(at, 8), :]
+        block = jnp.swapaxes(table_s[:, pl.ds(at, 8), :], 0, 1)
+        for n in range(0, 8, 2):
+            left, right = [], []
+            for j in (n, n + 1):
+                idx = index[j : j + 1]
+                high = idx >> 7
+                terms = block[j]
+                left.append(
+                    jnp.concatenate([jnp.where(high == a, terms, 0.0) for a in range(6)], axis=0)
+                )
+                right.append(jnp.where(low_bins == (idx & 127), 1.0, 0.0))
+            acc = acc + mm(
+                jnp.concatenate(left, axis=1).astype(BF16),
+                jnp.concatenate(right, axis=1).astype(BF16),
+                NT,
             )
-            right.append(jnp.where(low_bins == (idx & 255), 1.0, 0.0).astype(BF16))
-        return acc + mm(
-            jnp.concatenate(left, axis=1).astype(BF16), jnp.concatenate(right, axis=1), NT
-        )
-
-    table = lax.fori_loop(0, WIN_TOK // 2, bins, jnp.zeros((48, 256), F32))
-    for n in range(2):
-        at = ROW_TABLE + 48 * n
-        pack_ref[at : at + 48, :] = table[:, 128 * n : 128 * (n + 1)].astype(BF16)
+        return acc
+
+    table = lax.fori_loop(0, WIN_TOK // 8, bins, jnp.zeros((96, 128), F32))
+    pack_ref[ROW_TABLE : ROW_TABLE + 96, :] = table.astype(BF16)
     norm_rows = [a[:, k * 128 : (k + 1) * 128] for a in (grad_gain, grad_shift) for k in range(3)]
     norm_rows.append(jnp.zeros((10, 128), F32))
     pack_ref[ROW_NORM : ROW_NORM + 16, :] = jnp.concatenate(norm_rows, axis=0).astype(BF16)
     pack_ref[ROW_NORM + 16 :, :] = jnp.zeros((PACK_ROWS - ROW_NORM - 16, 128), BF16)
+    me = me_ref[0]
+    kept_ref[...] = pack_ref[pl.ds(pl.multiple_of(me * HALF, HALF), HALF), :]
+    sent_ref[...] = pack_ref[pl.ds(pl.multiple_of((1 - me) * HALF, HALF), HALF), :]
 
 
 def main_call(*args):
-    tile = jax.ShapeDtypeStruct((2, 16, 16, WIDTH), BF16)
     return pl.pallas_call(
         main_kernel,
-        out_shape=(tile, tile, jax.ShapeDtypeStruct((PACK_ROWS, 128), BF16)),
-        in_specs=whole(len(args)),
-        out_specs=tuple(whole(3)),
+        out_shape=(
+            in_vmem((HALF, 128), BF16),
+            in_vmem((HALF, 128), BF16),
+            in_vmem((3, TOK, GROUP), BF16),
+            in_vmem((TOK, WIDTH), F32),
+            in_vmem((TOK, 128), F32),
+            in_vmem((TOK, WIDTH), F32),
+        ),
+        in_specs=whole(len(args) - 1) + [pl.BlockSpec(memory_space=pltpu.SMEM)],
+        out_specs=tuple(whole(6)),
         scratch_shapes=[
-            pltpu.VMEM((TOK, WIDTH), F32),
-            pltpu.VMEM((TOK, 128), F32),
             pltpu.VMEM((TOK, WIDTH), BF16),
             pltpu.VMEM((TOK, WIDTH), BF16),
             pltpu.VMEM((9, TOK, GROUP), BF16),
             pltpu.VMEM((3, TOK, GROUP), BF16),
-            pltpu.VMEM((3, TOK, GROUP), BF16),
             pltpu.VMEM((9, TOK, GROUP), BF16),
             pltpu.VMEM((16, WIN_TOK, WIN_TOK), F32),
+            pltpu.VMEM((N_WIN, WIN_TOK, WIN_TOK), F32),
+            pltpu.VMEM((PACK_ROWS, 128), BF16),
         ],
         compiler_params=pltpu.CompilerParams(vmem_limit_bytes=VMEM_LIMIT),
         cost_estimate=pl.CostEstimate(
@@ -233,7 +290,43 @@
     )(*args)
 
 
-def unpack_kernel(factor, pack_ref, qkv_ref, proj_ref, table_ref, norm_ref):
+def token_kernel(att_ref, hat_ref, inv_ref, gnorm_ref, gain_ref, wproj_ref, branch_ref, back_ref):
+    attended = jnp.concatenate([att_ref[k] for k in range(3)], axis=1)
+    store_tile(branch_ref, mm(attended, wproj_ref[...], NN))
+    x_hat = hat_ref[...]
+    scaled = gnorm_ref[...] * gain_ref[...]
+    store_tile(
+        back_ref,
+        inv_ref[:, 0:1]
+        * (
+            scaled
+            - jnp.mean(scaled, axis=-1, keepdims=True)
+            - x_hat * jnp.mean(scaled * x_hat, axis=-1, keepdims=True)
+        ),
+    )
+
+
+def token_call(*args):
+    tile = in_vmem((2, 16, 16, WIDTH), BF16)
+    return pl.pallas_call(
+        token_kernel,
+        out_shape=(tile, tile),
+        in_specs=whole(len(args)),
+        out_specs=tuple(whole(2)),
+        compiler_params=pltpu.CompilerParams(vmem_limit_bytes=VMEM_LIMIT),
+        cost_estimate=pl.CostEstimate(
+            flops=200_000_000, bytes_accessed=4_000_000, transcendentals=0
+        ),
+        name="token_pass",
+    )(*args)
+
+
+def unpack_kernel(
+    factor, me_ref, own_ref, other_ref, qkv_ref, proj_ref, table_ref, gain_ref, shift_ref, pack_ref
+):
+    me = me_ref[0]
+    pack_ref[pl.ds(pl.multiple_of(me * HALF, HALF), HALF), :] = own_ref[...]
+    pack_ref[pl.ds(pl.multiple_of((1 - me) * HALF, HALF), HALF), :] = other_ref[...]
     for k in range(12):
         block = pack_ref[k * WIDTH : (k + 1) * WIDTH, :].astype(F32) * factor
         if k < 9:
@@ -241,29 +334,68 @@
         else:
             proj_ref[:, (k - 9) * 128 : (k - 8) * 128] = block
     table = pack_ref[ROW_TABLE : ROW_TABLE + 96, :].astype(F32) * factor
-    for a in range(3):
-        for n in range(2):
-            table_ref[:, (2 * a + n) * 128 : (2 * a + n + 1) * 128] = table[
-                48 * n + 16 * a : 48 * n + 16 * a + 16
-            ]
-    norm_ref[...] = pack_ref[ROW_NORM : ROW_NORM + 16, :].astype(F32) * factor
-
-
-def unpack(pack, factor):
+    wide = jnp.concatenate([table[16 * a : 16 * a + 16] for a in range(6)], axis=1)
+    table_ref[...] = wide[0:HEADS, 0:TABLE_ROWS]
+    norm = pack_ref[ROW_NORM : ROW_NORM + 16, :].astype(F32) * factor
+    for n, ref in enumerate((gain_ref, shift_ref)):
+        for k in range(3):
+            ref[:, k * 128 : (k + 1) * 128] = norm[3 * n + k : 3 * n + k + 1]
+
+
+def unpack(me, own, other, factor):
     return pl.pallas_call(
         functools.partial(unpack_kernel, factor),
         out_shape=(
             jax.ShapeDtypeStruct((WIDTH, 3 * WIDTH), F32),
             jax.ShapeDtypeStruct((WIDTH, WIDTH), F32),
-            jax.ShapeDtypeStruct((16, 768), F32),
-            jax.ShapeDtypeStruct((16, 128), F32),
-        ),
-        in_specs=whole(1),
-        out_specs=tuple(whole(4)),
+            jax.ShapeDtypeStruct((HEADS, TABLE_ROWS), F32),
+            jax.ShapeDtypeStruct((1, WIDTH), F32),
+            jax.ShapeDtypeStruct((1, WIDTH), F32),
+        ),
+        in_specs=[pl.BlockSpec(memory_space=pltpu.SMEM)] + whole(2),
+        out_specs=tuple(whole(5)),
+        scratch_shapes=[pltpu.VMEM((PACK_ROWS, 128), BF16)],
         compiler_params=pltpu.CompilerParams(vmem_limit_bytes=VMEM_LIMIT),
         cost_estimate=pl.CostEstimate(flops=600_000, bytes_accessed=3_600_000, transcendentals=0),
         name="unpack_sums",
-    )(pack)
+    )(me, own, other)
+
+
+def add_kernel(a_ref, b_ref, out_ref):
+    out_ref[...] = (a_ref[...].astype(F32) + b_ref[...].astype(F32)).astype(BF16)
+
+
+def add_halves(a, b):
+    return pl.pallas_call(
+        add_kernel,
+        out_shape=in_vmem((HALF, 128), BF16),
+        in_specs=whole(2),
+        out_specs=pl.BlockSpec(memory_space=pltpu.VMEM),
+        compiler_params=pltpu.CompilerParams(vmem_limit_bytes=VMEM_LIMIT),
+        cost_estimate=pl.CostEstimate(flops=300_000, bytes_accessed=1_800_000, transcendentals=0),
+        name="add_halves",
+    )(a, b)
+
+
+def copies_kernel(parts_ref, out_ref):
+    total = parts_ref[0].astype(F32)
+    for n in range(1, parts_ref.shape[0]):
+        total += parts_ref[n].astype(F32)
+    total = total.astype(BF16)
+    for n in range(out_ref.shape[0]):
+        out_ref[n] = total
+
+
+def sum_copies(parts, count):
+    return pl.pallas_call(
+        copies_kernel,
+        out_shape=in_vmem((count,) + parts.shape[1:], BF16),
+        in_specs=whole(1),
+        out_specs=pl.BlockSpec(memory_space=pltpu.VMEM),
+        compiler_params=pltpu.CompilerParams(vmem_limit_bytes=VMEM_LIMIT),
+        cost_estimate=pl.CostEstimate(flops=300_000, bytes_accessed=1_200_000, transcendentals=0),
+        name="sum_copies",
+    )(parts)
 
 
 ROW = ("z", "l", "c")
@@ -282,24 +414,14 @@
     return lax.ppermute(value, ALL, pairs)
 
 
-def sum_scatter(pack, axes):
-    count = lax.axis_size(axes)
-    got = lax.all_to_all(pack.reshape(count, -1, 128), axes, 0, 0)
-    return jnp.sum(got.astype(F32), axis=0).astype(BF16)
-
-
-def spread(part, axes):
-    count = lax.axis_size(axes)
-    sent = jnp.broadcast_to(part[None], (count,) + part.shape)
-    return lax.all_to_all(sent, axes, 0, 0)
-
-
-def sum_everywhere(pack):
-    part = sum_scatter(pack, ("c",))
-    part = sum_scatter(part, ("l", "h", "x"))
-    part = jnp.sum(spread(part, ("z",)).astype(F32), axis=0).astype(BF16)
-    part = spread(part, ("l", "h", "x")).reshape(-1, 128)
-    return spread(part, ("c",)).reshape(PACK_ROWS, 128)
+def exchange(parts, axes):
+    return lax.all_to_all(parts, axes, 0, 0)
+
+
+def swap_cores(value):
+    count = lax.axis_size(ALL)
+    cols = lax.axis_size(COL)
+    return lax.ppermute(value, ALL, [(i, i ^ cols) for i in range(count)])
 
 
 def body(
@@ -309,28 +431,35 @@
     frame_count, row_count, col_count, _ = frames_in.shape
     token_total = frame_count * row_count * col_count * lax.axis_size(ALL)
     both = (frames_in, grad_out)
-    below = shifted(jnp.stack([a[:, :4] for a in both]), -1, 0)
-    right = shifted(jnp.stack([a[:, :, :4] for a in both]), 0, -1)
-    corner = shifted(jnp.stack([a[:, :4, :4] for a in both]), -1, -1)
+    below, right, corner = edges(frames_in, grad_out)
+    below = shifted(below, -1, 0)
+    right = shifted(right, 0, -1)
+    corner = shifted(corner, -1, -1)
     rolled = []
     for n, a in enumerate(both):
-        upper = jnp.concatenate([a[:, 4:, 4:], right[n][:, 4:]], axis=2)
+        upper = jnp.concatenate([a[:, 4:, 4:], right[n]], axis=2)
         lower = jnp.concatenate([below[n][:, :, 4:], corner[n]], axis=2)
         tile = jnp.concatenate([upper, lower], axis=1)
         rolled.append(jnp.concatenate([tile[1:], tile[:1]], axis=0))
 
-    pos_t = pos_index.T
-    table_t = jnp.pad(bias_table.T, ((0, 4), (0, 768 - TABLE_ROWS)))
-    bias = gather_bias(pos_t, table_t)
+    bias, pos_t = gather_bias(pos_index, bias_table.T)
     ids = region_ids.reshape(2, 2, 8, 2, 8).transpose(1, 3, 0, 2, 4).reshape(N_WIN, WIN_TOK)
-    branch, back, pack = main_call(
+    me = lax.axis_index("c").reshape(1)
+    kept, sent, att, hat, inv, gnorm = main_call(
         rolled[0], rolled[1], norm_gain[None], norm_shift[None], qkv_weight, proj_weight, bias,
-        ids[:, None, :], ids[:, :, None], pos_t,
+        ids, pos_t, me,
     )
+    part = add_halves(kept, swap_cores(sent))
+    branch, back = token_call(att, hat, inv, gnorm, norm_gain[None], proj_weight)
+    plane = ("l", "h", "x")
+    part = exchange(part.reshape(lax.axis_size(plane), -1, 128), plane)
+    part, branch, back = lax.optimization_barrier((part, branch, back))
+    part = exchange(sum_copies(part, lax.axis_size("z")), ("z",))
     flipped = [jnp.concatenate([a[1:], a[:1]], axis=0) for a in (branch, back)]
     above = shifted(jnp.stack([a[:, 12:, :12] for a in flipped]), 1, 0)
     left = shifted(jnp.stack([a[:, :12, 12:] for a in flipped]), 0, 1)
     angle = shifted(jnp.stack([a[:, 12:, 12:] for a in flipped]), 1, 1)
+    part, above, left, angle = lax.optimization_barrier((part, above, left, angle))
     outs = []
     for n, a in enumerate(both):
         upper = jnp.concatenate([angle[n], above[n]], axis=2)
@@ -338,12 +467,11 @@
         moved = jnp.concatenate([upper, lower], axis=1)
         outs.append((a.astype(F32) + moved.astype(F32)).astype(BF16))
 
-    total = sum_everywhere(pack)
-    grad_qkv, grad_proj, table, norm = unpack(total, token_total**-0.5)
-    grad_table = table[:HEADS, :TABLE_ROWS].T
-    grad_gain = norm[0:3].reshape(WIDTH)
-    grad_shift = norm[3:6].reshape(WIDTH)
-    return outs[0], outs[1], grad_qkv, grad_proj, grad_table, grad_gain, grad_shift
+    own = exchange(sum_copies(part, lax.axis_size(plane)), plane).reshape(HALF, 128)
+    own, outs = lax.optimization_barrier((own, outs))
+    other = swap_cores(own)
+    grad_qkv, grad_proj, table, gain, shift = unpack(me, own, other, token_total**-0.5)
+    return outs[0], outs[1], grad_qkv, grad_proj, table.T, gain.reshape(WIDTH), shift.reshape(WIDTH)
 
 
 def solution(mesh):

time: 118 us -> 97.5 us (0.83)
  blocking collectives: 15 us -> 0 us
  Pallas kernels: 31.1 us -> 23.9 us
  waiting for transfers between devices: 22.2 us -> 29.3 us
  local copies, waits for them, and re-layouts: 9.53 us -> 5.67 us
    all_to_all x2 -> x0, blocking collectives: 15 us -> none  [the longest x1 8.41 us: spread(): return lax.all_to_all(sent, axes, 0, 0)]
    pallas_call x2 -> x7, Pallas kernels: 29.6 us -> 22.4 us  [the longest x1 15.5 us: main_call(): pl.pallas_call(main_kernel, out_shape=(in_vmem((HALF, 128), BF16), in_vme...]
    ppermute x6, waiting for transfers between devices: 2.6 us -> 8.3 us  [shifted(): return lax.ppermute(value, ALL, pairs)]
    ppermute x0 -> x2, starting transfers between devices: none -> 5.09 us  [swap_cores(): return lax.ppermute(value, ALL, [(i, i ^ cols) for i in range(count)])]
    ppermute x6, starting transfers between devices: 20.3 us -> 15.8 us  [shifted(): return lax.ppermute(value, ALL, pairs)]
    ppermute x0 -> x2, waiting for transfers between devices: none -> 3.71 us  [swap_cores(): return lax.ppermute(value, ALL, [(i, i ^ cols) for i in range(count)])]
    another operation x5 -> x0, local copies, waits for them, and re-layouts: 3.15 us -> none  [the longest x1 1.08 us: body(): right = shifted(jnp.stack([a[:, :, :4] for a in both]), 0, -1)]
    all_to_all x3, waiting for transfers between devices: 19.6 us -> 17.2 us  [exchange(): return lax.all_to_all(parts, axes, 0, 0)]
  transfers between devices with their start and end apart: 9 -> 11, of which waited for: 4 -> 5; matrix products, arithmetic and copies ran while one was open for 7% -> 5% of each run, Pallas kernels for 3% -> 3%
where the time goes in v2:
time: 97.5 us; the launch traced here: 96.9 us
  starting transfers between devices  33.2 us (34%)
  waiting for transfers between devices  29.3 us (30%)
  Pallas kernels  23.9 us (25%)
  local copies, waits for them, and re-layouts  5.67 us (6%)
  other arithmetic  3.82 us (4%)
  between operations  1.05 us (1%)
    all_to_all x3, waiting for transfers between devices, exchange(): return lax.all_to_all(parts, axes, 0, 0)  17.2 us
    ppermute x6, starting transfers between devices, shifted(): return lax.ppermute(value, ALL, pairs)  15.8 us
    pallas_call x1, Pallas kernels, main_call(): pl.pallas_call(main_kernel, out_shape=(in_vmem((HALF, 128), BF16), in_vme...  15.5 us
    all_to_all x3, starting transfers between devices, exchange(): return lax.all_to_all(parts, axes, 0, 0)  12.3 us
    ppermute x6, waiting for transfers between devices, shifted(): return lax.ppermute(value, ALL, pairs)  8.3 us
    ppermute x2, starting transfers between devices, swap_cores(): return lax.ppermute(value, ALL, [(i, i ^ cols) for i in range(count)])  5.09 us
    ppermute x2, waiting for transfers between devices, swap_cores(): return lax.ppermute(value, ALL, [(i, i ^ cols) for i in range(count)])  3.71 us
    unnamed x24, local copies, waits for them, and re-layouts  2.99 us
  transfers between devices with their start and end apart: 11, of which 5 were waited for; matrix products, arithmetic and copies ran while one was open for 5% of the time, Pallas kernels for 3%

profile of v2, /device:TPU:1, one launch (start us, length us, event | category | flops | bytes accessed | tf_op | source)
XLA Modules:
  0.0 96.9 jit_solution(14380525165085814135)
XLA Ops:
  0.7 1.2 %edges.1 = (bf16[2,2,4,16,384]{4,3,2,1,0:T(8,128)(2,1)S(1)}, bf16[2,2,12,4,384]{4,3,2,1,0:T(4,128)(2,1)S(1)}, bf16[2,2,4,4,384]{4,3,2,1,0:T(4,128)(2,1)S(1)}) custom-call(bf16[2,16,16,384]{3,2,1,0:T(8,128)(2,1)} %x_ref.1, bf16[2,16,16,384]{3,2,1,0:T(8,128)(2,1)} %g_ref.1), custom_call_target="tpu_custom_call" | custom-call | bytes 1200000 | tf_op jit(solution)/shard_map/edges/pallas_call | solution.py:64
  1.9 6.6 %collective-permute-start.2 = (bf16[2,2,4,4,384]{4,3,2,1,0:T(4,128)(2,1)S(1)}, bf16[2,2,4,4,384]{4,3,2,1,0:T(4,128)(2,1)S(1)}, u32[]{:S(2)}, u32[]{:S(2)}) collective-permute-start(bf16[2,2,4,4,384]{4,3,2,1,0:T(4,128)(2,1)S(1)} %get-tuple-element.37), channel_id=1, source_target_pairs={{0,255},{1,248},{2,249},{3,250},{4,251},{5,252},{6,253},{7,254},{8... | collective-permute-start | bytes 147464 | tf_op jit(solution)/shard_map/ppermute | solution.py:414
  9.0 6.1 %collective-permute-start.1 = (bf16[2,2,4,16,384]{4,3,2,1,0:T(8,128)(2,1)S(1)}, bf16[2,2,4,16,384]{4,3,2,1,0:T(8,128)(2,1)S(1)}, u32[]{:S(2)}, u32[]{:S(2)}) collective-permute-start(bf16[2,2,4,16,384]{4,3,2,1,0:T(8,128)(2,1)S(1)} %get-tuple-element.36), channel_id=1, source_target_pairs={{0,248},{1,249},{2,250},{3,251},{4,252},{5,253},{6,254},{7,255},{8... | collective-permute-start | bytes 589832 | tf_op jit(solution)/shard_map/ppermute | solution.py:414
  15.2 1.0 %slice.96 = bf16[2,12,12,384]{3,2,1,0:T(8,128)(2,1)S(1)} slice(bf16[2,16,16,384]{3,2,1,0:T(8,128)(2,1)} %x_ref.1), slice={[0:2], [4:16], [4:16], [0:384]} | slice | bytes 442368 | tf_op jit(solution)/shard_map/slice | solution.py:440
  16.2 1.0 %slice.103 = bf16[2,12,12,384]{3,2,1,0:T(8,128)(2,1)S(1)} slice(bf16[2,16,16,384]{3,2,1,0:T(8,128)(2,1)} %g_ref.1), slice={[0:2], [4:16], [4:16], [0:384]} | slice | bytes 442368 | tf_op jit(solution)/shard_map/slice | solution.py:440
  17.5 2.5 %gather_bias.1 = (f32[12,128,128]{2,1,0:T(8,128)S(1)}, s32[128,128]{1,0:T(8,128)S(1)}) custom-call(s32[128,128]{1,0:T(8,128)S(1)} %copy-done.4, f32[12,675]{1,0:T(8,128)S(1)} %bitcast.48), custom_call_target="tpu_custom_call" | custom-call | flops 4000000 | bytes 900000 | tf_op jit(solution)/shard_map/gather_bias/pallas_call | solution.py:107
  21.8 15.5 %block_pass.1 = (bf16[2432,128]{1,0:T(8,128)(2,1)S(1)}, bf16[2432,128]{1,0:T(8,128)(2,1)S(1)}, bf16[3,512,128]{2,1,0:T(8,128)(2,1)S(1)}, f32[512,384]{1,0:T(8,12...) custom-call(bf16[2,16,16,384]{3,2,1,0:T(8,128)(2,1)S(1)} %pad_maximum_fusion.2.x_ref, ...), custom_call_target="tpu_custom_call" | custom-call | flops 4000000000 | bytes 6000000 | tf_op jit(solution)/shard_map/block_pass/pallas_call | solution.py:263
  37.4 2.0 %collective-permute-done.3.b_ref = bf16[2432,128]{1,0:T(8,128)(2,1)S(1)} collective-permute-done((bf16[2432,128]{1,0:T(8,128)(2,1)S(1)}, bf16[2432,128]{1,0:T(8,128)(2,1)S(1)}, u32[]{:S(2)}, u32[]{:S(2)}) %collective-permute-start.3) | collective-permute-done | bytes 622624 | tf_op jit(solution)/shard_map/ppermute | solution.py:424
  39.4 1.0 add_halves.1
  40.4 4.6 %all-to-all-start = ((bf16[16,152,128]{2,1,0:T(8,128)(2,1)}), bf16[16,152,128]{2,1,0:T(8,128)(2,1)S(1)}, u32[]{:S(2)}, u32[]{:S(2)}) async-start(bf16[16,152,128]{2,1,0:T(8,128)(2,1)} %bitcast.9), calls=%async_computation | async-start | bytes 1245184 | tf_op jit(solution)/shard_map/all_to_all | solution.py:418
  45.0 1.0 copy-done.1
  45.9 0.9 copy-done.3
  47.4 9.6 %all-to-all-done.parts_ref = bf16[16,152,128]{2,1,0:T(8,128)(2,1)S(1)} async-done(((bf16[16,152,128]{2,1,0:T(8,128)(2,1)}), bf16[16,152,128]{2,1,0:T(8,128)(2,1)S(1)}, u32[]{:S(2)}, u32[]{:S(2)}) %all-to-all-start) | async-done | bytes 622624 | tf_op jit(solution)/shard_map/all_to_all | solution.py:418
  58.0 4.1 %all-to-all-start.1 = ((bf16[8,152,128]{2,1,0:T(8,128)(2,1)}), bf16[8,152,128]{2,1,0:T(8,128)(2,1)S(1)}, u32[]{:S(2)}, u32[]{:S(2)}) async-start(bf16[8,152,128]{2,1,0:T(8,128)(2,1)} %sum_copies.2), calls=%async_computation.1 | async-start | bytes 622592 | tf_op jit(solution)/shard_map/all_to_all | solution.py:418
  62.9 1.9 %collective-permute-start.4 = (bf16[2,2,4,12,384]{4,3,2,1,0:T(8,128)(2,1)S(1)}, bf16[2,2,4,12,384]{4,3,2,1,0:T(8,128)(2,1)S(1)}, u32[]{:S(2)}, u32[]{:S(2)}) collective-permute-start(bf16[2,2,4,12,384]{4,3,2,1,0:T(8,128)(2,1)S(1)} %pad_maximum_fusion.4), channel_id=1, source_target_pairs={{0,8},{1,9},{2,10},{3,11},{4,12},{5,13},{6,14},{7,15},{8,16},{9,17... | collective-permute-start | bytes 442376 | tf_op jit(solution)/shard_map/ppermute | solution.py:414
  65.1 8.3 %collective-permute-done.6 = bf16[2,2,4,4,384]{4,3,2,1,0:T(4,128)(2,1)S(1)} collective-permute-done((bf16[2,2,4,4,384]{4,3,2,1,0:T(4,128)(2,1)S(1)}, bf16[2,2,4,4,384]{4,3,2,1,0:T(4,128)(2,1)S(1)}, u32[]{:S(2)}, u32[]{:S(2)}) %collective-permute-start.6) | collective-permute-done | bytes 49184 | tf_op jit(solution)/shard_map/ppermute | solution.py:414
  73.5 0.9 sum_copies.3
  74.4 3.6 %all-to-all-start.2 = ((bf16[16,152,128]{2,1,0:T(8,128)(2,1)}), bf16[16,152,128]{2,1,0:T(8,128)(2,1)S(1)}, u32[]{:S(2)}, u32[]{:S(2)}) async-start(bf16[16,152,128]{2,1,0:T(8,128)(2,1)} %sum_copies.3), calls=%async_computation.2 | async-start | bytes 1245184 | tf_op jit(solution)/shard_map/all_to_all | solution.py:418
  78.0 1.0 add_convert_fusion.1
  79.0 0.9 add_convert_fusion
  79.9 7.6 %all-to-all-done.2 = bf16[16,152,128]{2,1,0:T(8,128)(2,1)S(1)} async-done(((bf16[16,152,128]{2,1,0:T(8,128)(2,1)}), bf16[16,152,128]{2,1,0:T(8,128)(2,1)S(1)}, u32[]{:S(2)}, u32[]{:S(2)}) %all-to-all-start.2) | async-done | bytes 622624 | tf_op jit(solution)/shard_map/all_to_all | solution.py:418
  87.5 5.0 %collective-permute-start.7 = (bf16[2432,128]{1,0:T(8,128)(2,1)S(1)}, bf16[2432,128]{1,0:T(8,128)(2,1)S(1)}, u32[]{:S(2)}, u32[]{:S(2)}) collective-permute-start(bf16[2432,128]{1,0:T(8,128)(2,1)S(1)} %bitcast.46), channel_id=1, source_target_pairs={{0,8},{1,9},{2,10},{3,11},{4,12},{5,13},{6,14},{7,15},{8,0},{9,1},... | collective-permute-start | bytes 1867784 | tf_op jit(solution)/shard_map/ppermute | solution.py:424
  92.5 1.7 %collective-permute-done.7.other_ref = bf16[2432,128]{1,0:T(8,128)(2,1)S(1)} collective-permute-done((bf16[2432,128]{1,0:T(8,128)(2,1)S(1)}, bf16[2432,128]{1,0:T(8,128)(2,1)S(1)}, u32[]{:S(2)}, u32[]{:S(2)}) %collective-permute-start.7) | collective-permute-done | bytes 622624 | tf_op jit(solution)/shard_map/ppermute | solution.py:424
  94.2 1.5 %unpack_sums.1 = (f32[384,1152]{1,0:T(8,128)}, f32[384,384]{1,0:T(8,128)}, f32[12,675]{1,0:T(8,128)}, f32[1,384]{1,0:T(1,128)S(1)}, f32[1,384]{1,0:T(1,128)S(1)}) custom-call(s32[1]{0:T(128)} %bitcast.8.me_ref, bf16[2432,128]{1,0:T(8,128)(2,1)S(1)} %bitcast.47, bf16[2432,128]{1,0:T(8,128)(2,1)S(1)} %collective-permute-done.7.other_ref), custom_call_target="tpu_custom_call" | custom-call | flops 600000 | bytes 3600000 | tf_op jit(solution)/shard_map/unpack_sums/pallas_call | solution.py:346
  (65 shorter events, 6.3 us)
Async XLA Ops:
  0.6 16.6 %copy-start.10 = (f32[384]{0:T(512)S(1)}, f32[384]{0:T(512)}, u32[]{:S(2)}) copy-start(f32[384]{0:T(512)} %param.11) | copy-start | bytes 4612
  0.6 16.6 %copy-start.11 = (f32[384]{0:T(512)S(1)}, f32[384]{0:T(512)}, u32[]{:S(2)}) copy-start(f32[384]{0:T(512)} %param.12) | copy-start | bytes 4612
  0.7 16.7 %copy-start.9 = (s32[2,16,16]{2,1,0:T(8,128)S(1)}, s32[2,16,16]{2,1,0:T(8,128)}, u32[]{:S(2)}) copy-start(s32[2,16,16]{2,1,0:T(8,128)} %param.17) | copy-start | bytes 6148
  0.7 16.8 %copy-start.4 = (s32[128,128]{1,0:T(8,128)S(1)}, s32[128,128]{1,0:T(8,128)}, u32[]{:S(2)}) copy-start(s32[128,128]{1,0:T(8,128)} %pos_ref.1) | copy-start | bytes 196612
  0.7 16.8 %copy-start.5 = (f32[675,12]{0,1:T(8,128)S(1)}, f32[675,12]{0,1:T(8,128)}, u32[]{:S(2)}) copy-start(f32[675,12]{0,1:T(8,128)} %param.15) | copy-start | bytes 97204
  1.9 18.1 %collective-permute-start.2 = (bf16[2,2,4,4,384]{4,3,2,1,0:T(4,128)(2,1)S(1)}, bf16[2,2,4,4,384]{4,3,2,1,0:T(4,128)(2,1)S(1)}, u32[]{:S(2)}, u32[]{:S(2)}) collective-permute-start(bf16[2,2,4,4,384]{4,3,2,1,0:T(4,128)(2,1)S(1)} %get-tuple-element.37), channel_id=1, source_target_pairs={{0,255},{1,248},{2,249},{3,250},{4,251},{5,252},{6,253},{7,254},{8... | collective-permute-start | bytes 147464 | tf_op jit(solution)/shard_map/ppermute | solution.py:414
  8.5 11.6 %collective-permute-start = (bf16[2,2,12,4,384]{4,3,2,1,0:T(4,128)(2,1)S(1)}, bf16[2,2,12,4,384]{4,3,2,1,0:T(4,128)(2,1)S(1)}, u32[]{:S(2)}, u32[]{:S(2)}) collective-permute-start(bf16[2,2,12,4,384]{4,3,2,1,0:T(4,128)(2,1)S(1)} %get-tuple-element.35), channel_id=1, source_target_pairs={{0,7},{1,0},{2,1},{3,2},{4,3},{5,4},{6,5},{7,6},{8,15},{9,8},{10,9... | collective-permute-start | bytes 442376 | tf_op jit(solution)/shard_map/ppermute | solution.py:414
  9.0 11.1 %collective-permute-start.1 = (bf16[2,2,4,16,384]{4,3,2,1,0:T(8,128)(2,1)S(1)}, bf16[2,2,4,16,384]{4,3,2,1,0:T(8,128)(2,1)S(1)}, u32[]{:S(2)}, u32[]{:S(2)}) collective-permute-start(bf16[2,2,4,16,384]{4,3,2,1,0:T(8,128)(2,1)S(1)} %get-tuple-element.36), channel_id=1, source_target_pairs={{0,248},{1,249},{2,250},{3,251},{4,252},{5,253},{6,254},{7,255},{8... | collective-permute-start | bytes 589832 | tf_op jit(solution)/shard_map/ppermute | solution.py:414
  20.5 1.0 copy-start
  20.5 1.3 %copy-start.6 = (bf16[384,1152]{1,0:T(8,128)(2,1)S(1)}, bf16[384,1152]{1,0:T(8,128)(2,1)}, u32[]{:S(2)}) copy-start(bf16[384,1152]{1,0:T(8,128)(2,1)} %wqkv_ref.1) | copy-start | bytes 2654212
  37.3 3.1 %copy-start.2 = (f32[512,128]{1,0:T(8,128)}, f32[512,128]{1,0:T(8,128)S(1)}, u32[]{:S(2)}) copy-start(f32[512,128]{1,0:T(8,128)S(1)} %get-tuple-element.44.inv_ref) | copy-start | bytes 786436
  37.3 2.1 %collective-permute-start.3 = (bf16[2432,128]{1,0:T(8,128)(2,1)S(1)}, bf16[2432,128]{1,0:T(8,128)(2,1)S(1)}, u32[]{:S(2)}, u32[]{:S(2)}) collective-permute-start(bf16[2432,128]{1,0:T(8,128)(2,1)S(1)} %get-tuple-element.41), channel_id=1, source_target_pairs={{0,8},{1,9},{2,10},{3,11},{4,12},{5,13},{6,14},{7,15},{8,0},{9,1},... | collective-permute-start | bytes 1867784 | tf_op jit(solution)/shard_map/ppermute | solution.py:424
  40.4 16.6 %all-to-all-start = ((bf16[16,152,128]{2,1,0:T(8,128)(2,1)}), bf16[16,152,128]{2,1,0:T(8,128)(2,1)S(1)}, u32[]{:S(2)}, u32[]{:S(2)}) async-start(bf16[16,152,128]{2,1,0:T(8,128)(2,1)} %bitcast.9), calls=%async_computation | async-start | bytes 1245184 | tf_op jit(solution)/shard_map/all_to_all | solution.py:418
  45.0 1.0 copy-start.1
  45.9 0.9 copy-start.3
  58.0 15.4 %all-to-all-start.1 = ((bf16[8,152,128]{2,1,0:T(8,128)(2,1)}), bf16[8,152,128]{2,1,0:T(8,128)(2,1)S(1)}, u32[]{:S(2)}, u32[]{:S(2)}) async-start(bf16[8,152,128]{2,1,0:T(8,128)(2,1)} %sum_copies.2), calls=%async_computation.1 | async-start | bytes 622592 | tf_op jit(solution)/shard_map/all_to_all | solution.py:418
  62.3 11.0 %collective-permute-start.5 = (bf16[2,2,12,4,384]{4,3,2,1,0:T(4,128)(2,1)S(1)}, bf16[2,2,12,4,384]{4,3,2,1,0:T(4,128)(2,1)S(1)}, u32[]{:S(2)}, u32[]{:S(2)}) collective-permute-start(bf16[2,2,12,4,384]{4,3,2,1,0:T(4,128)(2,1)S(1)} %pad_maximum_fusion.5), channel_id=1, source_target_pairs={{0,1},{1,2},{2,3},{3,4},{4,5},{5,6},{6,7},{7,0},{8,9},{9,10},{10,1... | collective-permute-start | bytes 442376 | tf_op jit(solution)/shard_map/ppermute | solution.py:414
  62.9 10.5 %collective-permute-start.4 = (bf16[2,2,4,12,384]{4,3,2,1,0:T(8,128)(2,1)S(1)}, bf16[2,2,4,12,384]{4,3,2,1,0:T(8,128)(2,1)S(1)}, u32[]{:S(2)}, u32[]{:S(2)}) collective-permute-start(bf16[2,2,4,12,384]{4,3,2,1,0:T(8,128)(2,1)S(1)} %pad_maximum_fusion.4), channel_id=1, source_target_pairs={{0,8},{1,9},{2,10},{3,11},{4,12},{5,13},{6,14},{7,15},{8,16},{9,17... | collective-permute-start | bytes 442376 | tf_op jit(solution)/shard_map/ppermute | solution.py:414
  64.8 13.2 %copy-start.7 = (bf16[2,16,16,384]{3,2,1,0:T(8,128)(2,1)S(1)}, bf16[2,16,16,384]{3,2,1,0:T(8,128)(2,1)}, u32[]{:S(2)}) copy-start(bf16[2,16,16,384]{3,2,1,0:T(8,128)(2,1)} %x_ref.1) | copy-start | bytes 1179652
  64.9 8.5 %collective-permute-start.6 = (bf16[2,2,4,4,384]{4,3,2,1,0:T(4,128)(2,1)S(1)}, bf16[2,2,4,4,384]{4,3,2,1,0:T(4,128)(2,1)S(1)}, u32[]{:S(2)}, u32[]{:S(2)}) collective-permute-start(bf16[2,2,4,4,384]{4,3,2,1,0:T(4,128)(2,1)S(1)} %pad_maximum_fusion.6), channel_id=1, source_target_pairs={{0,9},{1,10},{2,11},{3,12},{4,13},{5,14},{6,15},{7,8},{8,17},{9,18... | collective-permute-start | bytes 147464 | tf_op jit(solution)/shard_map/ppermute | solution.py:414
  73.5 5.5 %copy-start.8 = (bf16[2,16,16,384]{3,2,1,0:T(8,128)(2,1)S(1)}, bf16[2,16,16,384]{3,2,1,0:T(8,128)(2,1)}, u32[]{:S(2)}) copy-start(bf16[2,16,16,384]{3,2,1,0:T(8,128)(2,1)} %g_ref.1) | copy-start | bytes 1179652
  74.4 13.1 %all-to-all-start.2 = ((bf16[16,152,128]{2,1,0:T(8,128)(2,1)}), bf16[16,152,128]{2,1,0:T(8,128)(2,1)S(1)}, u32[]{:S(2)}, u32[]{:S(2)}) async-start(bf16[16,152,128]{2,1,0:T(8,128)(2,1)} %sum_copies.3), calls=%async_computation.2 | async-start | bytes 1245184 | tf_op jit(solution)/shard_map/all_to_all | solution.py:418
  87.5 6.7 %collective-permute-start.7 = (bf16[2432,128]{1,0:T(8,128)(2,1)S(1)}, bf16[2432,128]{1,0:T(8,128)(2,1)S(1)}, u32[]{:S(2)}, u32[]{:S(2)}) collective-permute-start(bf16[2432,128]{1,0:T(8,128)(2,1)S(1)} %bitcast.46), channel_id=1, source_target_pairs={{0,8},{1,9},{2,10},{3,11},{4,12},{5,13},{6,14},{7,15},{8,0},{9,1},... | collective-permute-start | bytes 1867784 | tf_op jit(solution)/shard_map/ppermute | solution.py:424

commit v3 on v2

--- a/solution.py
+++ b/solution.py
@@ -55,7 +55,7 @@
         copy.start()
     for n, ref in enumerate((x_s, g_s)):
         copies[n].wait()
-        below_ref[n] = ref[:, 0:4, :, :]
+        below_ref[n] = ref[:, 0:4, :, :].astype(F32)[:, :, 4:16, :].astype(BF16)
         right_ref[n] = ref[:, 4:16, 0:4, :]
         corner_ref[n] = ref[:, 0:4, 0:4, :]
 
@@ -64,24 +64,29 @@
     return pl.pallas_call(
         edge_kernel,
         out_shape=(
-            in_vmem((2, 2, 4, 16, WIDTH), BF16),
+            in_vmem((2, 2, 4, 12, WIDTH), BF16),
             in_vmem((2, 2, 12, 4, WIDTH), BF16),
             in_vmem((2, 2, 4, 4, WIDTH), BF16),
+            in_vmem((2, 16, 16, WIDTH), BF16),
+            in_vmem((2, 16, 16, WIDTH), BF16),
         ),
         in_specs=[pl.BlockSpec(memory_space=pltpu.HBM)] * 2,
-        out_specs=tuple(whole(3)),
-        scratch_shapes=[
-            pltpu.VMEM((2, 16, 16, WIDTH), BF16),
-            pltpu.VMEM((2, 16, 16, WIDTH), BF16),
-            pltpu.SemaphoreType.DMA((2,)),
-        ],
+        out_specs=tuple(whole(5)),
+        scratch_shapes=[pltpu.SemaphoreType.DMA((2,))],
         compiler_params=pltpu.CompilerParams(vmem_limit_bytes=VMEM_LIMIT),
         cost_estimate=pl.CostEstimate(flops=0, bytes_accessed=1_200_000, transcendentals=0),
         name="edges",
     )(*(pltpu.with_memory_space_constraint(a, pltpu.HBM) for a in (x, g)))
 
 
-def bias_kernel(pos_ref, table_ref, bias_ref, pos_t_ref, table_s):
+def bias_kernel(
+    pos_ref, table_ref, gain_ref, shift_ref, wqkv_ref, wproj_ref,
+    bias_ref, pos_t_ref, gain_v, shift_v, wqkv_v, wproj_v, table_s, sems,
+):
+    pairs = ((wqkv_ref, wqkv_v), (wproj_ref, wproj_v), (gain_ref, gain_v), (shift_ref, shift_v))
+    copies = [pltpu.make_async_copy(a, b, sems.at[n]) for n, (a, b) in enumerate(pairs)]
+    for copy in copies:
+        copy.start()
     pos_t_ref[...] = pos_ref[...].T
     table_s[...] = jnp.zeros_like(table_s)
     table_s[0:HEADS, 0:TABLE_ROWS] = table_ref[...]
@@ -101,22 +106,33 @@
         return carry
 
     lax.fori_loop(0, 16, rows, 0)
-
-
-def gather_bias(pos_index, table_t):
+    for copy in copies:
+        copy.wait()
+
+
+def gather_bias(pos_index, table_t, *params):
     return pl.pallas_call(
         bias_kernel,
         out_shape=(
             in_vmem((HEADS, WIN_TOK, WIN_TOK), F32),
             in_vmem((WIN_TOK, WIN_TOK), jnp.int32),
-        ),
-        in_specs=whole(2),
-        out_specs=tuple(whole(2)),
-        scratch_shapes=[pltpu.VMEM((16, 768), F32)],
+        )
+        + tuple(in_vmem(a.shape, a.dtype) for a in params),
+        in_specs=whole(2) + [pl.BlockSpec(memory_space=pltpu.HBM)] * 4,
+        out_specs=tuple(whole(6)),
+        scratch_shapes=[pltpu.VMEM((16, 768), F32), pltpu.SemaphoreType.DMA((4,))],
         compiler_params=pltpu.CompilerParams(vmem_limit_bytes=VMEM_LIMIT),
         cost_estimate=pl.CostEstimate(flops=4_000_000, bytes_accessed=900_000, transcendentals=0),
         name="gather_bias",
-    )(pos_index, table_t)
+    )(
+        pos_index,
+        table_t,
+        *(pltpu.with_memory_space_constraint(a, pltpu.HBM) for a in params),
+    )
+
+
+def row_of(ref):
+    return jnp.concatenate([ref[k * 128 : (k + 1) * 128].reshape(1, 128) for k in range(3)], axis=1)
 
 
 def window_tokens(ref, wr, wc):
@@ -135,9 +151,11 @@
 
 def main_kernel(
     x_ref, g_ref, gain_ref, shift_ref, wqkv_ref, wproj_ref, bias_ref, id_ref,
-    pos_ref, me_ref, kept_ref, sent_ref, att_s, hat_s, inv_s, gnorm_ref,
-    normed_s, g_s, qkv_s, da_s, gqkv_s, table_s, shut_s, pack_ref,
+    pos_ref, me_ref, kept_ref, sent_ref, branch_ref, back_ref,
+    att_s, hat_s, inv_s, normed_s, g_s, qkv_s, da_s, gqkv_s, table_s, shut_s, pack_ref,
 ):
+    gain = row_of(gain_ref)
+    shift = row_of(shift_ref)
     for wr in range(2):
         for wc in range(2):
             at = (2 * wr + wc) * WIN_TOK
@@ -149,7 +167,7 @@
             x_hat = centered * inv_std
             hat_s[rows, :] = x_hat
             inv_s[rows, :] = jnp.broadcast_to(inv_std, (WIN_TOK, 128))
-            normed_s[rows, :] = (x_hat * gain_ref[...] + shift_ref[...]).astype(BF16)
+            normed_s[rows, :] = (x_hat * gain + shift).astype(BF16)
             g_s[rows, :] = window_tokens(g_ref, wr, wc).astype(BF16)
     for p in range(3):
         part = mm(normed_s[...], wqkv_ref[:, p * WIDTH : (p + 1) * WIDTH], NN).astype(BF16)
@@ -180,13 +198,18 @@
             mine = lane == h
             heads.append(tuple(jnp.where(mine, a, zero) for a in (q, key, v, da)))
         probs, grads = [], []
+        q_all, key_all, v_all, da_all = (
+            jnp.concatenate([heads[h][n] for h in range(4)], axis=0) for n in range(4)
+        )
+        score_all = mm(key_all, q, NT)
+        grad_all = mm(v_all, da, NT)
         for h in range(4):
             _, key_h, v_h, _ = heads[h]
-            score = mm(key_h, q, NT) * SCALE + bias_ref[4 * k + h] + shut
+            score = score_all[128 * h : 128 * h + 128] * SCALE + bias_ref[4 * k + h] + shut
             top = jnp.max(score, axis=0, keepdims=True)
             e = jnp.exp(score - top)
             prob = e * (1.0 / jnp.sum(e, axis=0, keepdims=True))
-            grad_prob = mm(v_h, da, NT)
+            grad_prob = grad_all[128 * h : 128 * h + 128]
             inner = jnp.sum(prob * grad_prob, axis=0, keepdims=True)
             grad_score = prob * (grad_prob - inner)
             table_s[4 * k + h] += grad_score
@@ -194,18 +217,16 @@
             grads.append((grad_score * SCALE).astype(BF16))
         prob_rows = jnp.concatenate(probs, axis=0)
         grad_rows = jnp.concatenate(grads, axis=0)
-        q_all, key_all, v_all, da_all = (
-            jnp.concatenate([heads[h][n] for h in range(4)], axis=0) for n in range(4)
-        )
         att_s[k, rows, :] = mm(prob_rows, v_all, TN).astype(BF16)
         gqkv_s[k, rows, :] = mm(grad_rows, key_all, TN).astype(BF16)
         gqkv_s[3 + k, rows, :] = mm(jnp.concatenate(grads, axis=1), q_all, NN).astype(BF16)
         gqkv_s[6 + k, rows, :] = mm(jnp.concatenate(probs, axis=1), da_all, NN).astype(BF16)
         return carry
 
-    lax.fori_loop(0, 12, attend, 0)
+    lax.fori_loop(0, 12, attend, 0, unroll=6)
 
     attended = jnp.concatenate([att_s[k] for k in range(3)], axis=1)
+    store_tile(branch_ref, mm(attended, wproj_ref[...], NN))
     grad_proj = mm(attended, g_s[...], TN)
     for k in range(3):
         at = ROW_PROJ + k * WIDTH
@@ -223,7 +244,16 @@
     x_hat = hat_s[...]
     grad_gain = jnp.sum(grad_normed * x_hat, axis=0, keepdims=True)
     grad_shift = jnp.sum(grad_normed, axis=0, keepdims=True)
-    gnorm_ref[...] = grad_normed
+    scaled = grad_normed * gain
+    store_tile(
+        back_ref,
+        inv_s[:, 0:1]
+        * (
+            scaled
+            - jnp.mean(scaled, axis=-1, keepdims=True)
+            - x_hat * jnp.mean(scaled * x_hat, axis=-1, keepdims=True)
+        ),
+    )
 
     low_bins = lax.broadcasted_iota(jnp.int32, (128, WIN_TOK), 0)
 
@@ -248,7 +278,7 @@
             )
         return acc
 
-    table = lax.fori_loop(0, WIN_TOK // 8, bins, jnp.zeros((96, 128), F32))
+    table = lax.fori_loop(0, WIN_TOK // 8, bins, jnp.zeros((96, 128), F32), unroll=4)
     pack_ref[ROW_TABLE : ROW_TABLE + 96, :] = table.astype(BF16)
     norm_rows = [a[:, k * 128 : (k + 1) * 128] for a in (grad_gain, grad_shift) for k in range(3)]
     norm_rows.append(jnp.zeros((10, 128), F32))
@@ -265,14 +295,15 @@
         out_shape=(
             in_vmem((HALF, 128), BF16),
             in_vmem((HALF, 128), BF16),
-            in_vmem((3, TOK, GROUP), BF16),
-            in_vmem((TOK, WIDTH), F32),
-            in_vmem((TOK, 128), F32),
-            in_vmem((TOK, WIDTH), F32),
+            in_vmem((2, 16, 16, WIDTH), BF16),
+            in_vmem((2, 16, 16, WIDTH), BF16),
         ),
         in_specs=whole(len(args) - 1) + [pl.BlockSpec(memory_space=pltpu.SMEM)],
-        out_specs=tuple(whole(6)),
+        out_specs=tuple(whole(4)),
         scratch_shapes=[
+            pltpu.VMEM((3, TOK, GROUP), BF16),
+            pltpu.VMEM((TOK, WIDTH), F32),
+            pltpu.VMEM((TOK, 128), F32),
             pltpu.VMEM((TOK, WIDTH), BF16),
             pltpu.VMEM((TOK, WIDTH), BF16),
             pltpu.VMEM((9, TOK, GROUP), BF16),
@@ -287,37 +318,6 @@
             flops=4_000_000_000, bytes_accessed=6_000_000, transcendentals=800_000
         ),
         name="block_pass",
-    )(*args)
-
-
-def token_kernel(att_ref, hat_ref, inv_ref, gnorm_ref, gain_ref, wproj_ref, branch_ref, back_ref):
-    attended = jnp.concatenate([att_ref[k] for k in range(3)], axis=1)
-    store_tile(branch_ref, mm(attended, wproj_ref[...], NN))
-    x_hat = hat_ref[...]
-    scaled = gnorm_ref[...] * gain_ref[...]
-    store_tile(
-        back_ref,
-        inv_ref[:, 0:1]
-        * (
-            scaled
-            - jnp.mean(scaled, axis=-1, keepdims=True)
-            - x_hat * jnp.mean(scaled * x_hat, axis=-1, keepdims=True)
-        ),
-    )
-
-
-def token_call(*args):
-    tile = in_vmem((2, 16, 16, WIDTH), BF16)
-    return pl.pallas_call(
-        token_kernel,
-        out_shape=(tile, tile),
-        in_specs=whole(len(args)),
-        out_specs=tuple(whole(2)),
-        compiler_params=pltpu.CompilerParams(vmem_limit_bytes=VMEM_LIMIT),
-        cost_estimate=pl.CostEstimate(
-            flops=200_000_000, bytes_accessed=4_000_000, transcendentals=0
-        ),
-        name="token_pass",
     )(*args)
 
 
@@ -339,7 +339,7 @@
     norm = pack_ref[ROW_NORM : ROW_NORM + 16, :].astype(F32) * factor
     for n, ref in enumerate((gain_ref, shift_ref)):
         for k in range(3):
-            ref[:, k * 128 : (k + 1) * 128] = norm[3 * n + k : 3 * n + k + 1]
+            ref[k * 128 : (k + 1) * 128] = norm[3 * n + k]
 
 
 def unpack(me, own, other, factor):
@@ -349,8 +349,8 @@
             jax.ShapeDtypeStruct((WIDTH, 3 * WIDTH), F32),
             jax.ShapeDtypeStruct((WIDTH, WIDTH), F32),
             jax.ShapeDtypeStruct((HEADS, TABLE_ROWS), F32),
-            jax.ShapeDtypeStruct((1, WIDTH), F32),
-            jax.ShapeDtypeStruct((1, WIDTH), F32),
+            jax.ShapeDtypeStruct((WIDTH,), F32),
+            jax.ShapeDtypeStruct((WIDTH,), F32),
         ),
         in_specs=[pl.BlockSpec(memory_space=pltpu.SMEM)] + whole(2),
         out_specs=tuple(whole(5)),
@@ -431,26 +431,27 @@
     frame_count, row_count, col_count, _ = frames_in.shape
     token_total = frame_count * row_count * col_count * lax.axis_size(ALL)
     both = (frames_in, grad_out)
-    below, right, corner = edges(frames_in, grad_out)
+    below, right, corner, x_tile, g_tile = edges(frames_in, grad_out)
     below = shifted(below, -1, 0)
     right = shifted(right, 0, -1)
     corner = shifted(corner, -1, -1)
     rolled = []
-    for n, a in enumerate(both):
+    for n, a in enumerate((x_tile, g_tile)):
         upper = jnp.concatenate([a[:, 4:, 4:], right[n]], axis=2)
-        lower = jnp.concatenate([below[n][:, :, 4:], corner[n]], axis=2)
+        lower = jnp.concatenate([below[n], corner[n]], axis=2)
         tile = jnp.concatenate([upper, lower], axis=1)
         rolled.append(jnp.concatenate([tile[1:], tile[:1]], axis=0))
 
-    bias, pos_t = gather_bias(pos_index, bias_table.T)
+    bias, pos_t, gain_v, shift_v, wqkv_v, wproj_v = gather_bias(
+        pos_index, bias_table.T, norm_gain, norm_shift, qkv_weight, proj_weight
+    )
     ids = region_ids.reshape(2, 2, 8, 2, 8).transpose(1, 3, 0, 2, 4).reshape(N_WIN, WIN_TOK)
     me = lax.axis_index("c").reshape(1)
-    kept, sent, att, hat, inv, gnorm = main_call(
-        rolled[0], rolled[1], norm_gain[None], norm_shift[None], qkv_weight, proj_weight, bias,
+    kept, sent, branch, back = main_call(
+        rolled[0], rolled[1], gain_v, shift_v, wqkv_v, wproj_v, bias,
         ids, pos_t, me,
     )
     part = add_halves(kept, swap_cores(sent))
-    branch, back = token_call(att, hat, inv, gnorm, norm_gain[None], proj_weight)
     plane = ("l", "h", "x")
     part = exchange(part.reshape(lax.axis_size(plane), -1, 128), plane)
     part, branch, back = lax.optimization_barrier((part, branch, back))
@@ -471,7 +472,7 @@
     own, outs = lax.optimization_barrier((own, outs))
     other = swap_cores(own)
     grad_qkv, grad_proj, table, gain, shift = unpack(me, own, other, token_total**-0.5)
-    return outs[0], outs[1], grad_qkv, grad_proj, table.T, gain.reshape(WIDTH), shift.reshape(WIDTH)
+    return outs[0], outs[1], grad_qkv, grad_proj, table.T, gain, shift
 
 
 def solution(mesh):

time: 97.5 us -> 89.6 us (0.919)
  blocking collectives: 0 us -> 17.4 us
  waiting for transfers between devices: 29.3 us -> 19.3 us
  Pallas kernels: 23.9 us -> 18.4 us
  local copies, waits for them, and re-layouts: 5.67 us -> 1.43 us
  starting transfers between devices: 33.2 us -> 29.1 us
  other arithmetic: 3.82 us -> 2.63 us
    all_to_all x0 -> x1, blocking collectives: none -> 17.4 us  [exchange(): return lax.all_to_all(parts, axes, 0, 0)]
    all_to_all x3 -> x2, waiting for transfers between devices: 17.2 us -> 7.66 us  [exchange(): return lax.all_to_all(parts, axes, 0, 0)]
    all_to_all x3 -> x2, starting transfers between devices: 12.3 us -> 7.69 us  [exchange(): return lax.all_to_all(parts, axes, 0, 0)]
    pallas_call x1, Pallas kernels: 15.5 us -> 11.3 us  [main_call(): pl.pallas_call(main_kernel, out_shape=(in_vmem((HALF, 128), BF16), in_vme...]
    unnamed x24 -> x8, local copies, waits for them, and re-layouts: 2.99 us -> 0.02 us
    slice x2, local copies, waits for them, and re-layouts: 2.08 us -> 0.16 us  [body(): upper = jnp.concatenate([a[:, 4:, 4:], right[n]], axis=2)]
    pallas_call x2 -> x0, other arithmetic: 1.19 us -> none  [unpack(): pl.pallas_call(functools.partial(unpack_kernel, factor), out_shape=(jax.S...]
  transfers between devices with their start and end apart: 11 -> 10, of which waited for: 5 -> 4; matrix products, arithmetic and copies ran while one was open for 5% -> 4% of each run, Pallas kernels for 3% -> 3%
where the time goes in v3:
time: 89.6 us; the launch traced here: 89.2 us
  starting transfers between devices  29.1 us (32%)
  waiting for transfers between devices  19.3 us (22%)
  Pallas kernels  18.4 us (21%)
  blocking collectives  17.4 us (19%)
  other arithmetic  2.63 us (3%)
  local copies, waits for them, and re-layouts  1.43 us (2%)
  between operations  0.93 us (1%)
    all_to_all x1, blocking collectives, exchange(): return lax.all_to_all(parts, axes, 0, 0)  17.4 us
    ppermute x6, starting transfers between devices, shifted(): return lax.ppermute(value, ALL, pairs)  16.6 us
    pallas_call x1, Pallas kernels, main_call(): pl.pallas_call(main_kernel, out_shape=(in_vmem((HALF, 128), BF16), in_vme...  11.3 us
    ppermute x6, waiting for transfers between devices, shifted(): return lax.ppermute(value, ALL, pairs)  7.96 us
    all_to_all x2, starting transfers between devices, exchange(): return lax.all_to_all(parts, axes, 0, 0)  7.69 us
    all_to_all x2, waiting for transfers between devices, exchange(): return lax.all_to_all(parts, axes, 0, 0)  7.66 us
    ppermute x2, starting transfers between devices, swap_cores(): return lax.ppermute(value, ALL, [(i, i ^ cols) for i in range(count)])  4.81 us
    ppermute x2, waiting for transfers between devices, swap_cores(): return lax.ppermute(value, ALL, [(i, i ^ cols) for i in range(count)])  3.71 us
  transfers between devices with their start and end apart: 10, of which 4 were waited for; matrix products, arithmetic and copies ran while one was open for 4% of the time, Pallas kernels for 3%

profile of v3, /device:TPU:1, one launch (start us, length us, event | category | flops | bytes accessed | tf_op | source)
XLA Modules:
  0.0 89.2 jit_solution(12888385425633292580)
XLA Ops:
  0.7 1.2 %edges.1 = (bf16[2,2,4,12,384]{4,3,2,1,0:T(8,128)(2,1)S(1)}, bf16[2,2,12,4,384]{4,3,2,1,0:T(4,128)(2,1)S(1)}, bf16[2,2,4,4,384]{4,3,2,1,0:T(4,128)(2,1)S(1)}, bf...) custom-call(bf16[2,16,16,384]{3,2,1,0:T(8,128)(2,1)} %x_ref.1, bf16[2,16,16,384]{3,2,1,0:T(8,128)(2,1)} %g_ref.1), custom_call_target="tpu_custom_call" | custom-call | bytes 1200000 | tf_op jit(solution)/shard_map/edges/pallas_call | solution.py:64
  1.9 6.6 %collective-permute-start.2 = (bf16[2,2,4,4,384]{4,3,2,1,0:T(4,128)(2,1)S(1)}, bf16[2,2,4,4,384]{4,3,2,1,0:T(4,128)(2,1)S(1)}, u32[]{:S(2)}, u32[]{:S(2)}) collective-permute-start(bf16[2,2,4,4,384]{4,3,2,1,0:T(4,128)(2,1)S(1)} %get-tuple-element.40), channel_id=1, source_target_pairs={{0,255},{1,248},{2,249},{3,250},{4,251},{5,252},{6,253},{7,254},{8... | collective-permute-start | bytes 147464 | tf_op jit(solution)/shard_map/ppermute | solution.py:414
  8.5 0.5 collective-permute-start
  9.0 6.1 %collective-permute-start.1 = (bf16[2,2,4,12,384]{4,3,2,1,0:T(8,128)(2,1)S(1)}, bf16[2,2,4,12,384]{4,3,2,1,0:T(8,128)(2,1)S(1)}, u32[]{:S(2)}, u32[]{:S(2)}) collective-permute-start(bf16[2,2,4,12,384]{4,3,2,1,0:T(8,128)(2,1)S(1)} %get-tuple-element.39), channel_id=1, source_target_pairs={{0,248},{1,249},{2,250},{3,251},{4,252},{5,253},{6,254},{7,255},{8... | collective-permute-start | bytes 442376 | tf_op jit(solution)/shard_map/ppermute | solution.py:414
  15.1 0.8 reshape.29
  16.2 2.6 %gather_bias.1 = (f32[12,128,128]{2,1,0:T(8,128)S(1)}, s32[128,128]{1,0:T(8,128)S(1)}, f32[384]{0:T(512)S(1)}, f32[384]{0:T(512)S(1)}, bf16[384,1152]{1,0:T(8,128)(2,1)S(1)}, /*index=5*/bf16[384,384]{1,0:T(8,128)(2,1)S(1)}) custom-call(s32[128,128]{1,0:T(8,128)S(1)} %copy-done, f32[12,675]{1,0:T(8,128)S(1)} %bitcast.49, f32[384]{0:T(512)} %gain_ref.1, ...), custom_call_target="tpu_custom_call" | custom-call | flops 4000000 | bytes 900000 | tf_op jit(solution)/shard_map/gather_bias/pallas_call | solution.py:114
  18.9 0.2 maximum_maximum_fusion
  19.4 11.3 %block_pass.1 = (bf16[2432,128]{1,0:T(8,128)(2,1)S(1)}, bf16[2432,128]{1,0:T(8,128)(2,1)S(1)}, bf16[2,16,16,384]{3,2,1,0:T(8,128)(2,1)S(1)}, bf16[2,16,16,384]{3,2,1,0:T(8,128)(2,1)S(1)}) custom-call(bf16[2,16,16,384]{3,2,1,0:T(8,128)(2,1)S(1)} %pad_maximum_fusion.2.x_ref, bf16[2,16,16,384]{3,2,1,0:T(8,128)(2,1)S(1)} %pad_maximum_fusion.3.g_ref, ...), custom_call_target="tpu_custom_call" | custom-call | flops 4000000000 | bytes 6000000 | tf_op jit(solution)/shard_map/block_pass/pallas_call | solution.py:293
  30.8 2.0 %collective-permute-done.3.b_ref = bf16[2432,128]{1,0:T(8,128)(2,1)S(1)} collective-permute-done((bf16[2432,128]{1,0:T(8,128)(2,1)S(1)}, bf16[2432,128]{1,0:T(8,128)(2,1)S(1)}, u32[]{:S(2)}, u32[]{:S(2)}) %collective-permute-start.3) | collective-permute-done | bytes 622624 | tf_op jit(solution)/shard_map/ppermute | solution.py:424
  33.0 17.4 %all_to_all.15.parts_ref = bf16[16,152,128]{2,1,0:T(8,128)(2,1)S(1)} all-to-all(bf16[16,152,128]{2,1,0:T(8,128)(2,1)S(1)} %bitcast.48), channel_id=1, replica_groups=mesh['z'=8,'l'=2,'c'=2,'h'=2,'x'=4] {'l','h','x'}, dimensions={0} | all-to-all | bytes 1245184 | tf_op jit(solution)/shard_map/all_to_all | solution.py:418
  50.4 0.8 sum_copies.2
  51.3 4.1 %all-to-all-start.1 = ((bf16[8,152,128]{2,1,0:T(8,128)(2,1)}), bf16[8,152,128]{2,1,0:T(8,128)(2,1)S(1)}, u32[]{:S(2)}, u32[]{:S(2)}) async-start(bf16[8,152,128]{2,1,0:T(8,128)(2,1)} %sum_copies.2), calls=%async_computation.1 | async-start | bytes 622592 | tf_op jit(solution)/shard_map/all_to_all | solution.py:418
  55.6 0.8 collective-permute-start.5
  56.5 2.2 %collective-permute-start.4 = (bf16[2,2,4,12,384]{4,3,2,1,0:T(8,128)(2,1)S(1)}, bf16[2,2,4,12,384]{4,3,2,1,0:T(8,128)(2,1)S(1)}, u32[]{:S(2)}, u32[]{:S(2)}) collective-permute-start(bf16[2,2,4,12,384]{4,3,2,1,0:T(8,128)(2,1)S(1)} %pad_maximum_fusion.4), channel_id=1, source_target_pairs={{0,8},{1,9},{2,10},{3,11},{4,12},{5,13},{6,14},{7,15},{8,16},{9,17... | collective-permute-start | bytes 442376 | tf_op jit(solution)/shard_map/ppermute | solution.py:414
  58.8 0.4 collective-permute-start.6
  59.1 7.9 %collective-permute-done.6 = bf16[2,2,4,4,384]{4,3,2,1,0:T(4,128)(2,1)S(1)} collective-permute-done((bf16[2,2,4,4,384]{4,3,2,1,0:T(4,128)(2,1)S(1)}, bf16[2,2,4,4,384]{4,3,2,1,0:T(4,128)(2,1)S(1)}, u32[]{:S(2)}, u32[]{:S(2)}) %collective-permute-start.6) | collective-permute-done | bytes 49184 | tf_op jit(solution)/shard_map/ppermute | solution.py:414
  67.2 0.9 sum_copies.3
  68.1 3.6 %all-to-all-start.2 = ((bf16[16,152,128]{2,1,0:T(8,128)(2,1)}), bf16[16,152,128]{2,1,0:T(8,128)(2,1)S(1)}, u32[]{:S(2)}, u32[]{:S(2)}) async-start(bf16[16,152,128]{2,1,0:T(8,128)(2,1)} %sum_copies.3), calls=%async_computation.2 | async-start | bytes 1245184 | tf_op jit(solution)/shard_map/all_to_all | solution.py:418
  71.7 1.0 %add_convert_fusion.1 = bf16[2,16,16,384]{3,2,1,0:T(8,128)(2,1)} fusion(bf16[2,16,16,384]{3,2,1,0:T(8,128)(2,1)S(1)} %copy-done.2, bf16[1,16,16,384]{3,2,1,0:T(8,128)(2,1)S(1)} %get-tuple-element.67, bf16[1,16,16,384]{3,2,1,0:T(8,128)(2,1)S(1)} %get-tuple-element.68, bf16[2,12,4,384]{3,2,1,0:T(4,128)(2,1)S(1)} %get-tuple-element.80, ...), kind=kLoop, calls=%fused_computation.1 | loop fusion | flops 2555904 | bytes 1351680 | tf_op jit(solution)/shard_map/convert_element_type | solution.py:469
  72.7 0.9 %add_convert_fusion = bf16[2,16,16,384]{3,2,1,0:T(8,128)(2,1)} fusion(bf16[2,16,16,384]{3,2,1,0:T(8,128)(2,1)S(1)} %copy-done.3, bf16[1,16,16,384]{3,2,1,0:T(8,128)(2,1)S(1)} %get-tuple-element.69, bf16[1,16,16,384]{3,2,1,0:T(8,128)(2,1)S(1)} %get-tuple-element.70, bf16[2,12,4,384]{3,2,1,0:T(4,128)(2,1)S(1)} %get-tuple-element.79, ...), kind=kLoop, calls=%fused_computation | loop fusion | flops 2555904 | bytes 1351680 | tf_op jit(solution)/shard_map/convert_element_type | solution.py:469
  73.6 7.7 %all-to-all-done.2 = bf16[16,152,128]{2,1,0:T(8,128)(2,1)S(1)} async-done(((bf16[16,152,128]{2,1,0:T(8,128)(2,1)}), bf16[16,152,128]{2,1,0:T(8,128)(2,1)S(1)}, u32[]{:S(2)}, u32[]{:S(2)}) %all-to-all-start.2) | async-done | bytes 622624 | tf_op jit(solution)/shard_map/all_to_all | solution.py:418
  81.3 4.7 %collective-permute-start.7 = (bf16[2432,128]{1,0:T(8,128)(2,1)S(1)}, bf16[2432,128]{1,0:T(8,128)(2,1)S(1)}, u32[]{:S(2)}, u32[]{:S(2)}) collective-permute-start(bf16[2432,128]{1,0:T(8,128)(2,1)S(1)} %bitcast.46), channel_id=1, source_target_pairs={{0,8},{1,9},{2,10},{3,11},{4,12},{5,13},{6,14},{7,15},{8,0},{9,1},... | collective-permute-start | bytes 1867784 | tf_op jit(solution)/shard_map/ppermute | solution.py:424
  86.0 1.7 %collective-permute-done.7.other_ref = bf16[2432,128]{1,0:T(8,128)(2,1)S(1)} collective-permute-done((bf16[2432,128]{1,0:T(8,128)(2,1)S(1)}, bf16[2432,128]{1,0:T(8,128)(2,1)S(1)}, u32[]{:S(2)}, u32[]{:S(2)}) %collective-permute-start.7) | collective-permute-done | bytes 622624 | tf_op jit(solution)/shard_map/ppermute | solution.py:424
  87.7 1.5 %unpack_sums.1 = (f32[384,1152]{1,0:T(8,128)}, f32[384,384]{1,0:T(8,128)}, f32[12,675]{1,0:T(8,128)}, f32[384]{0:T(512)}, f32[384]{0:T(512)}) custom-call(s32[1]{0:T(128)} %bitcast.8.me_ref, bf16[2432,128]{1,0:T(8,128)(2,1)S(1)} %bitcast.47, bf16[2432,128]{1,0:T(8,128)(2,1)S(1)} %collective-permute-done.7.other_ref), custom_call_target="tpu_custom_call" | custom-call | flops 600000 | bytes 3600000 | tf_op jit(solution)/shard_map/unpack_sums/pallas_call | solution.py:346
  (41 shorter events, 1.4 us)
Async XLA Ops:
  0.6 15.6 %copy-start = (s32[128,128]{1,0:T(8,128)S(1)}, s32[128,128]{1,0:T(8,128)}, u32[]{:S(2)}) copy-start(s32[128,128]{1,0:T(8,128)} %pos_ref.1) | copy-start | bytes 196612
  0.6 15.6 %copy-start.1 = (f32[675,12]{0,1:T(8,128)S(1)}, f32[675,12]{0,1:T(8,128)}, u32[]{:S(2)}) copy-start(f32[675,12]{0,1:T(8,128)} %param.15) | copy-start | bytes 97204
  1.9 16.9 %collective-permute-start.2 = (bf16[2,2,4,4,384]{4,3,2,1,0:T(4,128)(2,1)S(1)}, bf16[2,2,4,4,384]{4,3,2,1,0:T(4,128)(2,1)S(1)}, u32[]{:S(2)}, u32[]{:S(2)}) collective-permute-start(bf16[2,2,4,4,384]{4,3,2,1,0:T(4,128)(2,1)S(1)} %get-tuple-element.40), channel_id=1, source_target_pairs={{0,255},{1,248},{2,249},{3,250},{4,251},{5,252},{6,253},{7,254},{8... | collective-permute-start | bytes 147464 | tf_op jit(solution)/shard_map/ppermute | solution.py:414
  8.5 10.4 %collective-permute-start = (bf16[2,2,12,4,384]{4,3,2,1,0:T(4,128)(2,1)S(1)}, bf16[2,2,12,4,384]{4,3,2,1,0:T(4,128)(2,1)S(1)}, u32[]{:S(2)}, u32[]{:S(2)}) collective-permute-start(bf16[2,2,12,4,384]{4,3,2,1,0:T(4,128)(2,1)S(1)} %get-tuple-element.38), channel_id=1, source_target_pairs={{0,7},{1,0},{2,1},{3,2},{4,3},{5,4},{6,5},{7,6},{8,15},{9,8},{10,9... | collective-permute-start | bytes 442376 | tf_op jit(solution)/shard_map/ppermute | solution.py:414
  9.0 9.9 %collective-permute-start.1 = (bf16[2,2,4,12,384]{4,3,2,1,0:T(8,128)(2,1)S(1)}, bf16[2,2,4,12,384]{4,3,2,1,0:T(8,128)(2,1)S(1)}, u32[]{:S(2)}, u32[]{:S(2)}) collective-permute-start(bf16[2,2,4,12,384]{4,3,2,1,0:T(8,128)(2,1)S(1)} %get-tuple-element.39), channel_id=1, source_target_pairs={{0,248},{1,249},{2,250},{3,251},{4,252},{5,253},{6,254},{7,255},{8... | collective-permute-start | bytes 442376 | tf_op jit(solution)/shard_map/ppermute | solution.py:414
  30.7 2.1 %collective-permute-start.3 = (bf16[2432,128]{1,0:T(8,128)(2,1)S(1)}, bf16[2432,128]{1,0:T(8,128)(2,1)S(1)}, u32[]{:S(2)}, u32[]{:S(2)}) collective-permute-start(bf16[2432,128]{1,0:T(8,128)(2,1)S(1)} %get-tuple-element.49), channel_id=1, source_target_pairs={{0,8},{1,9},{2,10},{3,11},{4,12},{5,13},{6,14},{7,15},{8,0},{9,1},... | collective-permute-start | bytes 1867784 | tf_op jit(solution)/shard_map/ppermute | solution.py:424
  51.3 15.8 %all-to-all-start.1 = ((bf16[8,152,128]{2,1,0:T(8,128)(2,1)}), bf16[8,152,128]{2,1,0:T(8,128)(2,1)S(1)}, u32[]{:S(2)}, u32[]{:S(2)}) async-start(bf16[8,152,128]{2,1,0:T(8,128)(2,1)} %sum_copies.2), calls=%async_computation.1 | async-start | bytes 622592 | tf_op jit(solution)/shard_map/all_to_all | solution.py:418
  55.6 11.5 %collective-permute-start.5 = (bf16[2,2,12,4,384]{4,3,2,1,0:T(4,128)(2,1)S(1)}, bf16[2,2,12,4,384]{4,3,2,1,0:T(4,128)(2,1)S(1)}, u32[]{:S(2)}, u32[]{:S(2)}) collective-permute-start(bf16[2,2,12,4,384]{4,3,2,1,0:T(4,128)(2,1)S(1)} %pad_maximum_fusion.5), channel_id=1, source_target_pairs={{0,1},{1,2},{2,3},{3,4},{4,5},{5,6},{6,7},{7,0},{8,9},{9,10},{10,1... | collective-permute-start | bytes 442376 | tf_op jit(solution)/shard_map/ppermute | solution.py:414
  56.5 10.6 %collective-permute-start.4 = (bf16[2,2,4,12,384]{4,3,2,1,0:T(8,128)(2,1)S(1)}, bf16[2,2,4,12,384]{4,3,2,1,0:T(8,128)(2,1)S(1)}, u32[]{:S(2)}, u32[]{:S(2)}) collective-permute-start(bf16[2,2,4,12,384]{4,3,2,1,0:T(8,128)(2,1)S(1)} %pad_maximum_fusion.4), channel_id=1, source_target_pairs={{0,8},{1,9},{2,10},{3,11},{4,12},{5,13},{6,14},{7,15},{8,16},{9,17... | collective-permute-start | bytes 442376 | tf_op jit(solution)/shard_map/ppermute | solution.py:414
  58.7 13.0 %copy-start.2 = (bf16[2,16,16,384]{3,2,1,0:T(8,128)(2,1)S(1)}, bf16[2,16,16,384]{3,2,1,0:T(8,128)(2,1)}, u32[]{:S(2)}) copy-start(bf16[2,16,16,384]{3,2,1,0:T(8,128)(2,1)} %x_ref.1) | copy-start | bytes 1179652
  58.8 8.3 %collective-permute-start.6 = (bf16[2,2,4,4,384]{4,3,2,1,0:T(4,128)(2,1)S(1)}, bf16[2,2,4,4,384]{4,3,2,1,0:T(4,128)(2,1)S(1)}, u32[]{:S(2)}, u32[]{:S(2)}) collective-permute-start(bf16[2,2,4,4,384]{4,3,2,1,0:T(4,128)(2,1)S(1)} %pad_maximum_fusion.6), channel_id=1, source_target_pairs={{0,9},{1,10},{2,11},{3,12},{4,13},{5,14},{6,15},{7,8},{8,17},{9,18... | collective-permute-start | bytes 147464 | tf_op jit(solution)/shard_map/ppermute | solution.py:414
  67.2 5.5 %copy-start.3 = (bf16[2,16,16,384]{3,2,1,0:T(8,128)(2,1)S(1)}, bf16[2,16,16,384]{3,2,1,0:T(8,128)(2,1)}, u32[]{:S(2)}) copy-start(bf16[2,16,16,384]{3,2,1,0:T(8,128)(2,1)} %g_ref.1) | copy-start | bytes 1179652
  68.1 13.2 %all-to-all-start.2 = ((bf16[16,152,128]{2,1,0:T(8,128)(2,1)}), bf16[16,152,128]{2,1,0:T(8,128)(2,1)S(1)}, u32[]{:S(2)}, u32[]{:S(2)}) async-start(bf16[16,152,128]{2,1,0:T(8,128)(2,1)} %sum_copies.3), calls=%async_computation.2 | async-start | bytes 1245184 | tf_op jit(solution)/shard_map/all_to_all | solution.py:418
  81.3 6.4 %collective-permute-start.7 = (bf16[2432,128]{1,0:T(8,128)(2,1)S(1)}, bf16[2432,128]{1,0:T(8,128)(2,1)S(1)}, u32[]{:S(2)}, u32[]{:S(2)}) collective-permute-start(bf16[2432,128]{1,0:T(8,128)(2,1)S(1)} %bitcast.46), channel_id=1, source_target_pairs={{0,8},{1,9},{2,10},{3,11},{4,12},{5,13},{6,14},{7,15},{8,0},{9,1},... | collective-permute-start | bytes 1867784 | tf_op jit(solution)/shard_map/ppermute | solution.py:424

commit v4 on v3

--- a/solution.py
+++ b/solution.py
@@ -46,11 +46,14 @@
     return pltpu.VMEM(shape, dtype)
 
 
-def edge_kernel(x_ref, g_ref, below_ref, right_ref, corner_ref, x_s, g_s, sems):
-    copies = [
-        pltpu.make_async_copy(x_ref, x_s, sems.at[0]),
-        pltpu.make_async_copy(g_ref, g_s, sems.at[1]),
-    ]
+def edge_kernel(
+    x_ref, g_ref, pos_ref, table_ref, id_ref,
+    below_ref, right_ref, corner_ref, x_s, g_s, pos_s, table_s, id_s, sems,
+):
+    pairs = (
+        (x_ref, x_s), (g_ref, g_s), (pos_ref, pos_s), (table_ref, table_s), (id_ref, id_s),
+    )
+    copies = [pltpu.make_async_copy(a, b, sems.at[n]) for n, (a, b) in enumerate(pairs)]
     for copy in copies:
         copy.start()
     for n, ref in enumerate((x_s, g_s)):
@@ -58,30 +61,32 @@
         below_ref[n] = ref[:, 0:4, :, :].astype(F32)[:, :, 4:16, :].astype(BF16)
         right_ref[n] = ref[:, 4:16, 0:4, :]
         corner_ref[n] = ref[:, 0:4, 0:4, :]
-
-
-def edges(x, g):
+    for copy in copies[2:]:
+        copy.wait()
+
+
+def edges(*args):
     return pl.pallas_call(
         edge_kernel,
         out_shape=(
             in_vmem((2, 2, 4, 12, WIDTH), BF16),
             in_vmem((2, 2, 12, 4, WIDTH), BF16),
             in_vmem((2, 2, 4, 4, WIDTH), BF16),
-            in_vmem((2, 16, 16, WIDTH), BF16),
-            in_vmem((2, 16, 16, WIDTH), BF16),
-        ),
-        in_specs=[pl.BlockSpec(memory_space=pltpu.HBM)] * 2,
-        out_specs=tuple(whole(5)),
-        scratch_shapes=[pltpu.SemaphoreType.DMA((2,))],
+        )
+        + tuple(in_vmem(a.shape, a.dtype) for a in args),
+        in_specs=[pl.BlockSpec(memory_space=pltpu.HBM)] * 5,
+        out_specs=tuple(whole(8)),
+        scratch_shapes=[pltpu.SemaphoreType.DMA((5,))],
         compiler_params=pltpu.CompilerParams(vmem_limit_bytes=VMEM_LIMIT),
         cost_estimate=pl.CostEstimate(flops=0, bytes_accessed=1_200_000, transcendentals=0),
         name="edges",
-    )(*(pltpu.with_memory_space_constraint(a, pltpu.HBM) for a in (x, g)))
+    )(*(pltpu.with_memory_space_constraint(a, pltpu.HBM) for a in args))
 
 
 def bias_kernel(
-    pos_ref, table_ref, gain_ref, shift_ref, wqkv_ref, wproj_ref,
-    bias_ref, pos_t_ref, gain_v, shift_v, wqkv_v, wproj_v, table_s, sems,
+    pos_ref, table_ref, x_ref, g_ref, id_ref, gain_ref, shift_ref, wqkv_ref, wproj_ref,
+    bias_ref, pos_t_ref, hat_ref, inv_ref, normed_ref, g0_ref, att_ref, gqkv_ref, sums_ref,
+    gain_v, shift_v, wqkv_v, wproj_v, table_s, qkv_s, da_s, sems,
 ):
     pairs = ((wqkv_ref, wqkv_v), (wproj_ref, wproj_v), (gain_ref, gain_v), (shift_ref, shift_v))
     copies = [pltpu.make_async_copy(a, b, sems.at[n]) for n, (a, b) in enumerate(pairs)]
@@ -108,25 +113,49 @@
     lax.fori_loop(0, 16, rows, 0)
     for copy in copies:
         copy.wait()
-
-
-def gather_bias(pos_index, table_t, *params):
+    sums_ref[...] = jnp.zeros_like(sums_ref)
+    first = slice(0, WIN_TOK)
+    x = window_tokens(0, x_ref, None, None, None, 0, 0)
+    g = window_tokens(1, g_ref, None, None, None, 0, 0)
+    normalize(x, g, row_of(gain_v), row_of(shift_v), first, hat_ref, inv_ref, normed_ref, g0_ref)
+    project(first, normed_ref, g0_ref, wqkv_v, wproj_v, qkv_s, da_s)
+    shut = shut_pairs(id_ref, 0)
+    for k in range(3):
+        attend(k, first, shut, bias_ref, qkv_s, da_s, att_ref, gqkv_ref, sums_ref)
+
+
+def gather_bias(pos_index, table_t, x, g, ids, *params):
     return pl.pallas_call(
         bias_kernel,
         out_shape=(
             in_vmem((HEADS, WIN_TOK, WIN_TOK), F32),
             in_vmem((WIN_TOK, WIN_TOK), jnp.int32),
+            in_vmem((WIN_TOK, WIDTH), F32),
+            in_vmem((WIN_TOK, 128), F32),
+            in_vmem((WIN_TOK, WIDTH), BF16),
+            in_vmem((WIN_TOK, WIDTH), BF16),
+            in_vmem((3, WIN_TOK, GROUP), BF16),
+            in_vmem((9, WIN_TOK, GROUP), BF16),
+            in_vmem((16, WIN_TOK, WIN_TOK), F32),
         )
         + tuple(in_vmem(a.shape, a.dtype) for a in params),
-        in_specs=whole(2) + [pl.BlockSpec(memory_space=pltpu.HBM)] * 4,
-        out_specs=tuple(whole(6)),
-        scratch_shapes=[pltpu.VMEM((16, 768), F32), pltpu.SemaphoreType.DMA((4,))],
+        in_specs=whole(5) + [pl.BlockSpec(memory_space=pltpu.HBM)] * 4,
+        out_specs=tuple(whole(13)),
+        scratch_shapes=[
+            pltpu.VMEM((16, 768), F32),
+            pltpu.VMEM((9, WIN_TOK, GROUP), BF16),
+            pltpu.VMEM((3, WIN_TOK, GROUP), BF16),
+            pltpu.SemaphoreType.DMA((4,)),
+        ],
         compiler_params=pltpu.CompilerParams(vmem_limit_bytes=VMEM_LIMIT),
         cost_estimate=pl.CostEstimate(flops=4_000_000, bytes_accessed=900_000, transcendentals=0),
         name="gather_bias",
     )(
         pos_index,
         table_t,
+        x,
+        g,
+        ids,
         *(pltpu.with_memory_space_constraint(a, pltpu.HBM) for a in params),
     )
 
@@ -135,9 +164,22 @@
     return jnp.concatenate([ref[k * 128 : (k + 1) * 128].reshape(1, 128) for k in range(3)], axis=1)
 
 
-def window_tokens(ref, wr, wc):
-    block = ref[:, 8 * wr : 8 * wr + 8, :, :].astype(F32)
-    return block[:, :, 8 * wc : 8 * wc + 8, :].reshape(WIN_TOK, WIDTH)
+def window_tokens(n, tile_ref, below_ref, right_ref, corner_ref, wr, wc):
+    def columns(rows, side):
+        if wc == 0:
+            return rows[:, :, 0:8, :]
+        return jnp.concatenate([rows[:, :, 8:12, :], side().astype(F32)], axis=2)
+
+    top = 4 + 8 * wr
+    own = 8 - 4 * wr
+    rows = columns(
+        tile_ref[:, top : top + own, :, :].astype(F32)[:, :, 4:16, :],
+        lambda: right_ref[n, :, top - 4 : top - 4 + own, :, :],
+    )
+    if wr == 1:
+        lower = columns(below_ref[n].astype(F32), lambda: corner_ref[n])
+        rows = jnp.concatenate([rows, lower], axis=1)
+    return jnp.concatenate([rows[1:], rows[:1]], axis=0).reshape(WIN_TOK, WIDTH)
 
 
 def store_tile(ref, tokens):
@@ -149,81 +191,97 @@
         ref[:, 8 * wr : 8 * wr + 8, :, :] = jnp.concatenate(pair, axis=2).astype(BF16)
 
 
+def normalize(x, g, gain, shift, rows, hat_s, inv_s, normed_s, g_s):
+    centered = x - jnp.mean(x, axis=-1, keepdims=True)
+    variance = jnp.mean(centered * centered, axis=-1, keepdims=True)
+    inv_std = lax.rsqrt(variance + NORM_EPS)
+    x_hat = centered * inv_std
+    hat_s[rows, :] = x_hat
+    inv_s[rows, :] = jnp.broadcast_to(inv_std, (WIN_TOK, 128))
+    normed_s[rows, :] = (x_hat * gain + shift).astype(BF16)
+    g_s[rows, :] = g.astype(BF16)
+
+
+def shut_pairs(id_ref, w):
+    ids = jnp.broadcast_to(id_ref[w : w + 1, :], (WIN_TOK, WIN_TOK))
+    return jnp.where(ids.T == ids, 0.0, -1e30)
+
+
+def project(rows, normed_s, g_s, wqkv_ref, wproj_ref, qkv_s, da_s):
+    for p in range(3):
+        part = mm(normed_s[rows, :], wqkv_ref[:, p * WIDTH : (p + 1) * WIDTH], NN).astype(BF16)
+        for k in range(3):
+            qkv_s[3 * p + k, rows, :] = part[:, k * GROUP : (k + 1) * GROUP]
+    part = mm(g_s[rows, :], wproj_ref[...], NT).astype(BF16)
+    for k in range(3):
+        da_s[k, rows, :] = part[:, k * GROUP : (k + 1) * GROUP]
+
+
+def attend(k, rows, shut, bias_ref, qkv_s, da_s, att_s, gqkv_s, table_s):
+    lane = lax.broadcasted_iota(jnp.int32, (WIN_TOK, GROUP), 1) // HEAD_DIM
+    q = qkv_s[k, rows, :]
+    key = qkv_s[3 + k, rows, :]
+    v = qkv_s[6 + k, rows, :]
+    da = da_s[k, rows, :]
+    zero = jnp.zeros_like(q)
+    q_all, key_all, v_all, da_all = (
+        jnp.concatenate([jnp.where(lane == h, a, zero) for h in range(4)], axis=0)
+        for a in (q, key, v, da)
+    )
+    score_all = mm(key_all, q, NT)
+    grad_all = mm(v_all, da, NT)
+    probs, grads = [], []
+    for h in range(4):
+        score = score_all[128 * h : 128 * h + 128] * SCALE + bias_ref[4 * k + h] + shut
+        top = jnp.max(score, axis=0, keepdims=True)
+        e = jnp.exp(score - top)
+        prob = e * (1.0 / jnp.sum(e, axis=0, keepdims=True))
+        grad_prob = grad_all[128 * h : 128 * h + 128]
+        inner = jnp.sum(prob * grad_prob, axis=0, keepdims=True)
+        grad_score = prob * (grad_prob - inner)
+        table_s[4 * k + h] += grad_score
+        probs.append(prob.astype(BF16))
+        grads.append((grad_score * SCALE).astype(BF16))
+    prob_rows = jnp.concatenate(probs, axis=0)
+    grad_rows = jnp.concatenate(grads, axis=0)
+    att_s[k, rows, :] = mm(prob_rows, v_all, TN).astype(BF16)
+    gqkv_s[k, rows, :] = mm(grad_rows, key_all, TN).astype(BF16)
+    gqkv_s[3 + k, rows, :] = mm(jnp.concatenate(grads, axis=1), q_all, NN).astype(BF16)
+    gqkv_s[6 + k, rows, :] = mm(jnp.concatenate(probs, axis=1), da_all, NN).astype(BF16)
+
+
 def main_kernel(
-    x_ref, g_ref, gain_ref, shift_ref, wqkv_ref, wproj_ref, bias_ref, id_ref,
-    pos_ref, me_ref, kept_ref, sent_ref, branch_ref, back_ref,
+    x_ref, g_ref, below_ref, right_ref, corner_ref, gain_ref, shift_ref, wqkv_ref, wproj_ref, bias_ref, id_ref,
+    pos_ref, hat0_ref, inv0_ref, normed0_ref, g0_ref, att0_ref, gqkv0_ref, table0_ref,
+    me_ref, kept_ref, sent_ref, branch_ref, back_ref,
     att_s, hat_s, inv_s, normed_s, g_s, qkv_s, da_s, gqkv_s, table_s, shut_s, pack_ref,
 ):
     gain = row_of(gain_ref)
     shift = row_of(shift_ref)
-    for wr in range(2):
-        for wc in range(2):
-            at = (2 * wr + wc) * WIN_TOK
-            rows = slice(at, at + WIN_TOK)
-            x = window_tokens(x_ref, wr, wc)
-            centered = x - jnp.mean(x, axis=-1, keepdims=True)
-            variance = jnp.mean(centered * centered, axis=-1, keepdims=True)
-            inv_std = lax.rsqrt(variance + NORM_EPS)
-            x_hat = centered * inv_std
-            hat_s[rows, :] = x_hat
-            inv_s[rows, :] = jnp.broadcast_to(inv_std, (WIN_TOK, 128))
-            normed_s[rows, :] = (x_hat * gain + shift).astype(BF16)
-            g_s[rows, :] = window_tokens(g_ref, wr, wc).astype(BF16)
-    for p in range(3):
-        part = mm(normed_s[...], wqkv_ref[:, p * WIDTH : (p + 1) * WIDTH], NN).astype(BF16)
-        for k in range(3):
-            qkv_s[3 * p + k] = part[:, k * GROUP : (k + 1) * GROUP]
-    part = mm(g_s[...], wproj_ref[...], NT).astype(BF16)
-    for k in range(3):
-        da_s[k] = part[:, k * GROUP : (k + 1) * GROUP]
-
-    for w in range(N_WIN):
-        ids = jnp.broadcast_to(id_ref[w : w + 1, :], (WIN_TOK, WIN_TOK))
-        shut_s[w] = jnp.where(ids.T == ids, 0.0, -1e30)
-    table_s[...] = jnp.zeros_like(table_s)
-    lane = lax.broadcasted_iota(jnp.int32, (WIN_TOK, GROUP), 1) // HEAD_DIM
-
-    def attend(step, carry):
-        w = step // 3
-        k = step % 3
+    edge_refs = (below_ref, right_ref, corner_ref)
+    first = slice(0, WIN_TOK)
+    hat_s[first, :] = hat0_ref[...]
+    inv_s[first, :] = inv0_ref[...]
+    normed_s[first, :] = normed0_ref[...]
+    g_s[first, :] = g0_ref[...]
+    att_s[:, first, :] = att0_ref[...]
+    gqkv_s[:, first, :] = gqkv0_ref[...]
+    table_s[...] = table0_ref[...]
+    for w in range(1, N_WIN):
+        x = window_tokens(0, x_ref, *edge_refs, w // 2, w % 2)
+        g = window_tokens(1, g_ref, *edge_refs, w // 2, w % 2)
+        rows = slice(w * WIN_TOK, (w + 1) * WIN_TOK)
+        normalize(x, g, gain, shift, rows, hat_s, inv_s, normed_s, g_s)
+        shut_s[w] = shut_pairs(id_ref, w)
+    project(slice(WIN_TOK, TOK), normed_s, g_s, wqkv_ref, wproj_ref, qkv_s, da_s)
+
+    def step_of(step, carry):
+        w = (step + 3) // 3
         rows = pl.ds(pl.multiple_of(w * WIN_TOK, WIN_TOK), WIN_TOK)
-        q = qkv_s[k, rows, :]
-        key = qkv_s[3 + k, rows, :]
-        v = qkv_s[6 + k, rows, :]
-        da = da_s[k, rows, :]
-        shut = shut_s[w]
-        zero = jnp.zeros_like(q)
-        heads = []
-        for h in range(4):
-            mine = lane == h
-            heads.append(tuple(jnp.where(mine, a, zero) for a in (q, key, v, da)))
-        probs, grads = [], []
-        q_all, key_all, v_all, da_all = (
-            jnp.concatenate([heads[h][n] for h in range(4)], axis=0) for n in range(4)
-        )
-        score_all = mm(key_all, q, NT)
-        grad_all = mm(v_all, da, NT)
-        for h in range(4):
-            _, key_h, v_h, _ = heads[h]
-            score = score_all[128 * h : 128 * h + 128] * SCALE + bias_ref[4 * k + h] + shut
-            top = jnp.max(score, axis=0, keepdims=True)
-            e = jnp.exp(score - top)
-            prob = e * (1.0 / jnp.sum(e, axis=0, keepdims=True))
-            grad_prob = grad_all[128 * h : 128 * h + 128]
-            inner = jnp.sum(prob * grad_prob, axis=0, keepdims=True)
-            grad_score = prob * (grad_prob - inner)
-            table_s[4 * k + h] += grad_score
-            probs.append(prob.astype(BF16))
-            grads.append((grad_score * SCALE).astype(BF16))
-        prob_rows = jnp.concatenate(probs, axis=0)
-        grad_rows = jnp.concatenate(grads, axis=0)
-        att_s[k, rows, :] = mm(prob_rows, v_all, TN).astype(BF16)
-        gqkv_s[k, rows, :] = mm(grad_rows, key_all, TN).astype(BF16)
-        gqkv_s[3 + k, rows, :] = mm(jnp.concatenate(grads, axis=1), q_all, NN).astype(BF16)
-        gqkv_s[6 + k, rows, :] = mm(jnp.concatenate(probs, axis=1), da_all, NN).astype(BF16)
+        attend(step % 3, rows, shut_s[w], bias_ref, qkv_s, da_s, att_s, gqkv_s, table_s)
         return carry
 
-    lax.fori_loop(0, 12, attend, 0, unroll=6)
+    lax.fori_loop(0, 9, step_of, 0, unroll=3)
 
     attended = jnp.concatenate([att_s[k] for k in range(3)], axis=1)
     store_tile(branch_ref, mm(attended, wproj_ref[...], NN))
@@ -431,25 +489,20 @@
     frame_count, row_count, col_count, _ = frames_in.shape
     token_total = frame_count * row_count * col_count * lax.axis_size(ALL)
     both = (frames_in, grad_out)
-    below, right, corner, x_tile, g_tile = edges(frames_in, grad_out)
+    below, right, corner, x_tile, g_tile, pos_v, table_v, ids = edges(
+        frames_in, grad_out, pos_index, bias_table.T, region_ids
+    )
     below = shifted(below, -1, 0)
     right = shifted(right, 0, -1)
     corner = shifted(corner, -1, -1)
-    rolled = []
-    for n, a in enumerate((x_tile, g_tile)):
-        upper = jnp.concatenate([a[:, 4:, 4:], right[n]], axis=2)
-        lower = jnp.concatenate([below[n], corner[n]], axis=2)
-        tile = jnp.concatenate([upper, lower], axis=1)
-        rolled.append(jnp.concatenate([tile[1:], tile[:1]], axis=0))
-
-    bias, pos_t, gain_v, shift_v, wqkv_v, wproj_v = gather_bias(
-        pos_index, bias_table.T, norm_gain, norm_shift, qkv_weight, proj_weight
-    )
-    ids = region_ids.reshape(2, 2, 8, 2, 8).transpose(1, 3, 0, 2, 4).reshape(N_WIN, WIN_TOK)
+    ids = ids.reshape(2, 2, 8, 2, 8).transpose(1, 3, 0, 2, 4).reshape(N_WIN, WIN_TOK)
+    bias, pos_t, *rest = gather_bias(
+        pos_v, table_v, x_tile, g_tile, ids, norm_gain, norm_shift, qkv_weight, proj_weight
+    )
+    first_window, params = rest[:7], rest[7:]
     me = lax.axis_index("c").reshape(1)
     kept, sent, branch, back = main_call(
-        rolled[0], rolled[1], gain_v, shift_v, wqkv_v, wproj_v, bias,
-        ids, pos_t, me,
+        x_tile, g_tile, below, right, corner, *params, bias, ids, pos_t, *first_window, me,
     )
     part = add_halves(kept, swap_cores(sent))
     plane = ("l", "h", "x")

time: 89.6 us -> 87.4 us (0.975)
  blocking collectives: 17.4 us -> 15 us
  starting transfers between devices: 29.1 us -> 30.2 us
  local copies, waits for them, and re-layouts: 1.43 us -> 0.37 us
    all_to_all x1, blocking collectives: 17.4 us -> 15 us  [exchange(): return lax.all_to_all(parts, axes, 0, 0)]
    pallas_call x1, Pallas kernels: 2.56 us -> 4.57 us  [gather_bias(): pl.pallas_call(bias_kernel, out_shape=(in_vmem((HEADS, WIN_TOK, WIN_TOK),...]
    pallas_call x1, Pallas kernels: 11.3 us -> 10 us  [main_call(): pl.pallas_call(main_kernel, out_shape=(in_vmem((HALF, 128), BF16), in_vme...]
    all_to_all x2, starting transfers between devices: 7.69 us -> 8.8 us  [exchange(): return lax.all_to_all(parts, axes, 0, 0)]
  transfers between devices with their start and end apart: 10 -> 10, of which waited for: 4 -> 4; matrix products, arithmetic and copies ran while one was open for 4% -> 3% of each run, Pallas kernels for 3% -> 5%
where the time goes in v4:
time: 87.4 us; the launch traced here: 87.1 us
  starting transfers between devices  30.2 us (35%)
  Pallas kernels  19.2 us (22%)
  waiting for transfers between devices  19.2 us (22%)
  blocking collectives  15 us (17%)
  other arithmetic  2.29 us (3%)
    ppermute x6, starting transfers between devices, shifted(): return lax.ppermute(value, ALL, pairs)  16.5 us
    all_to_all x1, blocking collectives, exchange(): return lax.all_to_all(parts, axes, 0, 0)  15 us
    pallas_call x1, Pallas kernels, main_call(): pl.pallas_call(main_kernel, out_shape=(in_vmem((HALF, 128), BF16), in_vme...  10 us
    all_to_all x2, starting transfers between devices, exchange(): return lax.all_to_all(parts, axes, 0, 0)  8.8 us
    ppermute x6, waiting for transfers between devices, shifted(): return lax.ppermute(value, ALL, pairs)  7.78 us
    all_to_all x2, waiting for transfers between devices, exchange(): return lax.all_to_all(parts, axes, 0, 0)  7.66 us
    ppermute x2, starting transfers between devices, swap_cores(): return lax.ppermute(value, ALL, [(i, i ^ cols) for i in range(count)])  4.93 us
    pallas_call x1, Pallas kernels, gather_bias(): pl.pallas_call(bias_kernel, out_shape=(in_vmem((HEADS, WIN_TOK, WIN_TOK),...  4.57 us
  transfers between devices with their start and end apart: 10, of which 4 were waited for; matrix products, arithmetic and copies ran while one was open for 3% of the time, Pallas kernels for 5%

profile of v4, /device:TPU:1, one launch (start us, length us, event | category | flops | bytes accessed | tf_op | source)
XLA Modules:
  0.0 87.1 jit_solution(5020675302382976292)
XLA Ops:
  0.6 1.2 %edges.1 = (bf16[2,2,4,12,384]{4,3,2,1,0:T(8,128)(2,1)S(1)}, bf16[2,2,12,4,384]{4,3,2,1,0:T(4,128)(2,1)S(1)}, bf16[2,2,4,4,384]{4,3,2,1,0:T(4,128)(2,1)S(1)}, bf...) custom-call(bf16[2,16,16,384]{3,2,1,0:T(8,128)(2,1)} %x_ref.1, ...), custom_call_target="tpu_custom_call" | custom-call | bytes 1200000 | tf_op jit(solution)/shard_map/edges/pallas_call | solution.py:69
  1.9 6.0 %collective-permute-start.1 = (bf16[2,2,12,4,384]{4,3,2,1,0:T(4,128)(2,1)S(1)}, bf16[2,2,12,4,384]{4,3,2,1,0:T(4,128)(2,1)S(1)}, u32[]{:S(2)}, u32[]{:S(2)}) collective-permute-start(bf16[2,2,12,4,384]{4,3,2,1,0:T(4,128)(2,1)S(1)} %get-tuple-element.50), channel_id=1, source_target_pairs={{0,7},{1,0},{2,1},{3,2},{4,3},{5,4},{6,5},{7,6},{8,15},{9,8},{10,9... | collective-permute-start | bytes 442376 | tf_op jit(solution)/shard_map/ppermute | solution.py:472
  7.9 1.0 %collective-permute-start = (bf16[2,2,4,12,384]{4,3,2,1,0:T(8,128)(2,1)S(1)}, bf16[2,2,4,12,384]{4,3,2,1,0:T(8,128)(2,1)S(1)}, u32[]{:S(2)}, u32[]{:S(2)}) collective-permute-start(bf16[2,2,4,12,384]{4,3,2,1,0:T(8,128)(2,1)S(1)} %get-tuple-element.49), channel_id=1, source_target_pairs={{0,248},{1,249},{2,250},{3,251},{4,252},{5,253},{6,254},{7,255},{8... | collective-permute-start | bytes 442376 | tf_op jit(solution)/shard_map/ppermute | solution.py:472
  8.8 6.2 %collective-permute-start.2 = (bf16[2,2,4,4,384]{4,3,2,1,0:T(4,128)(2,1)S(1)}, bf16[2,2,4,4,384]{4,3,2,1,0:T(4,128)(2,1)S(1)}, u32[]{:S(2)}, u32[]{:S(2)}) collective-permute-start(bf16[2,2,4,4,384]{4,3,2,1,0:T(4,128)(2,1)S(1)} %get-tuple-element.51), channel_id=1, source_target_pairs={{0,255},{1,248},{2,249},{3,250},{4,251},{5,252},{6,253},{7,254},{8... | collective-permute-start | bytes 147464 | tf_op jit(solution)/shard_map/ppermute | solution.py:472
  15.2 4.6 %gather_bias.1 = (f32[12,128,128]{2,1,0:T(8,128)S(1)}, s32[128,128]{1,0:T(8,128)S(1)}, f32[128,384]{1,0:T(8,128)S(1)}, f32[128,128]{1,0:T(8,128)S(1)}, bf16[128,...) custom-call(s32[128,128]{1,0:T(8,128)S(1)} %get-tuple-element.52.pos, ...), custom_call_target="tpu_custom_call" | custom-call | flops 4000000 | bytes 900000 | tf_op jit(solution)/shard_map/gather_bias/pallas_call | solution.py:128
  19.8 10.0 %block_pass.1 = (bf16[2432,128]{1,0:T(8,128)(2,1)S(1)}, bf16[2432,128]{1,0:T(8,128)(2,1)S(1)}, bf16[2,16,16,384]{3,2,1,0:T(8,128)(2,1)S(1)}, bf16[2,16,16,384]{3,2,1,0:T(8,128)(2,1)S(1)}) custom-call(bf16[2,16,16,384]{3,2,1,0:T(8,128)(2,1)S(1)} %get-tuple-element.47.x_ref, bf16[2,16,16,384]{3,2,1,0:T(8,128)(2,1)S(1)} %get-tuple-element.48.g_ref, ...), custom_call_target="tpu_custom_call" | custom-call | flops 4000000000 | bytes 6000000 | tf_op jit(solution)/shard_map/block_pass/pallas_call | solution.py:351
  29.9 2.0 %collective-permute-done.3.b_ref = bf16[2432,128]{1,0:T(8,128)(2,1)S(1)} collective-permute-done((bf16[2432,128]{1,0:T(8,128)(2,1)S(1)}, bf16[2432,128]{1,0:T(8,128)(2,1)S(1)}, u32[]{:S(2)}, u32[]{:S(2)}) %collective-permute-start.3) | collective-permute-done | bytes 622624 | tf_op jit(solution)/shard_map/ppermute | solution.py:482
  32.0 0.1 add_halves.1
  32.1 15.0 %all_to_all.15.parts_ref = bf16[16,152,128]{2,1,0:T(8,128)(2,1)S(1)} all-to-all(bf16[16,152,128]{2,1,0:T(8,128)(2,1)S(1)} %bitcast.36), channel_id=1, replica_groups=mesh['z'=8,'l'=2,'c'=2,'h'=2,'x'=4] {'l','h','x'}, dimensions={0} | all-to-all | bytes 1245184 | tf_op jit(solution)/shard_map/all_to_all | solution.py:476
  47.3 0.8 sum_copies.2
  48.1 5.2 %all-to-all-start.1 = ((bf16[8,152,128]{2,1,0:T(8,128)(2,1)}), bf16[8,152,128]{2,1,0:T(8,128)(2,1)S(1)}, u32[]{:S(2)}, u32[]{:S(2)}) async-start(bf16[8,152,128]{2,1,0:T(8,128)(2,1)} %sum_copies.2), calls=%async_computation.1 | async-start | bytes 622592 | tf_op jit(solution)/shard_map/all_to_all | solution.py:476
  53.3 0.1 pad_maximum_fusion.3
  53.5 0.6 collective-permute-start.5
  54.1 2.4 %collective-permute-start.4 = (bf16[2,2,4,12,384]{4,3,2,1,0:T(8,128)(2,1)S(1)}, bf16[2,2,4,12,384]{4,3,2,1,0:T(8,128)(2,1)S(1)}, u32[]{:S(2)}, u32[]{:S(2)}) collective-permute-start(bf16[2,2,4,12,384]{4,3,2,1,0:T(8,128)(2,1)S(1)} %pad_maximum_fusion.2), channel_id=1, source_target_pairs={{0,8},{1,9},{2,10},{3,11},{4,12},{5,13},{6,14},{7,15},{8,16},{9,17... | collective-permute-start | bytes 442376 | tf_op jit(solution)/shard_map/ppermute | solution.py:472
  56.6 0.4 collective-permute-start.6
  57.0 7.8 %collective-permute-done.6 = bf16[2,2,4,4,384]{4,3,2,1,0:T(4,128)(2,1)S(1)} collective-permute-done((bf16[2,2,4,4,384]{4,3,2,1,0:T(4,128)(2,1)S(1)}, bf16[2,2,4,4,384]{4,3,2,1,0:T(4,128)(2,1)S(1)}, u32[]{:S(2)}, u32[]{:S(2)}) %collective-permute-start.6) | collective-permute-done | bytes 49184 | tf_op jit(solution)/shard_map/ppermute | solution.py:472
  64.9 0.9 %sum_copies.3 = bf16[16,152,128]{2,1,0:T(8,128)(2,1)} custom-call(bf16[8,152,128]{2,1,0:T(8,128)(2,1)S(1)} %all-to-all-done.1.parts_ref), custom_call_target="tpu_custom_call" | custom-call | flops 300000 | bytes 1200000 | tf_op jit(solution)/shard_map/sum_copies/pallas_call | solution.py:448
  65.8 3.6 %all-to-all-start.2 = ((bf16[16,152,128]{2,1,0:T(8,128)(2,1)}), bf16[16,152,128]{2,1,0:T(8,128)(2,1)S(1)}, u32[]{:S(2)}, u32[]{:S(2)}) async-start(bf16[16,152,128]{2,1,0:T(8,128)(2,1)} %sum_copies.3), calls=%async_computation.2 | async-start | bytes 1245184 | tf_op jit(solution)/shard_map/all_to_all | solution.py:476
  69.5 1.0 %add_convert_fusion.1 = bf16[2,16,16,384]{3,2,1,0:T(8,128)(2,1)} fusion(bf16[2,16,16,384]{3,2,1,0:T(8,128)(2,1)S(1)} %copy-done, bf16[1,16,16,384]{3,2,1,0:T(8,128)(2,1)S(1)} %get-tuple-element.87, bf16[1,16,16,384]{3,2,1,0:T(8,128)(2,1)S(1)} %get-tuple-element.88, bf16[2,12,4,384]{3,2,1,0:T(4,128)(2,1)S(1)} %get-tuple-element.94, ...), kind=kLoop, calls=%fused_computation.1 | loop fusion | flops 2555904 | bytes 1351680 | tf_op jit(solution)/shard_map/convert_element_type | solution.py:522
  70.4 0.9 %add_convert_fusion = bf16[2,16,16,384]{3,2,1,0:T(8,128)(2,1)} fusion(bf16[2,16,16,384]{3,2,1,0:T(8,128)(2,1)S(1)} %copy-done.1, bf16[1,16,16,384]{3,2,1,0:T(8,128)(2,1)S(1)} %get-tuple-element.98, bf16[1,16,16,384]{3,2,1,0:T(8,128)(2,1)S(1)} %get-tuple-element.97, bf16[2,12,4,384]{3,2,1,0:T(4,128)(2,1)S(1)} %get-tuple-element.93, ...), kind=kLoop, calls=%fused_computation | loop fusion | flops 2555904 | bytes 1351680 | tf_op jit(solution)/shard_map/convert_element_type | solution.py:522
  71.4 7.7 %all-to-all-done.2 = bf16[16,152,128]{2,1,0:T(8,128)(2,1)S(1)} async-done(((bf16[16,152,128]{2,1,0:T(8,128)(2,1)}), bf16[16,152,128]{2,1,0:T(8,128)(2,1)S(1)}, u32[]{:S(2)}, u32[]{:S(2)}) %all-to-all-start.2) | async-done | bytes 622624 | tf_op jit(solution)/shard_map/all_to_all | solution.py:476
  79.0 4.8 %collective-permute-start.7 = (bf16[2432,128]{1,0:T(8,128)(2,1)S(1)}, bf16[2432,128]{1,0:T(8,128)(2,1)S(1)}, u32[]{:S(2)}, u32[]{:S(2)}) collective-permute-start(bf16[2432,128]{1,0:T(8,128)(2,1)S(1)} %bitcast.34), channel_id=1, source_target_pairs={{0,8},{1,9},{2,10},{3,11},{4,12},{5,13},{6,14},{7,15},{8,0},{9,1},... | collective-permute-start | bytes 1867784 | tf_op jit(solution)/shard_map/ppermute | solution.py:482
  83.9 1.7 %collective-permute-done.7.other_ref = bf16[2432,128]{1,0:T(8,128)(2,1)S(1)} collective-permute-done((bf16[2432,128]{1,0:T(8,128)(2,1)S(1)}, bf16[2432,128]{1,0:T(8,128)(2,1)S(1)}, u32[]{:S(2)}, u32[]{:S(2)}) %collective-permute-start.7) | collective-permute-done | bytes 622624 | tf_op jit(solution)/shard_map/ppermute | solution.py:482
  85.5 1.5 %unpack_sums.1 = (f32[384,1152]{1,0:T(8,128)}, f32[384,384]{1,0:T(8,128)}, f32[12,675]{1,0:T(8,128)}, f32[384]{0:T(512)}, f32[384]{0:T(512)}) custom-call(s32[1]{0:T(128)} %bitcast.2.me_ref, bf16[2432,128]{1,0:T(8,128)(2,1)S(1)} %bitcast.35, bf16[2432,128]{1,0:T(8,128)(2,1)S(1)} %collective-permute-done.7.other_ref), custom_call_target="tpu_custom_call" | custom-call | flops 600000 | bytes 3600000 | tf_op jit(solution)/shard_map/unpack_sums/pallas_call | solution.py:404
  (26 shorter events, 0.8 us)
Async XLA Ops:
  1.9 17.9 %collective-permute-start.1 = (bf16[2,2,12,4,384]{4,3,2,1,0:T(4,128)(2,1)S(1)}, bf16[2,2,12,4,384]{4,3,2,1,0:T(4,128)(2,1)S(1)}, u32[]{:S(2)}, u32[]{:S(2)}) collective-permute-start(bf16[2,2,12,4,384]{4,3,2,1,0:T(4,128)(2,1)S(1)} %get-tuple-element.50), channel_id=1, source_target_pairs={{0,7},{1,0},{2,1},{3,2},{4,3},{5,4},{6,5},{7,6},{8,15},{9,8},{10,9... | collective-permute-start | bytes 442376 | tf_op jit(solution)/shard_map/ppermute | solution.py:472
  7.9 11.9 %collective-permute-start = (bf16[2,2,4,12,384]{4,3,2,1,0:T(8,128)(2,1)S(1)}, bf16[2,2,4,12,384]{4,3,2,1,0:T(8,128)(2,1)S(1)}, u32[]{:S(2)}, u32[]{:S(2)}) collective-permute-start(bf16[2,2,4,12,384]{4,3,2,1,0:T(8,128)(2,1)S(1)} %get-tuple-element.49), channel_id=1, source_target_pairs={{0,248},{1,249},{2,250},{3,251},{4,252},{5,253},{6,254},{7,255},{8... | collective-permute-start | bytes 442376 | tf_op jit(solution)/shard_map/ppermute | solution.py:472
  8.8 10.9 %collective-permute-start.2 = (bf16[2,2,4,4,384]{4,3,2,1,0:T(4,128)(2,1)S(1)}, bf16[2,2,4,4,384]{4,3,2,1,0:T(4,128)(2,1)S(1)}, u32[]{:S(2)}, u32[]{:S(2)}) collective-permute-start(bf16[2,2,4,4,384]{4,3,2,1,0:T(4,128)(2,1)S(1)} %get-tuple-element.51), channel_id=1, source_target_pairs={{0,255},{1,248},{2,249},{3,250},{4,251},{5,252},{6,253},{7,254},{8... | collective-permute-start | bytes 147464 | tf_op jit(solution)/shard_map/ppermute | solution.py:472
  29.8 2.1 %collective-permute-start.3 = (bf16[2432,128]{1,0:T(8,128)(2,1)S(1)}, bf16[2432,128]{1,0:T(8,128)(2,1)S(1)}, u32[]{:S(2)}, u32[]{:S(2)}) collective-permute-start(bf16[2432,128]{1,0:T(8,128)(2,1)S(1)} %get-tuple-element.69), channel_id=1, source_target_pairs={{0,8},{1,9},{2,10},{3,11},{4,12},{5,13},{6,14},{7,15},{8,0},{9,1},... | collective-permute-start | bytes 1867784 | tf_op jit(solution)/shard_map/ppermute | solution.py:482
  48.1 16.7 %all-to-all-start.1 = ((bf16[8,152,128]{2,1,0:T(8,128)(2,1)}), bf16[8,152,128]{2,1,0:T(8,128)(2,1)S(1)}, u32[]{:S(2)}, u32[]{:S(2)}) async-start(bf16[8,152,128]{2,1,0:T(8,128)(2,1)} %sum_copies.2), calls=%async_computation.1 | async-start | bytes 622592 | tf_op jit(solution)/shard_map/all_to_all | solution.py:476
  53.5 11.3 %collective-permute-start.5 = (bf16[2,2,12,4,384]{4,3,2,1,0:T(4,128)(2,1)S(1)}, bf16[2,2,12,4,384]{4,3,2,1,0:T(4,128)(2,1)S(1)}, u32[]{:S(2)}, u32[]{:S(2)}) collective-permute-start(bf16[2,2,12,4,384]{4,3,2,1,0:T(4,128)(2,1)S(1)} %pad_maximum_fusion.3), channel_id=1, source_target_pairs={{0,1},{1,2},{2,3},{3,4},{4,5},{5,6},{6,7},{7,0},{8,9},{9,10},{10,1... | collective-permute-start | bytes 442376 | tf_op jit(solution)/shard_map/ppermute | solution.py:472
  54.1 10.6 %collective-permute-start.4 = (bf16[2,2,4,12,384]{4,3,2,1,0:T(8,128)(2,1)S(1)}, bf16[2,2,4,12,384]{4,3,2,1,0:T(8,128)(2,1)S(1)}, u32[]{:S(2)}, u32[]{:S(2)}) collective-permute-start(bf16[2,2,4,12,384]{4,3,2,1,0:T(8,128)(2,1)S(1)} %pad_maximum_fusion.2), channel_id=1, source_target_pairs={{0,8},{1,9},{2,10},{3,11},{4,12},{5,13},{6,14},{7,15},{8,16},{9,17... | collective-permute-start | bytes 442376 | tf_op jit(solution)/shard_map/ppermute | solution.py:472
  56.6 12.9 %copy-start = (bf16[2,16,16,384]{3,2,1,0:T(8,128)(2,1)S(1)}, bf16[2,16,16,384]{3,2,1,0:T(8,128)(2,1)}, u32[]{:S(2)}) copy-start(bf16[2,16,16,384]{3,2,1,0:T(8,128)(2,1)} %x_ref.1) | copy-start | bytes 1179652
  56.6 8.1 %collective-permute-start.6 = (bf16[2,2,4,4,384]{4,3,2,1,0:T(4,128)(2,1)S(1)}, bf16[2,2,4,4,384]{4,3,2,1,0:T(4,128)(2,1)S(1)}, u32[]{:S(2)}, u32[]{:S(2)}) collective-permute-start(bf16[2,2,4,4,384]{4,3,2,1,0:T(4,128)(2,1)S(1)} %pad_maximum_fusion.4), channel_id=1, source_target_pairs={{0,9},{1,10},{2,11},{3,12},{4,13},{5,14},{6,15},{7,8},{8,17},{9,18... | collective-permute-start | bytes 147464 | tf_op jit(solution)/shard_map/ppermute | solution.py:472
  64.9 5.6 %copy-start.1 = (bf16[2,16,16,384]{3,2,1,0:T(8,128)(2,1)S(1)}, bf16[2,16,16,384]{3,2,1,0:T(8,128)(2,1)}, u32[]{:S(2)}) copy-start(bf16[2,16,16,384]{3,2,1,0:T(8,128)(2,1)} %g_ref.1) | copy-start | bytes 1179652
  65.8 13.3 %all-to-all-start.2 = ((bf16[16,152,128]{2,1,0:T(8,128)(2,1)}), bf16[16,152,128]{2,1,0:T(8,128)(2,1)S(1)}, u32[]{:S(2)}, u32[]{:S(2)}) async-start(bf16[16,152,128]{2,1,0:T(8,128)(2,1)} %sum_copies.3), calls=%async_computation.2 | async-start | bytes 1245184 | tf_op jit(solution)/shard_map/all_to_all | solution.py:476
  79.0 6.5 %collective-permute-start.7 = (bf16[2432,128]{1,0:T(8,128)(2,1)S(1)}, bf16[2432,128]{1,0:T(8,128)(2,1)S(1)}, u32[]{:S(2)}, u32[]{:S(2)}) collective-permute-start(bf16[2432,128]{1,0:T(8,128)(2,1)S(1)} %bitcast.34), channel_id=1, source_target_pairs={{0,8},{1,9},{2,10},{3,11},{4,12},{5,13},{6,14},{7,15},{8,0},{9,1},... | collective-permute-start | bytes 1867784 | tf_op jit(solution)/shard_map/ppermute | solution.py:482

commit v5 on v4

--- a/solution.py
+++ b/solution.py
@@ -110,7 +110,7 @@
             bias_ref[h, pl.ds(at, 8), :] = got
         return carry
 
-    lax.fori_loop(0, 16, rows, 0)
+    lax.fori_loop(0, 16, rows, 0, unroll=2)
     for copy in copies:
         copy.wait()
     sums_ref[...] = jnp.zeros_like(sums_ref)
@@ -281,7 +281,7 @@
         attend(step % 3, rows, shut_s[w], bias_ref, qkv_s, da_s, att_s, gqkv_s, table_s)
         return carry
 
-    lax.fori_loop(0, 9, step_of, 0, unroll=3)
+    lax.fori_loop(0, 9, step_of, 0, unroll=9)
 
     attended = jnp.concatenate([att_s[k] for k in range(3)], axis=1)
     store_tile(branch_ref, mm(attended, wproj_ref[...], NN))
@@ -336,7 +336,7 @@
             )
         return acc
 
-    table = lax.fori_loop(0, WIN_TOK // 8, bins, jnp.zeros((96, 128), F32), unroll=4)
+    table = lax.fori_loop(0, WIN_TOK // 8, bins, jnp.zeros((96, 128), F32), unroll=8)
     pack_ref[ROW_TABLE : ROW_TABLE + 96, :] = table.astype(BF16)
     norm_rows = [a[:, k * 128 : (k + 1) * 128] for a in (grad_gain, grad_shift) for k in range(3)]
     norm_rows.append(jnp.zeros((10, 128), F32))

time: 87.4 us -> 86.5 us (0.990)
  Pallas kernels: 19.2 us -> 17.6 us
    pallas_call x1, Pallas kernels: 10 us -> 9.05 us  [main_call(): pl.pallas_call(main_kernel, out_shape=(in_vmem((HALF, 128), BF16), in_vme...]
where the time goes in v5:
time: 86.5 us; the launch traced here: 86.2 us
  starting transfers between devices  30.3 us (35%)
  waiting for transfers between devices  19.1 us (22%)
  Pallas kernels  17.6 us (20%)
  blocking collectives  15.6 us (18%)
  other arithmetic  2.29 us (3%)
    ppermute x6, starting transfers between devices, shifted(): return lax.ppermute(value, ALL, pairs)  16.6 us
    all_to_all x1, blocking collectives, exchange(): return lax.all_to_all(parts, axes, 0, 0)  15.6 us
    pallas_call x1, Pallas kernels, main_call(): pl.pallas_call(main_kernel, out_shape=(in_vmem((HALF, 128), BF16), in_vme...  9.05 us
    all_to_all x2, starting transfers between devices, exchange(): return lax.all_to_all(parts, axes, 0, 0)  8.79 us
    ppermute x6, waiting for transfers between devices, shifted(): return lax.ppermute(value, ALL, pairs)  7.74 us
    all_to_all x2, waiting for transfers between devices, exchange(): return lax.all_to_all(parts, axes, 0, 0)  7.66 us
    ppermute x2, starting transfers between devices, swap_cores(): return lax.ppermute(value, ALL, [(i, i ^ cols) for i in range(count)])  4.97 us
    pallas_call x1, Pallas kernels, gather_bias(): pl.pallas_call(bias_kernel, out_shape=(in_vmem((HEADS, WIN_TOK, WIN_TOK),...  3.97 us
  transfers between devices with their start and end apart: 10, of which 4 were waited for; matrix products, arithmetic and copies ran while one was open for 3% of the time, Pallas kernels for 5%

profile of v5, /device:TPU:1, one launch (start us, length us, event | category | flops | bytes accessed | tf_op | source)
XLA Modules:
  0.0 86.2 jit_solution(6928344134222154476)
XLA Ops:
  0.6 1.2 %edges.1 = (bf16[2,2,4,12,384]{4,3,2,1,0:T(8,128)(2,1)S(1)}, bf16[2,2,12,4,384]{4,3,2,1,0:T(4,128)(2,1)S(1)}, bf16[2,2,4,4,384]{4,3,2,1,0:T(4,128)(2,1)S(1)}, bf...) custom-call(bf16[2,16,16,384]{3,2,1,0:T(8,128)(2,1)} %x_ref.1, ...), custom_call_target="tpu_custom_call" | custom-call | bytes 1200000 | tf_op jit(solution)/shard_map/edges/pallas_call | solution.py:69
  1.9 6.0 %collective-permute-start.1 = (bf16[2,2,12,4,384]{4,3,2,1,0:T(4,128)(2,1)S(1)}, bf16[2,2,12,4,384]{4,3,2,1,0:T(4,128)(2,1)S(1)}, u32[]{:S(2)}, u32[]{:S(2)}) collective-permute-start(bf16[2,2,12,4,384]{4,3,2,1,0:T(4,128)(2,1)S(1)} %get-tuple-element.50), channel_id=1, source_target_pairs={{0,7},{1,0},{2,1},{3,2},{4,3},{5,4},{6,5},{7,6},{8,15},{9,8},{10,9... | collective-permute-start | bytes 442376 | tf_op jit(solution)/shard_map/ppermute | solution.py:472
  7.9 1.0 %collective-permute-start = (bf16[2,2,4,12,384]{4,3,2,1,0:T(8,128)(2,1)S(1)}, bf16[2,2,4,12,384]{4,3,2,1,0:T(8,128)(2,1)S(1)}, u32[]{:S(2)}, u32[]{:S(2)}) collective-permute-start(bf16[2,2,4,12,384]{4,3,2,1,0:T(8,128)(2,1)S(1)} %get-tuple-element.49), channel_id=1, source_target_pairs={{0,248},{1,249},{2,250},{3,251},{4,252},{5,253},{6,254},{7,255},{8... | collective-permute-start | bytes 442376 | tf_op jit(solution)/shard_map/ppermute | solution.py:472
  8.8 6.2 %collective-permute-start.2 = (bf16[2,2,4,4,384]{4,3,2,1,0:T(4,128)(2,1)S(1)}, bf16[2,2,4,4,384]{4,3,2,1,0:T(4,128)(2,1)S(1)}, u32[]{:S(2)}, u32[]{:S(2)}) collective-permute-start(bf16[2,2,4,4,384]{4,3,2,1,0:T(4,128)(2,1)S(1)} %get-tuple-element.51), channel_id=1, source_target_pairs={{0,255},{1,248},{2,249},{3,250},{4,251},{5,252},{6,253},{7,254},{8... | collective-permute-start | bytes 147464 | tf_op jit(solution)/shard_map/ppermute | solution.py:472
  15.2 4.0 %gather_bias.1 = (f32[12,128,128]{2,1,0:T(8,128)S(1)}, s32[128,128]{1,0:T(8,128)S(1)}, f32[128,384]{1,0:T(8,128)S(1)}, f32[128,128]{1,0:T(8,128)S(1)}, bf16[128,...) custom-call(s32[128,128]{1,0:T(8,128)S(1)} %get-tuple-element.52.pos, ...), custom_call_target="tpu_custom_call" | custom-call | flops 4000000 | bytes 900000 | tf_op jit(solution)/shard_map/gather_bias/pallas_call | solution.py:128
  19.2 9.1 %block_pass.1 = (bf16[2432,128]{1,0:T(8,128)(2,1)S(1)}, bf16[2432,128]{1,0:T(8,128)(2,1)S(1)}, bf16[2,16,16,384]{3,2,1,0:T(8,128)(2,1)S(1)}, bf16[2,16,16,384]{3,2,1,0:T(8,128)(2,1)S(1)}) custom-call(bf16[2,16,16,384]{3,2,1,0:T(8,128)(2,1)S(1)} %get-tuple-element.47.x_ref, bf16[2,16,16,384]{3,2,1,0:T(8,128)(2,1)S(1)} %get-tuple-element.48.g_ref, ...), custom_call_target="tpu_custom_call" | custom-call | flops 4000000000 | bytes 6000000 | tf_op jit(solution)/shard_map/block_pass/pallas_call | solution.py:351
  28.4 2.0 %collective-permute-done.3.b_ref = bf16[2432,128]{1,0:T(8,128)(2,1)S(1)} collective-permute-done((bf16[2432,128]{1,0:T(8,128)(2,1)S(1)}, bf16[2432,128]{1,0:T(8,128)(2,1)S(1)}, u32[]{:S(2)}, u32[]{:S(2)}) %collective-permute-start.3) | collective-permute-done | bytes 622624 | tf_op jit(solution)/shard_map/ppermute | solution.py:482
  30.4 0.1 add_halves.1
  30.6 15.6 %all_to_all.15.parts_ref = bf16[16,152,128]{2,1,0:T(8,128)(2,1)S(1)} all-to-all(bf16[16,152,128]{2,1,0:T(8,128)(2,1)S(1)} %bitcast.36), channel_id=1, replica_groups=mesh['z'=8,'l'=2,'c'=2,'h'=2,'x'=4] {'l','h','x'}, dimensions={0} | all-to-all | bytes 1245184 | tf_op jit(solution)/shard_map/all_to_all | solution.py:476
  46.3 0.8 sum_copies.2
  47.1 5.1 %all-to-all-start.1 = ((bf16[8,152,128]{2,1,0:T(8,128)(2,1)}), bf16[8,152,128]{2,1,0:T(8,128)(2,1)S(1)}, u32[]{:S(2)}, u32[]{:S(2)}) async-start(bf16[8,152,128]{2,1,0:T(8,128)(2,1)} %sum_copies.2), calls=%async_computation.1 | async-start | bytes 622592 | tf_op jit(solution)/shard_map/all_to_all | solution.py:476
  52.3 0.1 pad_maximum_fusion.3
  52.5 0.6 collective-permute-start.5
  53.2 2.4 %collective-permute-start.4 = (bf16[2,2,4,12,384]{4,3,2,1,0:T(8,128)(2,1)S(1)}, bf16[2,2,4,12,384]{4,3,2,1,0:T(8,128)(2,1)S(1)}, u32[]{:S(2)}, u32[]{:S(2)}) collective-permute-start(bf16[2,2,4,12,384]{4,3,2,1,0:T(8,128)(2,1)S(1)} %pad_maximum_fusion.2), channel_id=1, source_target_pairs={{0,8},{1,9},{2,10},{3,11},{4,12},{5,13},{6,14},{7,15},{8,16},{9,17... | collective-permute-start | bytes 442376 | tf_op jit(solution)/shard_map/ppermute | solution.py:472
  55.7 0.4 collective-permute-start.6
  56.1 7.7 %collective-permute-done.6 = bf16[2,2,4,4,384]{4,3,2,1,0:T(4,128)(2,1)S(1)} collective-permute-done((bf16[2,2,4,4,384]{4,3,2,1,0:T(4,128)(2,1)S(1)}, bf16[2,2,4,4,384]{4,3,2,1,0:T(4,128)(2,1)S(1)}, u32[]{:S(2)}, u32[]{:S(2)}) %collective-permute-start.6) | collective-permute-done | bytes 49184 | tf_op jit(solution)/shard_map/ppermute | solution.py:472
  63.9 0.9 %sum_copies.3 = bf16[16,152,128]{2,1,0:T(8,128)(2,1)} custom-call(bf16[8,152,128]{2,1,0:T(8,128)(2,1)S(1)} %all-to-all-done.1.parts_ref), custom_call_target="tpu_custom_call" | custom-call | flops 300000 | bytes 1200000 | tf_op jit(solution)/shard_map/sum_copies/pallas_call | solution.py:448
  64.8 3.6 %all-to-all-start.2 = ((bf16[16,152,128]{2,1,0:T(8,128)(2,1)}), bf16[16,152,128]{2,1,0:T(8,128)(2,1)S(1)}, u32[]{:S(2)}, u32[]{:S(2)}) async-start(bf16[16,152,128]{2,1,0:T(8,128)(2,1)} %sum_copies.3), calls=%async_computation.2 | async-start | bytes 1245184 | tf_op jit(solution)/shard_map/all_to_all | solution.py:476
  68.5 1.0 %add_convert_fusion.1 = bf16[2,16,16,384]{3,2,1,0:T(8,128)(2,1)} fusion(bf16[2,16,16,384]{3,2,1,0:T(8,128)(2,1)S(1)} %copy-done, bf16[1,16,16,384]{3,2,1,0:T(8,128)(2,1)S(1)} %get-tuple-element.87, bf16[1,16,16,384]{3,2,1,0:T(8,128)(2,1)S(1)} %get-tuple-element.88, bf16[2,12,4,384]{3,2,1,0:T(4,128)(2,1)S(1)} %get-tuple-element.94, ...), kind=kLoop, calls=%fused_computation.1 | loop fusion | flops 2555904 | bytes 1351680 | tf_op jit(solution)/shard_map/convert_element_type | solution.py:522
  69.4 0.9 %add_convert_fusion = bf16[2,16,16,384]{3,2,1,0:T(8,128)(2,1)} fusion(bf16[2,16,16,384]{3,2,1,0:T(8,128)(2,1)S(1)} %copy-done.1, bf16[1,16,16,384]{3,2,1,0:T(8,128)(2,1)S(1)} %get-tuple-element.98, bf16[1,16,16,384]{3,2,1,0:T(8,128)(2,1)S(1)} %get-tuple-element.97, bf16[2,12,4,384]{3,2,1,0:T(4,128)(2,1)S(1)} %get-tuple-element.93, ...), kind=kLoop, calls=%fused_computation | loop fusion | flops 2555904 | bytes 1351680 | tf_op jit(solution)/shard_map/convert_element_type | solution.py:522
  70.4 7.7 %all-to-all-done.2 = bf16[16,152,128]{2,1,0:T(8,128)(2,1)S(1)} async-done(((bf16[16,152,128]{2,1,0:T(8,128)(2,1)}), bf16[16,152,128]{2,1,0:T(8,128)(2,1)S(1)}, u32[]{:S(2)}, u32[]{:S(2)}) %all-to-all-start.2) | async-done | bytes 622624 | tf_op jit(solution)/shard_map/all_to_all | solution.py:476
  78.0 4.9 %collective-permute-start.7 = (bf16[2432,128]{1,0:T(8,128)(2,1)S(1)}, bf16[2432,128]{1,0:T(8,128)(2,1)S(1)}, u32[]{:S(2)}, u32[]{:S(2)}) collective-permute-start(bf16[2432,128]{1,0:T(8,128)(2,1)S(1)} %bitcast.34), channel_id=1, source_target_pairs={{0,8},{1,9},{2,10},{3,11},{4,12},{5,13},{6,14},{7,15},{8,0},{9,1},... | collective-permute-start | bytes 1867784 | tf_op jit(solution)/shard_map/ppermute | solution.py:482
  82.9 1.7 %collective-permute-done.7.other_ref = bf16[2432,128]{1,0:T(8,128)(2,1)S(1)} collective-permute-done((bf16[2432,128]{1,0:T(8,128)(2,1)S(1)}, bf16[2432,128]{1,0:T(8,128)(2,1)S(1)}, u32[]{:S(2)}, u32[]{:S(2)}) %collective-permute-start.7) | collective-permute-done | bytes 622624 | tf_op jit(solution)/shard_map/ppermute | solution.py:482
  84.6 1.5 %unpack_sums.1 = (f32[384,1152]{1,0:T(8,128)}, f32[384,384]{1,0:T(8,128)}, f32[12,675]{1,0:T(8,128)}, f32[384]{0:T(512)}, f32[384]{0:T(512)}) custom-call(s32[1]{0:T(128)} %bitcast.2.me_ref, bf16[2432,128]{1,0:T(8,128)(2,1)S(1)} %bitcast.35, bf16[2432,128]{1,0:T(8,128)(2,1)S(1)} %collective-permute-done.7.other_ref), custom_call_target="tpu_custom_call" | custom-call | flops 600000 | bytes 3600000 | tf_op jit(solution)/shard_map/unpack_sums/pallas_call | solution.py:404
  (26 shorter events, 0.8 us)
Async XLA Ops:
  1.9 17.3 %collective-permute-start.1 = (bf16[2,2,12,4,384]{4,3,2,1,0:T(4,128)(2,1)S(1)}, bf16[2,2,12,4,384]{4,3,2,1,0:T(4,128)(2,1)S(1)}, u32[]{:S(2)}, u32[]{:S(2)}) collective-permute-start(bf16[2,2,12,4,384]{4,3,2,1,0:T(4,128)(2,1)S(1)} %get-tuple-element.50), channel_id=1, source_target_pairs={{0,7},{1,0},{2,1},{3,2},{4,3},{5,4},{6,5},{7,6},{8,15},{9,8},{10,9... | collective-permute-start | bytes 442376 | tf_op jit(solution)/shard_map/ppermute | solution.py:472
  7.9 11.3 %collective-permute-start = (bf16[2,2,4,12,384]{4,3,2,1,0:T(8,128)(2,1)S(1)}, bf16[2,2,4,12,384]{4,3,2,1,0:T(8,128)(2,1)S(1)}, u32[]{:S(2)}, u32[]{:S(2)}) collective-permute-start(bf16[2,2,4,12,384]{4,3,2,1,0:T(8,128)(2,1)S(1)} %get-tuple-element.49), channel_id=1, source_target_pairs={{0,248},{1,249},{2,250},{3,251},{4,252},{5,253},{6,254},{7,255},{8... | collective-permute-start | bytes 442376 | tf_op jit(solution)/shard_map/ppermute | solution.py:472
  8.8 10.3 %collective-permute-start.2 = (bf16[2,2,4,4,384]{4,3,2,1,0:T(4,128)(2,1)S(1)}, bf16[2,2,4,4,384]{4,3,2,1,0:T(4,128)(2,1)S(1)}, u32[]{:S(2)}, u32[]{:S(2)}) collective-permute-start(bf16[2,2,4,4,384]{4,3,2,1,0:T(4,128)(2,1)S(1)} %get-tuple-element.51), channel_id=1, source_target_pairs={{0,255},{1,248},{2,249},{3,250},{4,251},{5,252},{6,253},{7,254},{8... | collective-permute-start | bytes 147464 | tf_op jit(solution)/shard_map/ppermute | solution.py:472
  28.3 2.1 %collective-permute-start.3 = (bf16[2432,128]{1,0:T(8,128)(2,1)S(1)}, bf16[2432,128]{1,0:T(8,128)(2,1)S(1)}, u32[]{:S(2)}, u32[]{:S(2)}) collective-permute-start(bf16[2432,128]{1,0:T(8,128)(2,1)S(1)} %get-tuple-element.69), channel_id=1, source_target_pairs={{0,8},{1,9},{2,10},{3,11},{4,12},{5,13},{6,14},{7,15},{8,0},{9,1},... | collective-permute-start | bytes 1867784 | tf_op jit(solution)/shard_map/ppermute | solution.py:482
  47.1 16.7 %all-to-all-start.1 = ((bf16[8,152,128]{2,1,0:T(8,128)(2,1)}), bf16[8,152,128]{2,1,0:T(8,128)(2,1)S(1)}, u32[]{:S(2)}, u32[]{:S(2)}) async-start(bf16[8,152,128]{2,1,0:T(8,128)(2,1)} %sum_copies.2), calls=%async_computation.1 | async-start | bytes 622592 | tf_op jit(solution)/shard_map/all_to_all | solution.py:476
  52.5 11.3 %collective-permute-start.5 = (bf16[2,2,12,4,384]{4,3,2,1,0:T(4,128)(2,1)S(1)}, bf16[2,2,12,4,384]{4,3,2,1,0:T(4,128)(2,1)S(1)}, u32[]{:S(2)}, u32[]{:S(2)}) collective-permute-start(bf16[2,2,12,4,384]{4,3,2,1,0:T(4,128)(2,1)S(1)} %pad_maximum_fusion.3), channel_id=1, source_target_pairs={{0,1},{1,2},{2,3},{3,4},{4,5},{5,6},{6,7},{7,0},{8,9},{9,10},{10,1... | collective-permute-start | bytes 442376 | tf_op jit(solution)/shard_map/ppermute | solution.py:472
  53.2 10.6 %collective-permute-start.4 = (bf16[2,2,4,12,384]{4,3,2,1,0:T(8,128)(2,1)S(1)}, bf16[2,2,4,12,384]{4,3,2,1,0:T(8,128)(2,1)S(1)}, u32[]{:S(2)}, u32[]{:S(2)}) collective-permute-start(bf16[2,2,4,12,384]{4,3,2,1,0:T(8,128)(2,1)S(1)} %pad_maximum_fusion.2), channel_id=1, source_target_pairs={{0,8},{1,9},{2,10},{3,11},{4,12},{5,13},{6,14},{7,15},{8,16},{9,17... | collective-permute-start | bytes 442376 | tf_op jit(solution)/shard_map/ppermute | solution.py:472
  55.6 12.9 %copy-start = (bf16[2,16,16,384]{3,2,1,0:T(8,128)(2,1)S(1)}, bf16[2,16,16,384]{3,2,1,0:T(8,128)(2,1)}, u32[]{:S(2)}) copy-start(bf16[2,16,16,384]{3,2,1,0:T(8,128)(2,1)} %x_ref.1) | copy-start | bytes 1179652
  55.7 8.1 %collective-permute-start.6 = (bf16[2,2,4,4,384]{4,3,2,1,0:T(4,128)(2,1)S(1)}, bf16[2,2,4,4,384]{4,3,2,1,0:T(4,128)(2,1)S(1)}, u32[]{:S(2)}, u32[]{:S(2)}) collective-permute-start(bf16[2,2,4,4,384]{4,3,2,1,0:T(4,128)(2,1)S(1)} %pad_maximum_fusion.4), channel_id=1, source_target_pairs={{0,9},{1,10},{2,11},{3,12},{4,13},{5,14},{6,15},{7,8},{8,17},{9,18... | collective-permute-start | bytes 147464 | tf_op jit(solution)/shard_map/ppermute | solution.py:472
  63.9 5.6 %copy-start.1 = (bf16[2,16,16,384]{3,2,1,0:T(8,128)(2,1)S(1)}, bf16[2,16,16,384]{3,2,1,0:T(8,128)(2,1)}, u32[]{:S(2)}) copy-start(bf16[2,16,16,384]{3,2,1,0:T(8,128)(2,1)} %g_ref.1) | copy-start | bytes 1179652
  64.8 13.3 %all-to-all-start.2 = ((bf16[16,152,128]{2,1,0:T(8,128)(2,1)}), bf16[16,152,128]{2,1,0:T(8,128)(2,1)S(1)}, u32[]{:S(2)}, u32[]{:S(2)}) async-start(bf16[16,152,128]{2,1,0:T(8,128)(2,1)} %sum_copies.3), calls=%async_computation.2 | async-start | bytes 1245184 | tf_op jit(solution)/shard_map/all_to_all | solution.py:476
  78.0 6.6 %collective-permute-start.7 = (bf16[2432,128]{1,0:T(8,128)(2,1)S(1)}, bf16[2432,128]{1,0:T(8,128)(2,1)S(1)}, u32[]{:S(2)}, u32[]{:S(2)}) collective-permute-start(bf16[2432,128]{1,0:T(8,128)(2,1)S(1)} %bitcast.34), channel_id=1, source_target_pairs={{0,8},{1,9},{2,10},{3,11},{4,12},{5,13},{6,14},{7,15},{8,0},{9,1},... | collective-permute-start | bytes 1867784 | tf_op jit(solution)/shard_map/ppermute | solution.py:482

commit v6 on v5

--- a/solution.py
+++ b/solution.py
@@ -110,7 +110,7 @@
             bias_ref[h, pl.ds(at, 8), :] = got
         return carry
 
-    lax.fori_loop(0, 16, rows, 0, unroll=2)
+    lax.fori_loop(0, 16, rows, 0, unroll=4)
     for copy in copies:
         copy.wait()
     sums_ref[...] = jnp.zeros_like(sums_ref)
@@ -336,7 +336,7 @@
             )
         return acc
 
-    table = lax.fori_loop(0, WIN_TOK // 8, bins, jnp.zeros((96, 128), F32), unroll=8)
+    table = lax.fori_loop(0, WIN_TOK // 8, bins, jnp.zeros((96, 128), F32), unroll=16)
     pack_ref[ROW_TABLE : ROW_TABLE + 96, :] = table.astype(BF16)
     norm_rows = [a[:, k * 128 : (k + 1) * 128] for a in (grad_gain, grad_shift) for k in range(3)]
     norm_rows.append(jnp.zeros((10, 128), F32))

time: 86.5 us -> 86.3 us (level)
  transfers between devices with their start and end apart: 10 -> 10, of which waited for: 4 -> 4; matrix products, arithmetic and copies ran while one was open for 3% -> 3% of each run, Pallas kernels for 5% -> 4%
where the time goes in v6:
time: 86.3 us; the launch traced here: 86 us
  starting transfers between devices  30.1 us (35%)
  waiting for transfers between devices  19.3 us (22%)
  Pallas kernels  17.2 us (20%)
  blocking collectives  15.9 us (18%)
  other arithmetic  2.29 us (3%)
    ppermute x6, starting transfers between devices, shifted(): return lax.ppermute(value, ALL, pairs)  16.6 us
    all_to_all x1, blocking collectives, exchange(): return lax.all_to_all(parts, axes, 0, 0)  15.9 us
    pallas_call x1, Pallas kernels, main_call(): pl.pallas_call(main_kernel, out_shape=(in_vmem((HALF, 128), BF16), in_vme...  8.87 us
    all_to_all x2, starting transfers between devices, exchange(): return lax.all_to_all(parts, axes, 0, 0)  8.74 us
    ppermute x6, waiting for transfers between devices, shifted(): return lax.ppermute(value, ALL, pairs)  7.96 us
    all_to_all x2, waiting for transfers between devices, exchange(): return lax.all_to_all(parts, axes, 0, 0)  7.66 us
    ppermute x2, starting transfers between devices, swap_cores(): return lax.ppermute(value, ALL, [(i, i ^ cols) for i in range(count)])  4.81 us
    ppermute x2, waiting for transfers between devices, swap_cores(): return lax.ppermute(value, ALL, [(i, i ^ cols) for i in range(count)])  3.71 us
  transfers between devices with their start and end apart: 10, of which 4 were waited for; matrix products, arithmetic and copies ran while one was open for 3% of the time, Pallas kernels for 4%

profile of v6, /device:TPU:1, one launch (start us, length us, event | category | flops | bytes accessed | tf_op | source)
XLA Modules:
  0.0 86.0 jit_solution(16577328627952859095)
XLA Ops:
  0.6 1.2 %edges.1 = (bf16[2,2,4,12,384]{4,3,2,1,0:T(8,128)(2,1)S(1)}, bf16[2,2,12,4,384]{4,3,2,1,0:T(4,128)(2,1)S(1)}, bf16[2,2,4,4,384]{4,3,2,1,0:T(4,128)(2,1)S(1)}, bf...) custom-call(bf16[2,16,16,384]{3,2,1,0:T(8,128)(2,1)} %x_ref.1, ...), custom_call_target="tpu_custom_call" | custom-call | bytes 1200000 | tf_op jit(solution)/shard_map/edges/pallas_call | solution.py:69
  1.9 6.0 %collective-permute-start.1 = (bf16[2,2,12,4,384]{4,3,2,1,0:T(4,128)(2,1)S(1)}, bf16[2,2,12,4,384]{4,3,2,1,0:T(4,128)(2,1)S(1)}, u32[]{:S(2)}, u32[]{:S(2)}) collective-permute-start(bf16[2,2,12,4,384]{4,3,2,1,0:T(4,128)(2,1)S(1)} %get-tuple-element.50), channel_id=1, source_target_pairs={{0,7},{1,0},{2,1},{3,2},{4,3},{5,4},{6,5},{7,6},{8,15},{9,8},{10,9... | collective-permute-start | bytes 442376 | tf_op jit(solution)/shard_map/ppermute | solution.py:472
  7.9 1.0 %collective-permute-start = (bf16[2,2,4,12,384]{4,3,2,1,0:T(8,128)(2,1)S(1)}, bf16[2,2,4,12,384]{4,3,2,1,0:T(8,128)(2,1)S(1)}, u32[]{:S(2)}, u32[]{:S(2)}) collective-permute-start(bf16[2,2,4,12,384]{4,3,2,1,0:T(8,128)(2,1)S(1)} %get-tuple-element.49), channel_id=1, source_target_pairs={{0,248},{1,249},{2,250},{3,251},{4,252},{5,253},{6,254},{7,255},{8... | collective-permute-start | bytes 442376 | tf_op jit(solution)/shard_map/ppermute | solution.py:472
  8.8 6.2 %collective-permute-start.2 = (bf16[2,2,4,4,384]{4,3,2,1,0:T(4,128)(2,1)S(1)}, bf16[2,2,4,4,384]{4,3,2,1,0:T(4,128)(2,1)S(1)}, u32[]{:S(2)}, u32[]{:S(2)}) collective-permute-start(bf16[2,2,4,4,384]{4,3,2,1,0:T(4,128)(2,1)S(1)} %get-tuple-element.51), channel_id=1, source_target_pairs={{0,255},{1,248},{2,249},{3,250},{4,251},{5,252},{6,253},{7,254},{8... | collective-permute-start | bytes 147464 | tf_op jit(solution)/shard_map/ppermute | solution.py:472
  15.2 3.7 %gather_bias.1 = (f32[12,128,128]{2,1,0:T(8,128)S(1)}, s32[128,128]{1,0:T(8,128)S(1)}, f32[128,384]{1,0:T(8,128)S(1)}, f32[128,128]{1,0:T(8,128)S(1)}, bf16[128,...) custom-call(s32[128,128]{1,0:T(8,128)S(1)} %get-tuple-element.52.pos, ...), custom_call_target="tpu_custom_call" | custom-call | flops 4000000 | bytes 900000 | tf_op jit(solution)/shard_map/gather_bias/pallas_call | solution.py:128
  18.9 8.9 %block_pass.1 = (bf16[2432,128]{1,0:T(8,128)(2,1)S(1)}, bf16[2432,128]{1,0:T(8,128)(2,1)S(1)}, bf16[2,16,16,384]{3,2,1,0:T(8,128)(2,1)S(1)}, bf16[2,16,16,384]{3,2,1,0:T(8,128)(2,1)S(1)}) custom-call(bf16[2,16,16,384]{3,2,1,0:T(8,128)(2,1)S(1)} %get-tuple-element.47.x_ref, bf16[2,16,16,384]{3,2,1,0:T(8,128)(2,1)S(1)} %get-tuple-element.48.g_ref, ...), custom_call_target="tpu_custom_call" | custom-call | flops 4000000000 | bytes 6000000 | tf_op jit(solution)/shard_map/block_pass/pallas_call | solution.py:351
  27.9 2.0 %collective-permute-done.3.b_ref = bf16[2432,128]{1,0:T(8,128)(2,1)S(1)} collective-permute-done((bf16[2432,128]{1,0:T(8,128)(2,1)S(1)}, bf16[2432,128]{1,0:T(8,128)(2,1)S(1)}, u32[]{:S(2)}, u32[]{:S(2)}) %collective-permute-start.3) | collective-permute-done | bytes 622624 | tf_op jit(solution)/shard_map/ppermute | solution.py:482
  29.9 0.1 add_halves.1
  30.1 15.9 %all_to_all.15.parts_ref = bf16[16,152,128]{2,1,0:T(8,128)(2,1)S(1)} all-to-all(bf16[16,152,128]{2,1,0:T(8,128)(2,1)S(1)} %bitcast.36), channel_id=1, replica_groups=mesh['z'=8,'l'=2,'c'=2,'h'=2,'x'=4] {'l','h','x'}, dimensions={0} | all-to-all | bytes 1245184 | tf_op jit(solution)/shard_map/all_to_all | solution.py:476
  46.2 0.8 sum_copies.2
  47.0 5.2 %all-to-all-start.1 = ((bf16[8,152,128]{2,1,0:T(8,128)(2,1)}), bf16[8,152,128]{2,1,0:T(8,128)(2,1)S(1)}, u32[]{:S(2)}, u32[]{:S(2)}) async-start(bf16[8,152,128]{2,1,0:T(8,128)(2,1)} %sum_copies.2), calls=%async_computation.1 | async-start | bytes 622592 | tf_op jit(solution)/shard_map/all_to_all | solution.py:476
  52.2 0.1 pad_maximum_fusion.3
  52.3 0.9 %collective-permute-start.5 = (bf16[2,2,12,4,384]{4,3,2,1,0:T(4,128)(2,1)S(1)}, bf16[2,2,12,4,384]{4,3,2,1,0:T(4,128)(2,1)S(1)}, u32[]{:S(2)}, u32[]{:S(2)}) collective-permute-start(bf16[2,2,12,4,384]{4,3,2,1,0:T(4,128)(2,1)S(1)} %pad_maximum_fusion.3), channel_id=1, source_target_pairs={{0,1},{1,2},{2,3},{3,4},{4,5},{5,6},{6,7},{7,0},{8,9},{9,10},{10,1... | collective-permute-start | bytes 442376 | tf_op jit(solution)/shard_map/ppermute | solution.py:472
  53.2 2.2 %collective-permute-start.4 = (bf16[2,2,4,12,384]{4,3,2,1,0:T(8,128)(2,1)S(1)}, bf16[2,2,4,12,384]{4,3,2,1,0:T(8,128)(2,1)S(1)}, u32[]{:S(2)}, u32[]{:S(2)}) collective-permute-start(bf16[2,2,4,12,384]{4,3,2,1,0:T(8,128)(2,1)S(1)} %pad_maximum_fusion.2), channel_id=1, source_target_pairs={{0,8},{1,9},{2,10},{3,11},{4,12},{5,13},{6,14},{7,15},{8,16},{9,17... | collective-permute-start | bytes 442376 | tf_op jit(solution)/shard_map/ppermute | solution.py:472
  55.5 0.4 collective-permute-start.6
  55.9 7.9 %collective-permute-done.6 = bf16[2,2,4,4,384]{4,3,2,1,0:T(4,128)(2,1)S(1)} collective-permute-done((bf16[2,2,4,4,384]{4,3,2,1,0:T(4,128)(2,1)S(1)}, bf16[2,2,4,4,384]{4,3,2,1,0:T(4,128)(2,1)S(1)}, u32[]{:S(2)}, u32[]{:S(2)}) %collective-permute-start.6) | collective-permute-done | bytes 49184 | tf_op jit(solution)/shard_map/ppermute | solution.py:472
  64.0 0.9 %sum_copies.3 = bf16[16,152,128]{2,1,0:T(8,128)(2,1)} custom-call(bf16[8,152,128]{2,1,0:T(8,128)(2,1)S(1)} %all-to-all-done.1.parts_ref), custom_call_target="tpu_custom_call" | custom-call | flops 300000 | bytes 1200000 | tf_op jit(solution)/shard_map/sum_copies/pallas_call | solution.py:448
  64.9 3.6 %all-to-all-start.2 = ((bf16[16,152,128]{2,1,0:T(8,128)(2,1)}), bf16[16,152,128]{2,1,0:T(8,128)(2,1)S(1)}, u32[]{:S(2)}, u32[]{:S(2)}) async-start(bf16[16,152,128]{2,1,0:T(8,128)(2,1)} %sum_copies.3), calls=%async_computation.2 | async-start | bytes 1245184 | tf_op jit(solution)/shard_map/all_to_all | solution.py:476
  68.5 1.0 %add_convert_fusion.1 = bf16[2,16,16,384]{3,2,1,0:T(8,128)(2,1)} fusion(bf16[2,16,16,384]{3,2,1,0:T(8,128)(2,1)S(1)} %copy-done, bf16[1,16,16,384]{3,2,1,0:T(8,128)(2,1)S(1)} %get-tuple-element.87, bf16[1,16,16,384]{3,2,1,0:T(8,128)(2,1)S(1)} %get-tuple-element.88, bf16[2,12,4,384]{3,2,1,0:T(4,128)(2,1)S(1)} %get-tuple-element.94, ...), kind=kLoop, calls=%fused_computation.1 | loop fusion | flops 2555904 | bytes 1351680 | tf_op jit(solution)/shard_map/convert_element_type | solution.py:522
  69.4 0.9 %add_convert_fusion = bf16[2,16,16,384]{3,2,1,0:T(8,128)(2,1)} fusion(bf16[2,16,16,384]{3,2,1,0:T(8,128)(2,1)S(1)} %copy-done.1, bf16[1,16,16,384]{3,2,1,0:T(8,128)(2,1)S(1)} %get-tuple-element.98, bf16[1,16,16,384]{3,2,1,0:T(8,128)(2,1)S(1)} %get-tuple-element.97, bf16[2,12,4,384]{3,2,1,0:T(4,128)(2,1)S(1)} %get-tuple-element.93, ...), kind=kLoop, calls=%fused_computation | loop fusion | flops 2555904 | bytes 1351680 | tf_op jit(solution)/shard_map/convert_element_type | solution.py:522
  70.4 7.7 %all-to-all-done.2 = bf16[16,152,128]{2,1,0:T(8,128)(2,1)S(1)} async-done(((bf16[16,152,128]{2,1,0:T(8,128)(2,1)}), bf16[16,152,128]{2,1,0:T(8,128)(2,1)S(1)}, u32[]{:S(2)}, u32[]{:S(2)}) %all-to-all-start.2) | async-done | bytes 622624 | tf_op jit(solution)/shard_map/all_to_all | solution.py:476
  78.0 4.7 %collective-permute-start.7 = (bf16[2432,128]{1,0:T(8,128)(2,1)S(1)}, bf16[2432,128]{1,0:T(8,128)(2,1)S(1)}, u32[]{:S(2)}, u32[]{:S(2)}) collective-permute-start(bf16[2432,128]{1,0:T(8,128)(2,1)S(1)} %bitcast.34), channel_id=1, source_target_pairs={{0,8},{1,9},{2,10},{3,11},{4,12},{5,13},{6,14},{7,15},{8,0},{9,1},... | collective-permute-start | bytes 1867784 | tf_op jit(solution)/shard_map/ppermute | solution.py:482
  82.8 1.7 %collective-permute-done.7.other_ref = bf16[2432,128]{1,0:T(8,128)(2,1)S(1)} collective-permute-done((bf16[2432,128]{1,0:T(8,128)(2,1)S(1)}, bf16[2432,128]{1,0:T(8,128)(2,1)S(1)}, u32[]{:S(2)}, u32[]{:S(2)}) %collective-permute-start.7) | collective-permute-done | bytes 622624 | tf_op jit(solution)/shard_map/ppermute | solution.py:482
  84.4 1.5 %unpack_sums.1 = (f32[384,1152]{1,0:T(8,128)}, f32[384,384]{1,0:T(8,128)}, f32[12,675]{1,0:T(8,128)}, f32[384]{0:T(512)}, f32[384]{0:T(512)}) custom-call(s32[1]{0:T(128)} %bitcast.2.me_ref, bf16[2432,128]{1,0:T(8,128)(2,1)S(1)} %bitcast.35, bf16[2432,128]{1,0:T(8,128)(2,1)S(1)} %collective-permute-done.7.other_ref), custom_call_target="tpu_custom_call" | custom-call | flops 600000 | bytes 3600000 | tf_op jit(solution)/shard_map/unpack_sums/pallas_call | solution.py:404
  (26 shorter events, 0.8 us)
Async XLA Ops:
  1.9 17.0 %collective-permute-start.1 = (bf16[2,2,12,4,384]{4,3,2,1,0:T(4,128)(2,1)S(1)}, bf16[2,2,12,4,384]{4,3,2,1,0:T(4,128)(2,1)S(1)}, u32[]{:S(2)}, u32[]{:S(2)}) collective-permute-start(bf16[2,2,12,4,384]{4,3,2,1,0:T(4,128)(2,1)S(1)} %get-tuple-element.50), channel_id=1, source_target_pairs={{0,7},{1,0},{2,1},{3,2},{4,3},{5,4},{6,5},{7,6},{8,15},{9,8},{10,9... | collective-permute-start | bytes 442376 | tf_op jit(solution)/shard_map/ppermute | solution.py:472
  7.9 11.0 %collective-permute-start = (bf16[2,2,4,12,384]{4,3,2,1,0:T(8,128)(2,1)S(1)}, bf16[2,2,4,12,384]{4,3,2,1,0:T(8,128)(2,1)S(1)}, u32[]{:S(2)}, u32[]{:S(2)}) collective-permute-start(bf16[2,2,4,12,384]{4,3,2,1,0:T(8,128)(2,1)S(1)} %get-tuple-element.49), channel_id=1, source_target_pairs={{0,248},{1,249},{2,250},{3,251},{4,252},{5,253},{6,254},{7,255},{8... | collective-permute-start | bytes 442376 | tf_op jit(solution)/shard_map/ppermute | solution.py:472
  8.8 10.1 %collective-permute-start.2 = (bf16[2,2,4,4,384]{4,3,2,1,0:T(4,128)(2,1)S(1)}, bf16[2,2,4,4,384]{4,3,2,1,0:T(4,128)(2,1)S(1)}, u32[]{:S(2)}, u32[]{:S(2)}) collective-permute-start(bf16[2,2,4,4,384]{4,3,2,1,0:T(4,128)(2,1)S(1)} %get-tuple-element.51), channel_id=1, source_target_pairs={{0,255},{1,248},{2,249},{3,250},{4,251},{5,252},{6,253},{7,254},{8... | collective-permute-start | bytes 147464 | tf_op jit(solution)/shard_map/ppermute | solution.py:472
  27.8 2.1 %collective-permute-start.3 = (bf16[2432,128]{1,0:T(8,128)(2,1)S(1)}, bf16[2432,128]{1,0:T(8,128)(2,1)S(1)}, u32[]{:S(2)}, u32[]{:S(2)}) collective-permute-start(bf16[2432,128]{1,0:T(8,128)(2,1)S(1)} %get-tuple-element.69), channel_id=1, source_target_pairs={{0,8},{1,9},{2,10},{3,11},{4,12},{5,13},{6,14},{7,15},{8,0},{9,1},... | collective-permute-start | bytes 1867784 | tf_op jit(solution)/shard_map/ppermute | solution.py:482
  47.0 16.9 %all-to-all-start.1 = ((bf16[8,152,128]{2,1,0:T(8,128)(2,1)}), bf16[8,152,128]{2,1,0:T(8,128)(2,1)S(1)}, u32[]{:S(2)}, u32[]{:S(2)}) async-start(bf16[8,152,128]{2,1,0:T(8,128)(2,1)} %sum_copies.2), calls=%async_computation.1 | async-start | bytes 622592 | tf_op jit(solution)/shard_map/all_to_all | solution.py:476
  52.3 11.5 %collective-permute-start.5 = (bf16[2,2,12,4,384]{4,3,2,1,0:T(4,128)(2,1)S(1)}, bf16[2,2,12,4,384]{4,3,2,1,0:T(4,128)(2,1)S(1)}, u32[]{:S(2)}, u32[]{:S(2)}) collective-permute-start(bf16[2,2,12,4,384]{4,3,2,1,0:T(4,128)(2,1)S(1)} %pad_maximum_fusion.3), channel_id=1, source_target_pairs={{0,1},{1,2},{2,3},{3,4},{4,5},{5,6},{6,7},{7,0},{8,9},{9,10},{10,1... | collective-permute-start | bytes 442376 | tf_op jit(solution)/shard_map/ppermute | solution.py:472
  53.2 10.6 %collective-permute-start.4 = (bf16[2,2,4,12,384]{4,3,2,1,0:T(8,128)(2,1)S(1)}, bf16[2,2,4,12,384]{4,3,2,1,0:T(8,128)(2,1)S(1)}, u32[]{:S(2)}, u32[]{:S(2)}) collective-permute-start(bf16[2,2,4,12,384]{4,3,2,1,0:T(8,128)(2,1)S(1)} %pad_maximum_fusion.2), channel_id=1, source_target_pairs={{0,8},{1,9},{2,10},{3,11},{4,12},{5,13},{6,14},{7,15},{8,16},{9,17... | collective-permute-start | bytes 442376 | tf_op jit(solution)/shard_map/ppermute | solution.py:472
  55.4 13.0 %copy-start = (bf16[2,16,16,384]{3,2,1,0:T(8,128)(2,1)S(1)}, bf16[2,16,16,384]{3,2,1,0:T(8,128)(2,1)}, u32[]{:S(2)}) copy-start(bf16[2,16,16,384]{3,2,1,0:T(8,128)(2,1)} %x_ref.1) | copy-start | bytes 1179652
  55.5 8.3 %collective-permute-start.6 = (bf16[2,2,4,4,384]{4,3,2,1,0:T(4,128)(2,1)S(1)}, bf16[2,2,4,4,384]{4,3,2,1,0:T(4,128)(2,1)S(1)}, u32[]{:S(2)}, u32[]{:S(2)}) collective-permute-start(bf16[2,2,4,4,384]{4,3,2,1,0:T(4,128)(2,1)S(1)} %pad_maximum_fusion.4), channel_id=1, source_target_pairs={{0,9},{1,10},{2,11},{3,12},{4,13},{5,14},{6,15},{7,8},{8,17},{9,18... | collective-permute-start | bytes 147464 | tf_op jit(solution)/shard_map/ppermute | solution.py:472
  63.9 5.5 %copy-start.1 = (bf16[2,16,16,384]{3,2,1,0:T(8,128)(2,1)S(1)}, bf16[2,16,16,384]{3,2,1,0:T(8,128)(2,1)}, u32[]{:S(2)}) copy-start(bf16[2,16,16,384]{3,2,1,0:T(8,128)(2,1)} %g_ref.1) | copy-start | bytes 1179652
  64.9 13.2 %all-to-all-start.2 = ((bf16[16,152,128]{2,1,0:T(8,128)(2,1)}), bf16[16,152,128]{2,1,0:T(8,128)(2,1)S(1)}, u32[]{:S(2)}, u32[]{:S(2)}) async-start(bf16[16,152,128]{2,1,0:T(8,128)(2,1)} %sum_copies.3), calls=%async_computation.2 | async-start | bytes 1245184 | tf_op jit(solution)/shard_map/all_to_all | solution.py:476
  78.0 6.4 %collective-permute-start.7 = (bf16[2432,128]{1,0:T(8,128)(2,1)S(1)}, bf16[2432,128]{1,0:T(8,128)(2,1)S(1)}, u32[]{:S(2)}, u32[]{:S(2)}) collective-permute-start(bf16[2432,128]{1,0:T(8,128)(2,1)S(1)} %bitcast.34), channel_id=1, source_target_pairs={{0,8},{1,9},{2,10},{3,11},{4,12},{5,13},{6,14},{7,15},{8,0},{9,1},... | collective-permute-start | bytes 1867784 | tf_op jit(solution)/shard_map/ppermute | solution.py:482
